TPU v7x, 32 devices: a whole 2x2x4 slice. The times are simulated.
32 devices in a mesh: ctx: 16 (over z, x, core), dp: 2 (over y).
Axes of the slice: x: 2, y: 2, z: 4, core: 2. Of those that a mesh axis runs over, the one named last changes fastest.
Arguments:
- tokens: bfloat16 [4, 1024, 768], P('dp', 'ctx'), may hold values from -6 to 6
- cotangent: bfloat16 [4, 1024, 768], P('dp', 'ctx'), may hold values from -6 to 6
- block_order: int32 [32], replicated, may hold values from 0 to 31, each once
- input_weight: float32 [2, 768, 2304], P('dp', None, 'ctx'), may hold values from -0.3125 to 0.3125
- output_weight: float32 [2, 768, 768], P('dp', None, 'ctx'), may hold values from -0.4375 to 0.4375
- expand_weight: float32 [2, 768, 3072], P('dp', None, 'ctx'), may hold values from -0.21875 to 0.21875
- reduce_weight: float32 [2, 3072, 768], P('dp', 'ctx'), may hold values from -0.109375 to 0.109375
- vectors: float32 [2, 9216], P('dp', 'ctx'), may hold values from -0.8 to 1.6, as said below
- input_moment: float32 [2, 768, 2304], P('dp', None, 'ctx'), may hold values from -80 to 80
- output_moment: float32 [2, 768, 768], P('dp', None, 'ctx'), may hold values from -96 to 96
- expand_moment: float32 [2, 768, 3072], P('dp', None, 'ctx'), may hold values from -192 to 192
- reduce_moment: float32 [2, 3072, 768], P('dp', 'ctx'), may hold values from -192 to 192
- vector_first: float32 [2, 9216], P('dp', 'ctx'), may hold values from -112 to 112
- vector_second: float32 [2, 9216], P('dp', 'ctx'), may hold values from 53.248 to 217.088
Outputs:
- block_output: float32 [4, 1024, 768], P('dp', 'ctx')
- input_grad: float32 [4, 1024, 768], P('dp', 'ctx')
- new_input_weight: float32 [2, 768, 2304], P('dp', None, 'ctx')
- new_output_weight: float32 [2, 768, 768], P('dp', None, 'ctx')
- new_expand_weight: float32 [2, 768, 3072], P('dp', None, 'ctx')
- new_reduce_weight: float32 [2, 3072, 768], P('dp', 'ctx')
- new_input_moment: float32 [2, 768, 2304], P('dp', None, 'ctx')
- new_output_moment: float32 [2, 768, 768], P('dp', None, 'ctx')
- new_expand_moment: float32 [2, 768, 3072], P('dp', None, 'ctx')
- new_reduce_moment: float32 [2, 3072, 768], P('dp', 'ctx')
- new_vectors: float32 [2, 9216], P('dp', 'ctx')
- new_vector_first: float32 [2, 9216], P('dp', 'ctx')
- new_vector_second: float32 [2, 9216], P('dp', 'ctx')
Inputs may be any that keep to these rules, and one draw needn't show every extreme that they name: Stored block j of every sequence holds the 32 positions from block_order[j] * 32 on; each of the 32 blocks once. `vectors`: in each layer entries 0 to 767 and 3840 to 4607 are norm gains, the others biases.
All inputs are finite; a program needn't handle non-finite values.
Results may differ from a plain program's by a relative error of at most 0.023.
Values may be sent and summed in bfloat16 or wider, within the bound.
No kernel may reach another device: no remote copies, remote signals or barrier semaphores. Data moves between devices by JAX's collectives and lax.ppermute only.
A program may use at most 320 MiB of HBM per device.

v0:
```python
import math

import jax
import jax.numpy as jnp
from jax import lax
from jax.sharding import PartitionSpec as P

D = 768
FF = 3072
HEADS = 12
NS_STEPS = 5
STEP = 10


norm_epsilon = 1e-05
neg_large = -1e30
score_scale = 0.125
coef_first = 3.4445
coef_second = -4.775
coef_third = 2.0315
ortho_epsilon = 1e-07
muon_rate = 0.15
muon_moment = 0.95
muon_decay = 0.01
adam_rate = 0.3
beta_first = 0.9
beta_second = 0.95
adam_epsilon = 1e-08
highest = lax.Precision.HIGHEST


def contract_rows(left, right):
    return lax.dot_general(
        left, right, (((0,), (0,)), ((), ())), preferred_element_type=jnp.float32
    )


def contract_last(left, right):
    return lax.dot_general(
        left, right, (((1,), (1,)), ((), ())), preferred_element_type=jnp.float32
    )


def norm_forward(values_in, gain, shift):
    centred = values_in - jnp.mean(values_in, axis=-1, keepdims=True)
    inv_std = lax.rsqrt(jnp.mean(centred * centred, axis=-1, keepdims=True) + norm_epsilon)
    normed = centred * inv_std
    return (normed * gain + shift, normed, inv_std)


def norm_backward(grad_out, normed, inv_std, gain):
    scaled = grad_out * gain
    grad_in = inv_std * (
        scaled
        - jnp.mean(scaled, axis=-1, keepdims=True)
        - normed * jnp.mean(scaled * normed, axis=-1, keepdims=True)
    )
    return (grad_in, jnp.sum(grad_out * normed, axis=0), jnp.sum(grad_out, axis=0))


def gelu_tanh(values_in):
    return jax.nn.gelu(values_in, approximate=True)


def block_positions(block_order, first_row, row_count, block_len):
    blocks = lax.dynamic_slice_in_dim(block_order, first_row // block_len, row_count // block_len)
    within = jnp.arange(row_count, dtype=jnp.int32) % block_len
    return jnp.repeat(blocks, block_len, total_repeat_length=row_count) * block_len + within


def take_rows(array, offset, row_count):
    return lax.dynamic_slice_in_dim(array, offset, row_count, 1)


def softmax_tile(query_heads, key_heads, log_total, query_pos, key_pos):
    scores = (
        jnp.einsum("sthd,skhd->shtk", query_heads, key_heads, preferred_element_type=jnp.float32)
        * score_scale
    )
    allowed = key_pos[None, :] <= query_pos[:, None]
    return jnp.where(allowed, jnp.exp(scores - log_total[..., None]), 0.0)


def attend_forward(query_rows, key_rows, value_rows, block_order, block_len):
    seqs, local, width = query_rows.shape
    head_shape = (seqs, local, HEADS, width // HEADS)
    query_pos = block_positions(block_order, lax.axis_index("ctx") * local, local, block_len)
    query_heads = query_rows.reshape(head_shape)
    start_stats = (
        jnp.full((seqs, HEADS, local), neg_large, jnp.float32),
        jnp.zeros((seqs, HEADS, local), jnp.float32),
    )
    key_piece = lax.all_gather(key_rows, "ctx", axis=1, tiled=True)

    def stats_step(number, inner):
        offset = number * local
        key_part = take_rows(key_piece, offset, local).reshape(head_shape)
        key_pos = block_positions(block_order, offset, local, block_len)
        run_max, run_sum = inner
        scores = (
            jnp.einsum("sthd,skhd->shtk", query_heads, key_part, preferred_element_type=jnp.float32)
            * score_scale
        )
        allowed = key_pos[None, :] <= query_pos[:, None]
        scores = jnp.where(allowed, scores, neg_large)
        new_max = jnp.maximum(run_max, jnp.max(scores, axis=-1))
        expo = jnp.where(allowed, jnp.exp(scores - new_max[..., None]), 0.0)
        return (new_max, run_sum * jnp.exp(run_max - new_max) + jnp.sum(expo, axis=-1))

    run_max, run_sum = lax.fori_loop(0, key_piece.shape[1] // local, stats_step, start_stats)
    log_total = run_max + jnp.log(run_sum)
    value_key_piece = lax.all_gather(key_rows, "ctx", axis=1, tiled=True)
    value_piece = lax.all_gather(value_rows, "ctx", axis=1, tiled=True)

    def value_step(number, inner):
        offset = number * local
        key_part = take_rows(value_key_piece, offset, local).reshape(head_shape)
        value_part = take_rows(value_piece, offset, local).reshape(head_shape)
        key_pos = block_positions(block_order, offset, local, block_len)
        prob = softmax_tile(query_heads, key_part, log_total, query_pos, key_pos)
        return inner + jnp.einsum(
            "shtk,skhd->sthd",
            prob.astype(jnp.bfloat16),
            value_part,
            preferred_element_type=jnp.float32,
        )

    accum = lax.fori_loop(
        0, value_key_piece.shape[1] // local, value_step, jnp.zeros(head_shape, jnp.float32)
    )
    return (accum.reshape(seqs, local, width), log_total)


def attend_backward(
    query_rows, key_rows, value_rows, grad_rows, out_full, log_total, block_order, block_len
):
    seqs, local, width = query_rows.shape
    head_shape = (seqs, local, HEADS, width // HEADS)
    query_pos = block_positions(block_order, lax.axis_index("ctx") * local, local, block_len)
    query_heads = query_rows.reshape(head_shape)
    key_heads = key_rows.reshape(head_shape)
    value_heads = value_rows.reshape(head_shape)
    grad_heads = grad_rows.reshape(head_shape)
    row_dot = jnp.sum(grad_heads.astype(jnp.float32) * out_full.reshape(head_shape), axis=-1)
    dot_cols = jnp.swapaxes(row_dot, 1, 2)
    total_rows = jnp.swapaxes(log_total, 1, 2)
    key_piece = lax.all_gather(key_rows, "ctx", axis=1, tiled=True)
    value_piece = lax.all_gather(value_rows, "ctx", axis=1, tiled=True)

    def query_step(number, inner):
        offset = number * local
        key_part = take_rows(key_piece, offset, local).reshape(head_shape)
        value_part = take_rows(value_piece, offset, local).reshape(head_shape)
        key_pos = block_positions(block_order, offset, local, block_len)
        prob = softmax_tile(query_heads, key_part, log_total, query_pos, key_pos)
        prob_grad = jnp.einsum(
            "sthd,skhd->shtk", grad_heads, value_part, preferred_element_type=jnp.float32
        )
        score_grad = (prob * (prob_grad - dot_cols[..., None])).astype(jnp.bfloat16)
        return (
            inner
            + jnp.einsum(
                "shtk,skhd->sthd", score_grad, key_part, preferred_element_type=jnp.float32
            )
            * score_scale
        )

    grad_query = lax.fori_loop(
        0, key_piece.shape[1] // local, query_step, jnp.zeros(head_shape, jnp.float32)
    )
    empty = jnp.zeros(head_shape, jnp.float32)
    query_piece = lax.all_gather(query_rows.astype(jnp.float32), "ctx", axis=1, tiled=True)
    grad_piece = lax.all_gather(grad_rows.astype(jnp.float32), "ctx", axis=1, tiled=True)
    total_piece = lax.all_gather(total_rows, "ctx", axis=1, tiled=True)
    dot_piece = lax.all_gather(row_dot, "ctx", axis=1, tiled=True)

    def key_step(number, inner):
        grad_keys, grad_values = inner
        offset = number * local
        query_part = take_rows(query_piece, offset, local).astype(jnp.bfloat16).reshape(head_shape)
        grad_part = take_rows(grad_piece, offset, local).astype(jnp.bfloat16).reshape(head_shape)
        total_part = jnp.swapaxes(take_rows(total_piece, offset, local), 1, 2)
        dot_part = jnp.swapaxes(take_rows(dot_piece, offset, local), 1, 2)
        part_pos = block_positions(block_order, offset, local, block_len)
        prob = softmax_tile(query_part, key_heads, total_part, part_pos, query_pos)
        prob_grad = jnp.einsum(
            "sthd,skhd->shtk", grad_part, value_heads, preferred_element_type=jnp.float32
        )
        score_grad = (prob * (prob_grad - dot_part[..., None])).astype(jnp.bfloat16)
        grad_values = grad_values + jnp.einsum(
            "shtk,sthd->skhd",
            prob.astype(jnp.bfloat16),
            grad_part,
            preferred_element_type=jnp.float32,
        )
        grad_keys = (
            grad_keys
            + jnp.einsum(
                "shtk,sthd->skhd", score_grad, query_part, preferred_element_type=jnp.float32
            )
            * score_scale
        )
        return (grad_keys, grad_values)

    grad_keys, grad_values = lax.fori_loop(
        0, query_piece.shape[1] // local, key_step, (empty, empty)
    )
    flat = (seqs * local, width)
    return (
        grad_query.reshape(flat).astype(jnp.bfloat16),
        grad_keys.reshape(flat).astype(jnp.bfloat16),
        grad_values.reshape(flat).astype(jnp.bfloat16),
    )


def split_vector(vec_row, width):
    params = vec_row.astype(jnp.float32)
    pieces = [params[number * width : (number + 1) * width] for number in range(8)]
    return (pieces, params[8 * width :])


def layer_forward(stream, mix_in, mix_out, feed_in, feed_out, vec_row, block_order, seqs, local):
    width = stream.shape[1]
    pieces, bias_hidden = split_vector(vec_row, width)
    normed_in, normed_one, inv_one = norm_forward(stream, pieces[0], pieces[1])
    first_in = normed_in.astype(jnp.bfloat16)
    projected = jnp.dot(first_in, mix_in, preferred_element_type=jnp.float32)
    query_rows = (projected[:, :width] + pieces[2]).astype(jnp.bfloat16)
    key_rows = projected[:, width : 2 * width].astype(jnp.bfloat16)
    value_rows = (projected[:, 2 * width :] + pieces[3]).astype(jnp.bfloat16)
    seq_shape = (seqs, local, width)
    out_full, log_total = attend_forward(
        query_rows.reshape(seq_shape),
        key_rows.reshape(seq_shape),
        value_rows.reshape(seq_shape),
        block_order,
        local // 2,
    )
    mixed_in = out_full.reshape(seqs * local, width).astype(jnp.bfloat16)
    middle = stream + (jnp.dot(mixed_in, mix_out, preferred_element_type=jnp.float32) + pieces[4])
    normed_mid, normed_two, inv_two = norm_forward(middle, pieces[5], pieces[6])
    second_in = normed_mid.astype(jnp.bfloat16)
    hidden_pre = jnp.dot(second_in, feed_in, preferred_element_type=jnp.float32) + bias_hidden
    active = gelu_tanh(hidden_pre).astype(jnp.bfloat16)
    result = middle + (jnp.dot(active, feed_out, preferred_element_type=jnp.float32) + pieces[7])
    kept = (
        normed_one,
        inv_one,
        first_in,
        query_rows,
        key_rows,
        value_rows,
        out_full,
        log_total,
        mixed_in,
        normed_two,
        inv_two,
        second_in,
        hidden_pre,
        active,
    )
    return (result, kept)


def layer_backward(
    grad_out, kept, mix_in, mix_out, feed_in, feed_out, vec_row, block_order, seqs, local
):
    (
        normed_one,
        inv_one,
        first_in,
        query_rows,
        key_rows,
        value_rows,
        out_full,
        log_total,
        mixed_in,
        normed_two,
        inv_two,
        second_in,
        hidden_pre,
        active,
    ) = kept
    width = grad_out.shape[1]
    pieces, bias_hidden = split_vector(vec_row, width)
    grad_branch = grad_out.astype(jnp.bfloat16)
    grad_bias_feed = jnp.sum(grad_branch.astype(jnp.float32), axis=0)
    grad_feed_out = contract_rows(active, grad_branch)
    grad_active = contract_last(grad_branch, feed_out)
    unused, pull = jax.vjp(gelu_tanh, hidden_pre)
    grad_hidden = pull(grad_active)[0].astype(jnp.bfloat16)
    grad_bias_hidden = jnp.sum(grad_hidden.astype(jnp.float32), axis=0)
    grad_feed_in = contract_rows(second_in, grad_hidden)
    grad_second = contract_last(grad_hidden, feed_in)
    grad_mid_norm, grad_gain_two, grad_shift_two = norm_backward(
        grad_second, normed_two, inv_two, pieces[5]
    )
    grad_middle = grad_out + grad_mid_norm
    grad_mix_branch = grad_middle.astype(jnp.bfloat16)
    grad_bias_mix = jnp.sum(grad_mix_branch.astype(jnp.float32), axis=0)
    grad_mix_out = contract_rows(mixed_in, grad_mix_branch)
    grad_attn = contract_last(grad_mix_branch, mix_out).astype(jnp.bfloat16)
    seq_shape = (seqs, local, width)
    grad_query, grad_key, grad_value = attend_backward(
        query_rows.reshape(seq_shape),
        key_rows.reshape(seq_shape),
        value_rows.reshape(seq_shape),
        grad_attn.reshape(seq_shape),
        out_full,
        log_total,
        block_order,
        local // 2,
    )
    grad_bias_query = jnp.sum(grad_query.astype(jnp.float32), axis=0)
    grad_bias_value = jnp.sum(grad_value.astype(jnp.float32), axis=0)
    grad_projected = jnp.concatenate([grad_query, grad_key, grad_value], axis=1)
    grad_mix_in = contract_rows(first_in, grad_projected)
    grad_first = contract_last(grad_projected, mix_in)
    grad_in_norm, grad_gain_one, grad_shift_one = norm_backward(
        grad_first, normed_one, inv_one, pieces[0]
    )
    grad_stream = grad_middle + grad_in_norm
    grad_vector = jnp.concatenate(
        [
            grad_gain_one,
            grad_shift_one,
            grad_bias_query,
            grad_bias_value,
            grad_bias_mix,
            grad_gain_two,
            grad_shift_two,
            grad_bias_feed,
            grad_bias_hidden,
        ]
    )
    return (grad_stream, (grad_mix_in, grad_mix_out, grad_feed_in, grad_feed_out, grad_vector))


def gram_all(parts):
    terms = jnp.stack([jnp.dot(part, part.T, precision=highest) for part in parts])
    received = lax.all_to_all(terms[None], "ctx", split_axis=2, concat_axis=0, tiled=True)
    shared = jnp.sum(received, axis=0)
    return lax.all_gather(shared, "ctx", axis=1, tiled=True)


def column_form(grads):
    return (grads[0], grads[1], grads[2], jnp.swapaxes(grads[3], 1, 2), grads[4][:, None, :])


def row_form(summed):
    return (summed[0], summed[1], summed[2], jnp.swapaxes(summed[3], 1, 2), summed[4][:, 0, :])


def body(
    tokens,
    cotangent,
    block_order,
    input_weight,
    output_weight,
    expand_weight,
    reduce_weight,
    vectors,
    input_moment,
    output_moment,
    expand_moment,
    reduce_moment,
    vector_first,
    vector_second,
):
    seqs, local, width = tokens.shape
    rows = seqs * local
    wide = (
        lax.all_gather(input_weight.astype(jnp.bfloat16), "ctx", axis=2, tiled=True),
        lax.all_gather(output_weight.astype(jnp.bfloat16), "ctx", axis=2, tiled=True),
        lax.all_gather(expand_weight.astype(jnp.bfloat16), "ctx", axis=2, tiled=True),
        lax.all_gather(reduce_weight.astype(jnp.bfloat16), "ctx", axis=1, tiled=True),
        lax.all_gather(vectors.astype(jnp.bfloat16), "ctx", axis=1, tiled=True),
    )
    full = (
        lax.all_gather(wide[0], "dp", axis=0, tiled=True),
        lax.all_gather(wide[1], "dp", axis=0, tiled=True),
        lax.all_gather(wide[2], "dp", axis=0, tiled=True),
        lax.all_gather(wide[3], "dp", axis=0, tiled=True),
        lax.all_gather(wide[4], "dp", axis=0, tiled=True),
    )
    layer_count = full[0].shape[0]
    stream = tokens.astype(jnp.float32).reshape(rows, width)
    saved = []
    for layer_index in range(layer_count):
        stream, kept = layer_forward(
            stream,
            full[0][layer_index],
            full[1][layer_index],
            full[2][layer_index],
            full[3][layer_index],
            full[4][layer_index],
            block_order,
            seqs,
            local,
        )
        saved.append(kept)
    block_output = stream.reshape(seqs, local, width)
    grad_stream = cotangent.astype(jnp.float32).reshape(rows, width)
    layer_grads = [None] * layer_count
    for layer_index in reversed(range(layer_count)):
        grad_stream, layer_grads[layer_index] = layer_backward(
            grad_stream,
            saved[layer_index],
            full[0][layer_index],
            full[1][layer_index],
            full[2][layer_index],
            full[3][layer_index],
            full[4][layer_index],
            block_order,
            seqs,
            local,
        )
    input_grad = grad_stream.reshape(seqs, local, width)
    stacked = [
        jnp.stack([layer_grads[layer_index][kind] for layer_index in range(layer_count)])
        for kind in range(5)
    ]
    cols = column_form(stacked)
    received = (
        lax.all_to_all(cols[0][None], "ctx", split_axis=3, concat_axis=0, tiled=True),
        lax.all_to_all(cols[1][None], "ctx", split_axis=3, concat_axis=0, tiled=True),
        lax.all_to_all(cols[2][None], "ctx", split_axis=3, concat_axis=0, tiled=True),
        lax.all_to_all(cols[3][None], "ctx", split_axis=3, concat_axis=0, tiled=True),
        lax.all_to_all(cols[4][None], "ctx", split_axis=3, concat_axis=0, tiled=True),
    )
    partial_sums = row_form([jnp.sum(piece, axis=0) for piece in received])
    owned = (
        lax.psum_scatter(partial_sums[0], "dp", scatter_dimension=0, tiled=True),
        lax.psum_scatter(partial_sums[1], "dp", scatter_dimension=0, tiled=True),
        lax.psum_scatter(partial_sums[2], "dp", scatter_dimension=0, tiled=True),
        lax.psum_scatter(partial_sums[3], "dp", scatter_dimension=0, tiled=True),
        lax.psum_scatter(partial_sums[4], "dp", scatter_dimension=0, tiled=True),
    )
    old_moments = (input_moment, output_moment, expand_moment, reduce_moment)
    new_moments = [muon_moment * old_moments[kind] + owned[kind] for kind in range(4)]
    mats = [
        new_moments[0][0],
        new_moments[1][0],
        new_moments[2][0],
        jnp.swapaxes(new_moments[3][0], 0, 1),
    ]
    grams = gram_all(mats)
    traces = jnp.trace(grams, axis1=1, axis2=2)
    scales = 1.0 / (jnp.sqrt(traces) + ortho_epsilon)
    mats = [mats[kind] * scales[kind] for kind in range(4)]
    grams = grams * (scales * scales)[:, None, None]
    for sweep in range(NS_STEPS):
        if sweep > 0:
            grams = gram_all(mats)
        poly = coef_second * grams + coef_third * jnp.einsum(
            "kij,kjl->kil", grams, grams, precision=highest
        )
        mats = [
            coef_first * mats[kind] + jnp.dot(poly[kind], mats[kind], precision=highest)
            for kind in range(4)
        ]
    directions = [mats[0], mats[1], mats[2], jnp.swapaxes(mats[3], 0, 1)]
    largest = (3 * D, D, FF, FF)
    old_weights = (input_weight, output_weight, expand_weight, reduce_weight)
    new_weights = [
        old_weights[kind] * (1.0 - muon_rate * muon_decay)
        - muon_rate * 0.2 * math.sqrt(largest[kind]) * directions[kind][None]
        for kind in range(4)
    ]
    vec_grad = owned[4]
    new_vector_first = beta_first * vector_first + (1.0 - beta_first) * vec_grad
    new_vector_second = beta_second * vector_second + (1.0 - beta_second) * vec_grad * vec_grad
    corr_first = 1.0 - beta_first**STEP
    corr_second = 1.0 - beta_second**STEP
    new_vectors = vectors - adam_rate * (new_vector_first / corr_first) / (
        jnp.sqrt(new_vector_second / corr_second) + adam_epsilon
    )
    return (
        block_output,
        input_grad,
        new_weights[0],
        new_weights[1],
        new_weights[2],
        new_weights[3],
        new_moments[0],
        new_moments[1],
        new_moments[2],
        new_moments[3],
        new_vectors,
        new_vector_first,
        new_vector_second,
    )


def solution(mesh):
    return jax.shard_map(
        body,
        mesh=mesh,
        in_specs=(
            P("dp", "ctx", None),
            P("dp", "ctx", None),
            P(),
            P("dp", None, "ctx"),
            P("dp", None, "ctx"),
            P("dp", None, "ctx"),
            P("dp", "ctx", None),
            P("dp", "ctx"),
            P("dp", None, "ctx"),
            P("dp", None, "ctx"),
            P("dp", None, "ctx"),
            P("dp", "ctx", None),
            P("dp", "ctx"),
            P("dp", "ctx"),
        ),
        out_specs=(
            P("dp", "ctx", None),
            P("dp", "ctx", None),
            P("dp", None, "ctx"),
            P("dp", None, "ctx"),
            P("dp", None, "ctx"),
            P("dp", "ctx", None),
            P("dp", None, "ctx"),
            P("dp", None, "ctx"),
            P("dp", None, "ctx"),
            P("dp", "ctx", None),
            P("dp", "ctx"),
            P("dp", "ctx"),
            P("dp", "ctx"),
        ),
        check_vma=False,
    )
```

profile of v0, /device:TPU:0, one launch (start us, length us, event | category | flops | bytes accessed | tf_op | source)
XLA Modules:
  0.0 4750.4 jit_solution(1343227451754072201)
XLA Ops:
  357.1 74.2 %while.156 = (s32[]{:T(128)}, f32[2,12,64]{2,1,0:T(8,128)S(1)}, f32[2,12,64]{2,1,0:T(8,128)S(1)}, s32[32]{0:T(128)}, s32[64]{0:T(128)S(1)}, /*index=5*/bf16[2,10...) while((s32[]{:T(128)}, f32[2,12,64]{2,1,0:T(8,128)S(1)}, ...), condition=%wide.region_5.8_spmd.clone, body=%wide.region_2.0_spmd.clone.sunk | while | flops 13185112 | bytes 2059509 | solution.py:110
  432.3 79.3 %while.157 = (s32[]{:T(128)}, f32[2,64,12,64]{1,3,2,0:T(8,128)S(1)}, bf16[2,1024,768]{2,1,0:T(8,128)(2,1)}, s32[32]{0:T(128)}, s32[64]{0:T(128)S(1)}, /*index=5*...) while((s32[]{:T(128)}, f32[2,64,12,64]{1,3,2,0:T(8,128)S(1)}, ...), condition=%wide.region_7.10_spmd.clone, body=%wide.region_6.9_spmd.clone.sunk | while | flops 25760344 | bytes 2964732 | solution.py:128
  559.7 116.3 %all-gather.41.cloned.1.call-done = bf16[2,3072,768]{2,1,0:T(8,128)(2,1)} async-done(((bf16[1,3072,768]{2,1,0:T(8,128)(2,1)}), bf16[2,3072,768]{2,1,0:T(8,128)(2,1)}) %all-gather.41.cloned.1.call-update) | async-done | bytes 9437200 | tf_op jit(solution)/shard_map/all_gather | solution.py:383
  734.8 74.9 %while.158 = (s32[]{:T(128)}, f32[2,12,64]{2,1,0:T(8,128)S(1)}, f32[2,12,64]{2,1,0:T(8,128)S(1)}, s32[32]{0:T(128)}, s32[64]{0:T(128)S(1)}, /*index=5*/bf16[2,10...) while((s32[]{:T(128)}, f32[2,12,64]{2,1,0:T(8,128)S(1)}, ...), condition=%wide.region_15.18_spmd.clone, body=%wide.region_12.17_spmd.clone.sunk | while | flops 13185112 | bytes 2059509 | solution.py:110
  810.5 110.3 %while.159 = (s32[]{:T(128)}, f32[2,64,12,64]{1,3,2,0:T(8,128)}, bf16[2,1024,768]{2,1,0:T(8,128)(2,1)}, s32[32]{0:T(128)}, s32[64]{0:T(128)S(1)}, /*index=5*/bf1...) while((s32[]{:T(128)}, f32[2,64,12,64]{1,3,2,0:T(8,128)}, ...), condition=%wide.region_17.20_spmd.clone, body=%wide.region_16.19_spmd.clone.sunk | while | flops 25760344 | bytes 2964732 | solution.py:128
  984.8 130.8 %while.160 = (s32[]{:T(128)}, f32[2,64,12,64]{1,3,2,0:T(8,128)}, bf16[2,1024,768]{2,1,0:T(8,128)(2,1)}, s32[32]{0:T(128)}, s32[64]{0:T(128)S(1)}, /*index=5*/bf1...) while((s32[]{:T(128)}, f32[2,64,12,64]{1,3,2,0:T(8,128)}, ...), condition=%wide.region_24.27_spmd.clone, body=%wide.region_23.26_spmd.clone.sunk | while | flops 38638168 | bytes 3953932 | solution.py:168
  1163.4 185.6 %while.161 = (s32[]{:T(128)}, f32[2,64,12,64]{1,3,2,0:T(8,128)}, f32[2,64,12,64]{1,3,2,0:T(8,128)}, bf16[2,1024,768]{2,1,0:T(8,128)(2,1)}, s32[64]{0:T(128)S(1)}...) while((s32[]{:T(128)}, f32[2,64,12,64]{1,3,2,0:T(8,128)}, ...), condition=%wide.region_26.29_spmd.clone, body=%wide.region_25.28_spmd.clone.sunk | while | flops 51515992 | bytes 5944605 | solution.py:205
  1371.7 116.8 %while.162 = (s32[]{:T(128)}, f32[2,64,12,64]{1,3,2,0:T(8,128)}, bf16[2,1024,768]{2,1,0:T(8,128)(2,1)}, s32[32]{0:T(128)}, s32[64]{0:T(128)S(1)}, /*index=5*/bf1...) while((s32[]{:T(128)}, f32[2,64,12,64]{1,3,2,0:T(8,128)}, ...), condition=%wide.region_33.36_spmd.clone, body=%wide.region_32.35_spmd.clone.sunk | while | flops 38638168 | bytes 7099716 | solution.py:168
  1540.1 154.1 %while.163 = (s32[]{:T(128)}, f32[2,64,12,64]{1,3,2,0:T(8,128)S(1)}, f32[2,64,12,64]{1,3,2,0:T(8,128)S(1)}, bf16[2,1024,768]{2,1,0:T(8,128)(2,1)}, s32[64]{0:T(1...) while((s32[]{:T(128)}, f32[2,64,12,64]{1,3,2,0:T(8,128)S(1)}, ...), condition=%wide.region_35.38_spmd.clone, body=%wide.region_34.37_spmd.clone.sunk | while | flops 51515992 | bytes 6732445 | solution.py:205
  1806.3 189.2 %all-to-all-done = f32[1,2,768,2304]{2,1,0,3:T(2,128)} async-done(((f32[1,2,768,2304]{2,1,0,3:T(2,128)}), f32[1,2,768,2304]{2,1,0,3:T(2,128)}, u32[]{:S(2)}, u32[]{:S(2)}) %all-to-all-start) | async-done | bytes 14155808 | tf_op jit(solution)/shard_map/all_to_all | solution.py:425
  1995.5 59.7 %all-to-all-start.3 = ((f32[1,2,768,3072]{2,1,0,3:T(2,128)}), f32[1,2,768,3072]{2,1,0,3:T(2,128)}, u32[]{:S(2)}, u32[]{:S(2)}) async-start(f32[1,2,768,3072]{2,1,0,3:T(2,128)} %copy.380), calls=%async_computation.6 | async-start | bytes 37748736 | tf_op jit(solution)/shard_map/all_to_all | solution.py:428
  2093.6 294.9 %all-to-all-done.3 = f32[1,2,768,3072]{2,1,0,3:T(2,128)} async-done(((f32[1,2,768,3072]{2,1,0,3:T(2,128)}), f32[1,2,768,3072]{2,1,0,3:T(2,128)}, u32[]{:S(2)}, u32[]{:S(2)}) %all-to-all-start.3) | async-done | bytes 18874400 | tf_op jit(solution)/shard_map/all_to_all | solution.py:428
  2388.5 78.7 %all-to-all-start.2 = ((f32[1,2,768,3072]{2,1,0,3:T(2,128)}), f32[1,2,768,3072]{2,1,0,3:T(2,128)}, u32[]{:S(2)}, u32[]{:S(2)}) async-start(f32[1,2,768,3072]{2,1,0,3:T(2,128)} %copy.378), calls=%async_computation.4 | async-start | bytes 37748736 | tf_op jit(solution)/shard_map/all_to_all | solution.py:427
  2489.2 311.2 %all-to-all-done.2 = f32[1,2,768,3072]{2,1,0,3:T(2,128)} async-done(((f32[1,2,768,3072]{2,1,0,3:T(2,128)}), f32[1,2,768,3072]{2,1,0,3:T(2,128)}, u32[]{:S(2)}, u32[]{:S(2)}) %all-to-all-start.2) | async-done | bytes 18874400 | tf_op jit(solution)/shard_map/all_to_all | solution.py:427
  2822.9 81.6 %reduce-scatter.9.cloned.1.call-done = f32[1,768,192]{1,2,0:T(8,128)} async-done(((f32[2,768,192]{1,2,0:T(8,128)}), f32[1,768,192]{1,2,0:T(8,128)}) %reduce-scatter.9.cloned.1.call-update) | async-done | bytes 589840 | tf_op jit(solution)/shard_map/reduce_scatter | solution.py:435
  2926.7 210.3 %all_to_all.120 = f32[1,4,768,768]{3,1,0,2:T(4,128)} all-to-all(f32[1,4,768,768]{3,1,0,2:T(4,128)} %copy.382), channel_id=1, replica_groups=mesh['ctx'=16,'dp'=2] {'ctx'}, dimensions={2} | all-to-all | bytes 18874368 | tf_op jit(solution)/shard_map/all_to_all | solution.py:341
  3143.4 81.6 %all-gather.55.cloned.1.call-done = f32[4,768,768]{2,1,0:T(8,128)} async-done(((f32[4,48,768]{2,1,0:T(8,128)}), f32[4,768,768]{2,1,0:T(8,128)}) %all-gather.55.cloned.1.call-update) | async-done | bytes 9437200 | tf_op jit(solution)/shard_map/all_gather | solution.py:343
  3296.7 209.7 %all_to_all.121 = f32[1,4,768,768]{3,1,0,2:T(4,128)} all-to-all(f32[1,4,768,768]{3,1,0,2:T(4,128)} %copy.384), channel_id=1, replica_groups=mesh['ctx'=16,'dp'=2] {'ctx'}, dimensions={2} | all-to-all | bytes 18874368 | tf_op jit(solution)/shard_map/all_to_all | solution.py:341
  3512.6 82.0 %all-gather.57.cloned.1.call-done = f32[4,768,768]{2,1,0:T(8,128)} async-done(((f32[4,48,768]{2,1,0:T(8,128)}), f32[4,768,768]{2,1,0:T(8,128)}) %all-gather.57.cloned.1.call-update) | async-done | bytes 9437200 | tf_op jit(solution)/shard_map/all_gather | solution.py:343
  3661.2 209.7 %all_to_all.122 = f32[1,4,768,768]{3,1,0,2:T(4,128)} all-to-all(f32[1,4,768,768]{3,1,0,2:T(4,128)} %copy.386), channel_id=1, replica_groups=mesh['ctx'=16,'dp'=2] {'ctx'}, dimensions={2} | all-to-all | bytes 18874368 | tf_op jit(solution)/shard_map/all_to_all | solution.py:341
  3877.1 82.0 %all-gather.59.cloned.1.call-done = f32[4,768,768]{2,1,0:T(8,128)} async-done(((f32[4,48,768]{2,1,0:T(8,128)}), f32[4,768,768]{2,1,0:T(8,128)}) %all-gather.59.cloned.1.call-update) | async-done | bytes 9437200 | tf_op jit(solution)/shard_map/all_gather | solution.py:343
  4024.9 209.7 %all_to_all.123 = f32[1,4,768,768]{3,1,0,2:T(4,128)} all-to-all(f32[1,4,768,768]{3,1,0,2:T(4,128)} %copy.388), channel_id=1, replica_groups=mesh['ctx'=16,'dp'=2] {'ctx'}, dimensions={2} | all-to-all | bytes 18874368 | tf_op jit(solution)/shard_map/all_to_all | solution.py:341
  4240.9 82.0 %all-gather.61.cloned.1.call-done = f32[4,768,768]{2,1,0:T(8,128)} async-done(((f32[4,48,768]{2,1,0:T(8,128)}), f32[4,768,768]{2,1,0:T(8,128)}) %all-gather.61.cloned.1.call-update) | async-done | bytes 9437200 | tf_op jit(solution)/shard_map/all_gather | solution.py:343
  4388.8 209.7 %all_to_all.124 = f32[1,4,768,768]{3,1,0,2:T(4,128)} all-to-all(f32[1,4,768,768]{3,1,0,2:T(4,128)} %copy.390), channel_id=1, replica_groups=mesh['ctx'=16,'dp'=2] {'ctx'}, dimensions={2} | all-to-all | bytes 18874368 | tf_op jit(solution)/shard_map/all_to_all | solution.py:341
  (2189 shorter events, 2212.9 us)
Async XLA Ops:
  69.0 237.5 %all-gather.39.cloned.1.call-start = ((), (), s32[]{:S(2)}) async-start(), calls=%async_computation.22 | async-start | bytes 5013504 | tf_op jit(solution)/shard_map/all_gather | solution.py:376
  69.8 283.4 %all-gather.29.cloned.1.call-start = ((), (), s32[]{:S(2)}) async-start(), calls=%async_computation.17 | async-start | bytes 3342336 | tf_op jit(solution)/shard_map/all_gather | solution.py:112
  159.4 272.3 %all-gather.27.cloned.1.call-start = ((), (), s32[]{:S(2)}) async-start(), calls=%async_computation.16 | async-start | bytes 3342336 | tf_op jit(solution)/shard_map/all_gather | solution.py:113
  160.3 352.1 %all-gather.33.cloned.1.call-start = ((), (), s32[]{:S(2)}) async-start(), calls=%async_computation.19 | async-start | bytes 3538944 | tf_op jit(solution)/shard_map/all_gather | solution.py:381
  199.5 357.0 %all-gather.37.cloned.1.call-start = ((), (), s32[]{:S(2)}) async-start(), calls=%async_computation.21 | async-start | bytes 14155776 | tf_op jit(solution)/shard_map/all_gather | solution.py:382
  258.7 417.3 %all-gather.41.cloned.1.call-start = ((), (), s32[]{:S(2)}) async-start(), calls=%async_computation.23 | async-start | bytes 14155776 | tf_op jit(solution)/shard_map/all_gather | solution.py:383
  306.5 424.3 %all-gather.45.cloned.1.call-start = ((), (), s32[]{:S(2)}) async-start(), calls=%async_computation.25 | async-start | bytes 3342336 | tf_op jit(solution)/shard_map/all_gather | solution.py:112
  687.4 475.9 %all-gather.47.cloned.1.call-start = ((), (), s32[]{:S(2)}) async-start(), calls=%async_computation.26 | async-start | bytes 3342336 | tf_op jit(solution)/shard_map/all_gather | solution.py:172
  688.6 474.8 %all-gather.49.cloned.1.call-start = ((), (), s32[]{:S(2)}) async-start(), calls=%async_computation.27 | async-start | bytes 3342336 | tf_op jit(solution)/shard_map/all_gather | solution.py:173
  938.0 602.1 %all-gather.51.cloned.1.call-start = ((), (), s32[]{:S(2)}) async-start(), calls=%async_computation.28 | async-start | bytes 3342336 | tf_op jit(solution)/shard_map/all_gather | solution.py:172
  942.7 597.4 %all-gather.53.cloned.1.call-start = ((), (), s32[]{:S(2)}) async-start(), calls=%async_computation.29 | async-start | bytes 3342336 | tf_op jit(solution)/shard_map/all_gather | solution.py:173
  1530.6 207.3 %all-to-all-start.1 = ((f32[1,2,768,768]{2,1,0,3:T(2,128)}), f32[1,2,768,768]{2,1,0,3:T(2,128)}, u32[]{:S(2)}, u32[]{:S(2)}) async-start(f32[1,2,768,768]{2,1,0,3:T(2,128)} %copy.376), calls=%async_computation.2 | async-start | bytes 9437184 | tf_op jit(solution)/shard_map/all_to_all | solution.py:426
  1737.9 257.6 %all-to-all-start = ((f32[1,2,768,2304]{2,1,0,3:T(2,128)}), f32[1,2,768,2304]{2,1,0,3:T(2,128)}, u32[]{:S(2)}, u32[]{:S(2)}) async-start(f32[1,2,768,2304]{2,1,0,3:T(2,128)} %copy.374), calls=%async_computation | async-start | bytes 28311552 | tf_op jit(solution)/shard_map/all_to_all | solution.py:425
  1995.5 393.0 %all-to-all-start.3 = ((f32[1,2,768,3072]{2,1,0,3:T(2,128)}), f32[1,2,768,3072]{2,1,0,3:T(2,128)}, u32[]{:S(2)}, u32[]{:S(2)}) async-start(f32[1,2,768,3072]{2,1,0,3:T(2,128)} %copy.380), calls=%async_computation.6 | async-start | bytes 37748736 | tf_op jit(solution)/shard_map/all_to_all | solution.py:428
  2388.5 412.0 %all-to-all-start.2 = ((f32[1,2,768,3072]{2,1,0,3:T(2,128)}), f32[1,2,768,3072]{2,1,0,3:T(2,128)}, u32[]{:S(2)}, u32[]{:S(2)}) async-start(f32[1,2,768,3072]{2,1,0,3:T(2,128)} %copy.378), calls=%async_computation.4 | async-start | bytes 37748736 | tf_op jit(solution)/shard_map/all_to_all | solution.py:427
  2467.2 342.5 %reduce-scatter.7.cloned.1.call-start = ((), (), s32[]{:S(2)}) async-start(), calls=%async_computation.31 | async-start | bytes 442368 | tf_op jit(solution)/shard_map/reduce_scatter | solution.py:434
  2472.0 340.6 %reduce-scatter.5.cloned.1.call-start = ((), (), s32[]{:S(2)}) async-start(), calls=%async_computation.30 | async-start | bytes 1327104 | tf_op jit(solution)/shard_map/reduce_scatter | solution.py:433
  2480.0 338.0 %reduce-scatter.11.cloned.1.call-start = ((), (), s32[]{:S(2)}) async-start(), calls=%async_computation.33 | async-start | bytes 1769472 | tf_op jit(solution)/shard_map/reduce_scatter | solution.py:436
  2489.2 415.3 %reduce-scatter.9.cloned.1.call-start = ((), (), s32[]{:S(2)}) async-start(), calls=%async_computation.32 | async-start | bytes 1769472 | tf_op jit(solution)/shard_map/reduce_scatter | solution.py:435
  2809.5 415.5 %all-gather.55.cloned.1.call-start = ((), (), s32[]{:S(2)}) async-start(), calls=%async_computation.34 | async-start | bytes 10027008 | tf_op jit(solution)/shard_map/all_gather | solution.py:343
  3143.2 451.5 %all-gather.57.cloned.1.call-start = ((), (), s32[]{:S(2)}) async-start(), calls=%async_computation.35 | async-start | bytes 10027008 | tf_op jit(solution)/shard_map/all_gather | solution.py:343
  3512.6 446.6 %all-gather.59.cloned.1.call-start = ((), (), s32[]{:S(2)}) async-start(), calls=%async_computation.36 | async-start | bytes 10027008 | tf_op jit(solution)/shard_map/all_gather | solution.py:343
  3877.1 445.8 %all-gather.61.cloned.1.call-start = ((), (), s32[]{:S(2)}) async-start(), calls=%async_computation.37 | async-start | bytes 10027008 | tf_op jit(solution)/shard_map/all_gather | solution.py:343
  4240.8 459.0 %all-gather.63.cloned.1.call-start = ((), (), s32[]{:S(2)}) async-start(), calls=%async_computation.38 | async-start | bytes 10027008 | tf_op jit(solution)/shard_map/all_gather | solution.py:343
  (260 other events, 9026.8 us)
Sparse Core Ops, SparseCore 0:
  10.9 49.8 all-gather.22
  66.8 89.0 all-gather.24
  158.7 38.3 all-gather.30
  199.8 52.1 all-gather.34
  254.7 51.7 all-gather.38
  309.2 43.9 all-gather.28
  356.1 44.2 all-gather.26
  401.9 34.8 all-gather.32
  438.4 117.9 all-gather.36
  557.9 118.0 all-gather.40
  685.6 45.1 all-gather.44
  733.5 44.1 all-gather.42
  780.0 44.0 all-gather.46
  938.1 46.5 all-gather.48
  986.8 44.6 all-gather.50
  1371.8 44.4 all-gather.52
  2486.7 18.5 reduce-scatter.4
  2507.5 21.7 reduce-scatter.10
  2809.7 94.7 reduce-scatter.8
  3143.3 81.6 all-gather.54
  3512.7 81.8 all-gather.56
  3877.2 81.8 all-gather.58
  4240.9 81.8 all-gather.60
  4604.9 83.4 all-gather.62
  (1 shorter events, 12.3 us)
where the time goes:
time: 4780 us; the launch traced here: 4750 us
  waiting for transfers between devices  1660 us (35%)
  blocking collectives  1210 us (25%)
  local copies, waits for them, and re-layouts  707 us (15%)
  matrix products  621 us (13%)
  other arithmetic  359 us (8%)
  starting transfers between devices  157 us (3%)
    all_to_all x5, blocking collectives, gram_all(): lax.all_to_all(terms[None], 'ctx', split_axis=2, concat_axis=0, tiled=True)  1050 us
    all_gather x5, waiting for transfers between devices, gram_all(): return lax.all_gather(shared, 'ctx', axis=1, tiled=True)  328 us
    all_to_all x1, waiting for transfers between devices, body(): lax.all_to_all(cols[2][None], 'ctx', split_axis=3, concat_axis=0, tiled=T...  311 us
    all_to_all x1, waiting for transfers between devices, body(): lax.all_to_all(cols[3][None], 'ctx', split_axis=3, concat_axis=0, tiled=T...  295 us
    all_to_all x1, waiting for transfers between devices, body(): lax.all_to_all(cols[0][None], 'ctx', split_axis=3, concat_axis=0, tiled=T...  189 us
    add x129, other arithmetic, block_positions(): jnp.repeat(blocks, block_len, total_repeat_length=row_count) * block_len  168 us
    dot_general x5, matrix products, body(): jnp.einsum('kij,kjl->kil', grams, grams, precision=highest)  144 us
    dynamic_slice x192, local copies, waits for them, and re-layouts, take_rows(): return lax.dynamic_slice_in_dim(array, offset, row_count, 1)  141 us
  transfers between devices with their start and end apart: 30, of which 18 were waited for; matrix products, arithmetic and copies ran while one was open for 27% of the time, Pallas kernels for 0%

commit v1 on v0

v1 whole, which is shorter than its diff:
```python
import functools
import math

import jax
import jax.numpy as jnp
from jax import lax
from jax.experimental import pallas as pl
from jax.experimental.pallas import tpu as pltpu
from jax.sharding import PartitionSpec as P

HEADS = 12
NS_STEPS = 5
STEP = 10
PIECES = 8

norm_epsilon = 1e-05
neg_large = -1e30
score_scale = 0.125
coef_first = 3.4445
coef_second = -4.775
coef_third = 2.0315
ortho_epsilon = 1e-07
muon_rate = 0.15
muon_moment = 0.95
muon_decay = 0.01
adam_rate = 0.3
beta_first = 0.9
beta_second = 0.95
adam_epsilon = 1e-08
gelu_inner = 0.7978845608
gelu_cubic = 0.044715
shifts = (0.0, 0.0, 0.17, 1.0, 0.8)

f32 = jnp.float32
bf16 = jnp.bfloat16
vmem_limit = 56 * 1024 * 1024


def mm(left, right):
    return jnp.dot(left, right, preferred_element_type=f32)


def mm_nt(left, right):
    return lax.dot_general(left, right, (((1,), (1,)), ((), ())), preferred_element_type=f32)


def mm_tn(left, right):
    return lax.dot_general(left, right, (((0,), (0,)), ((), ())), preferred_element_type=f32)


def cost(micros):
    return pl.CostEstimate(
        flops=int(micros * 1e9), bytes_accessed=int(micros * 1e6), transcendentals=0
    )


def params(grid_dims):
    return pltpu.CompilerParams(
        dimension_semantics=("arbitrary",) * grid_dims, vmem_limit_bytes=vmem_limit
    )


def normalized(values_in):
    centred = values_in - jnp.mean(values_in, axis=-1, keepdims=True)
    inv_std = lax.rsqrt(jnp.mean(centred * centred, axis=-1, keepdims=True) + norm_epsilon)
    return centred * inv_std, inv_std


def norm_backward(grad_out, normed, inv_std, gain):
    scaled = grad_out * gain
    return inv_std * (
        scaled
        - jnp.mean(scaled, axis=-1, keepdims=True)
        - normed * jnp.mean(scaled * normed, axis=-1, keepdims=True)
    )


def pair_lanes(values_in, local, start, size):
    return jnp.concatenate(
        [values_in[:local, start : start + size], values_in[local:, start : start + size]], axis=1
    )


def join_heads(ref, local, hd):
    rows = []
    for s in range(2):
        rows.append(
            jnp.concatenate(
                [ref[h][:, s * hd : (s + 1) * hd].astype(f32) for h in range(HEADS)], axis=1
            )
        )
    return jnp.concatenate(rows, axis=0)


def qkv_kernel(x_ref, vec_ref, w_ref, a_ref, out_ref, proj_ref):
    step = pl.program_id(0)
    steps, _, chunk = proj_ref.shape
    local = out_ref.shape[1]
    hd = out_ref.shape[2] // 6
    width = x_ref.shape[1]

    @pl.when(step == 0)
    def _():
        normed, _ = normalized(x_ref[...].astype(f32))
        a_ref[...] = (normed * vec_ref[0:1, :] + vec_ref[1:2, :]).astype(bf16)

    proj_ref[step] = mm_nt(a_ref[...], w_ref[...].reshape(chunk, width))

    @pl.when(step == steps - 1)
    def _():
        proj = jnp.concatenate([proj_ref[i] for i in range(steps)], axis=1)
        bias = (vec_ref[2:3, :], jnp.zeros((1, width), f32), vec_ref[3:4, :])
        for part in range(3):
            piece = proj[:, part * width : (part + 1) * width] + bias[part]
            for h in range(HEADS):
                out_ref[h, :, part * 2 * hd : (part + 1) * 2 * hd] = pair_lanes(
                    piece, local, h * hd, hd
                ).astype(bf16)
        for h in range(HEADS, out_ref.shape[0]):
            out_ref[h] = jnp.zeros(out_ref.shape[1:], bf16)


def shard_blocks(array, start, own, steps):
    ctx, _, width = array.shape
    group = ctx // steps
    if own % 16 == 0 and start % own == 0:
        return array, pl.BlockSpec(
            (group, own, width), lambda i: (i if steps > 1 else 0, start // own, 0)
        )
    part = array[:, start : start + own].reshape(steps, group * own, width)
    return part, pl.BlockSpec((1, group * own, width), lambda i: (i if steps > 1 else 0, 0, 0))


def qkv_forward(x, vec, weights, at, own_in, local):
    rows, width = x.shape
    ctx = weights.shape[0]
    hd = width // HEADS
    steps = 4
    w_array, w_spec = shard_blocks(weights, at, own_in, steps)
    whole = lambda i: (0, 0)
    return pl.pallas_call(
        qkv_kernel,
        grid=(steps,),
        in_specs=[
            pl.BlockSpec((rows, width), whole),
            pl.BlockSpec(vec.shape, whole),
            w_spec,
        ],
        out_specs=[
            pl.BlockSpec((rows, width), whole),
            pl.BlockSpec((ctx, local, 6 * hd), lambda i: (0, 0, 0)),
        ],
        out_shape=[
            jax.ShapeDtypeStruct((rows, width), bf16),
            jax.ShapeDtypeStruct((ctx, local, 6 * hd), bf16),
        ],
        scratch_shapes=[pltpu.VMEM((steps, rows, 3 * width // steps), f32)],
        compiler_params=params(1),
        cost_estimate=cost(5),
        name="qkv_forward",
    )(x, vec, w_array)


def head_qkv_kernel(head_ref, x_ref, vec_ref, bias_ref, w_ref, a_ref, out_ref, w_all_ref, own_ref):
    shards, rows, width = x_ref.shape
    local = rows // 2
    hd = out_ref.shape[1] // 6

    @pl.when(pl.program_id(0) == 0)
    def _():
        w_all_ref[...] = w_ref[...].reshape(w_all_ref.shape)
        for part in range(3):
            first = pl.multiple_of(part * width + head_ref[0] * hd, hd)
            own_ref[part * hd : (part + 1) * hd, :] = w_all_ref[pl.ds(first, hd), :]

    normed, _ = normalized(x_ref[...].reshape(shards * rows, width).astype(f32))
    first_in = (normed * vec_ref[0:1, :] + vec_ref[1:2, :]).astype(bf16)
    a_ref[...] = first_in.reshape(shards, rows, width)
    proj = (mm_nt(first_in, own_ref[...]) + bias_ref[...]).reshape(shards, 2, local, 3 * hd)
    sides = [proj[:, s].reshape(shards * local, 3 * hd) for s in range(2)]
    for part in range(3):
        cut = slice(part * hd, (part + 1) * hd)
        out_ref[:, 2 * part * hd : 2 * (part + 1) * hd] = jnp.concatenate(
            [sides[0][:, cut], sides[1][:, cut]], axis=1
        ).astype(bf16)


def head_qkv(head, tokens_all, tokens_at, vec, bias, weights, at, own_in, rows):
    ctx, _, width = tokens_all.shape
    hd = width // HEADS
    local = rows // 2
    x_array, x_spec = shard_blocks(tokens_all, tokens_at, rows, ctx // 4)
    w_array, w_spec = shard_blocks(weights, at, own_in, 1)
    whole = lambda i: (0, 0)
    return pl.pallas_call(
        head_qkv_kernel,
        grid=(ctx // 4,),
        in_specs=[
            pl.BlockSpec(memory_space=pltpu.SMEM),
            x_spec,
            pl.BlockSpec(vec.shape, whole),
            pl.BlockSpec(bias.shape, whole),
            w_spec,
        ],
        out_specs=[
            pl.BlockSpec((4, rows, width), lambda i: (i, 0, 0)),
            pl.BlockSpec((4 * local, 6 * hd), lambda i: (i, 0)),
        ],
        out_shape=[
            jax.ShapeDtypeStruct((ctx, rows, width), bf16),
            jax.ShapeDtypeStruct((ctx * local, 6 * hd), bf16),
        ],
        scratch_shapes=[pltpu.VMEM((3 * width, width), bf16), pltpu.VMEM((3 * hd, width), bf16)],
        compiler_params=params(1),
        cost_estimate=cost(6),
        name="head_qkv",
    )(head, x_array, vec, bias, w_array)


def lane_masks(rows, lanes):
    lane = lax.broadcasted_iota(jnp.int32, (rows, lanes), 1)
    first = jnp.where(lane < lanes // 2, 1.0, 0.0)
    return first.astype(bf16), (1.0 - first).astype(bf16)


def attn_fwd_kernel(qpos_ref, kpos_ref, q_ref, k_ref, v_ref, of_ref, ob_ref, p_ref):
    allowed = kpos_ref[...] <= qpos_ref[...]
    q_masks = lane_masks(*q_ref.shape)
    v_masks = lane_masks(*v_ref.shape)
    out = jnp.zeros(of_ref.shape, f32)
    for s in range(2):
        scores = mm_nt(q_ref[...] * q_masks[s], k_ref[...]) * score_scale
        scores = jnp.where(allowed, scores, neg_large)
        expo = jnp.exp(scores - jnp.max(scores, axis=-1, keepdims=True))
        prob = (expo * (1.0 / jnp.sum(expo, axis=-1, keepdims=True))).astype(bf16)
        p_ref[s] = prob
        out = out + mm(prob, v_ref[...] * v_masks[s])
    of_ref[...] = out
    ob_ref[...] = out.astype(bf16)


def attn_forward(qkv, qpos, kpos):
    length, lanes = qkv.shape
    pair = lanes // 3
    tile = min(256, length)
    return pl.pallas_call(
        attn_fwd_kernel,
        grid=(length // tile,),
        in_specs=[
            pl.BlockSpec((tile, 1), lambda i: (i, 0)),
            pl.BlockSpec((1, length), lambda i: (0, 0)),
            pl.BlockSpec((tile, pair), lambda i: (i, 0)),
            pl.BlockSpec((length, pair), lambda i: (0, 1)),
            pl.BlockSpec((length, pair), lambda i: (0, 2)),
        ],
        out_specs=[
            pl.BlockSpec((tile, pair), lambda i: (i, 0)),
            pl.BlockSpec((tile, pair), lambda i: (i, 0)),
            pl.BlockSpec((2, tile, length), lambda i: (0, i, 0)),
        ],
        out_shape=[
            jax.ShapeDtypeStruct((length, pair), f32),
            jax.ShapeDtypeStruct((length, pair), bf16),
            jax.ShapeDtypeStruct((2, length, length), bf16),
        ],
        compiler_params=params(1),
        cost_estimate=cost(8),
        name="attn_forward",
    )(qpos, kpos, qkv, qkv, qkv)


def attn_bwd_kernel(q_ref, go_ref, of_ref, p_ref, k_ref, v_ref, out_ref, dk_ref, dv_ref):
    step = pl.program_id(0)
    tile, pair = q_ref.shape
    masks = lane_masks(tile, pair)
    k_masks = lane_masks(*k_ref.shape)

    @pl.when(step == 0)
    def _():
        dk_ref[...] = jnp.zeros_like(dk_ref)
        dv_ref[...] = jnp.zeros_like(dv_ref)

    dq = jnp.zeros((tile, pair), f32)
    for s in range(2):
        go = go_ref[...] * masks[s]
        row_dot = jnp.sum(go.astype(f32) * of_ref[...], axis=-1, keepdims=True)
        prob = p_ref[s]
        grad_prob = mm_nt(go, v_ref[...])
        ds = (prob.astype(f32) * (grad_prob - row_dot)).astype(bf16)
        dv_ref[...] += mm_tn(go, prob)
        dk_ref[...] += mm_tn(q_ref[...] * masks[s], ds)
        dq = dq + mm(ds, k_ref[...] * k_masks[s])
    out_ref[pl.ds(pl.multiple_of(step * tile, tile), tile), 0:pair] = (dq * score_scale).astype(bf16)

    @pl.when(step == pl.num_programs(0) - 1)
    def _():
        out_ref[:, pair : 2 * pair] = (dk_ref[...].T * score_scale).astype(bf16)
        out_ref[:, 2 * pair :] = dv_ref[...].T.astype(bf16)


def attn_backward(qkv, go, out_full, prob):
    length, lanes = qkv.shape
    pair = lanes // 3
    tile = min(256, length)
    return pl.pallas_call(
        attn_bwd_kernel,
        grid=(length // tile,),
        in_specs=[
            pl.BlockSpec((tile, pair), lambda i: (i, 0)),
            pl.BlockSpec((tile, pair), lambda i: (i, 0)),
            pl.BlockSpec((tile, pair), lambda i: (i, 0)),
            pl.BlockSpec((2, tile, length), lambda i: (0, i, 0)),
            pl.BlockSpec((length, pair), lambda i: (0, 1)),
            pl.BlockSpec((length, pair), lambda i: (0, 2)),
        ],
        out_specs=pl.BlockSpec((length, lanes), lambda i: (0, 0)),
        out_shape=jax.ShapeDtypeStruct((length, lanes), bf16),
        scratch_shapes=[pltpu.VMEM((pair, length), f32), pltpu.VMEM((pair, length), f32)],
        compiler_params=params(1),
        cost_estimate=cost(8),
        name="attn_backward",
    )(qkv, go, out_full, prob, qkv, qkv)


def mlp_fwd_kernel(o_ref, x_ref, vec_ref, mix_ref, fc_ref, red_ref, mid_ref, c_ref, h_ref, out_ref):
    step = pl.program_id(0)
    rows, width = x_ref.shape

    @pl.when(step == 0)
    def _():
        mixed = join_heads(o_ref, rows // 2, o_ref.shape[2] // 2).astype(bf16)
        mix_w = mix_ref[...].reshape(width, width)
        middle = x_ref[...].astype(f32) + (mm_nt(mixed, mix_w) + vec_ref[4:5, :])
        mid_ref[...] = middle
        normed, _ = normalized(middle)
        c_ref[...] = (normed * vec_ref[5:6, :] + vec_ref[6:7, :]).astype(bf16)
        out_ref[...] = middle + vec_ref[7:8, :]

    hidden = mm_nt(c_ref[...], fc_ref[...].reshape(width, width))
    hidden = hidden + vec_ref[pl.ds(PIECES + step, 1), :]
    h_ref[...] = hidden
    inner = jnp.tanh(gelu_inner * (hidden + gelu_cubic * hidden * hidden * hidden))
    active = (0.5 * hidden * (1.0 + inner)).astype(bf16)
    out_ref[...] += mm(active, red_ref[...].reshape(width, width))


def mlp_forward(o_pack, x, vec, weights, at, own_ff, own_mix):
    rows, width = x.shape
    hidden = weights.shape[0] * own_ff
    steps = hidden // width
    fc_array, fc_spec = shard_blocks(weights, at["fc"], own_ff, steps)
    red_array, red_spec = shard_blocks(weights, at["red"], own_ff, steps)
    mix_array, mix_spec = shard_blocks(weights, at["mix"], own_mix, 1)
    whole = lambda i: (0, 0)
    return pl.pallas_call(
        mlp_fwd_kernel,
        grid=(steps,),
        in_specs=[
            pl.BlockSpec(o_pack.shape, lambda i: (0, 0, 0)),
            pl.BlockSpec((rows, width), whole),
            pl.BlockSpec(vec.shape, whole),
            mix_spec,
            fc_spec,
            red_spec,
        ],
        out_specs=[
            pl.BlockSpec((rows, width), whole),
            pl.BlockSpec((rows, width), whole),
            pl.BlockSpec((rows, width), lambda i: (0, i)),
            pl.BlockSpec((rows, width), whole),
        ],
        out_shape=[
            jax.ShapeDtypeStruct((rows, width), f32),
            jax.ShapeDtypeStruct((rows, width), bf16),
            jax.ShapeDtypeStruct((rows, hidden), f32),
            jax.ShapeDtypeStruct((rows, width), f32),
        ],
        compiler_params=params(1),
        cost_estimate=cost(8),
        name="mlp_forward",
    )(o_pack, x, vec, mix_array, fc_array, red_array)


def gelu_slope(hidden):
    square = hidden * hidden
    inner = jnp.tanh(gelu_inner * (hidden + gelu_cubic * hidden * square))
    slope = 0.5 * (1.0 + inner) + (0.5 * gelu_inner) * hidden * (1.0 - inner * inner) * (
        1.0 + (3.0 * gelu_cubic) * square
    )
    return inner, slope


def mlp_bwd_kernel(
    gr_ref, mid_ref, h_ref, vec_ref, mix_ref, fc_ref, red_ref,
    gz_ref, gmid_ref, gy_ref, go_ref, vg_ref, gc_ref,
):
    step = pl.program_id(0)
    rows, width = gr_ref.shape

    @pl.when(step == 0)
    def _():
        gz_ref[...] = gr_ref[...].astype(bf16)
        gc_ref[...] = jnp.zeros_like(gc_ref)

    _, slope = gelu_slope(h_ref[...])
    grad_hidden = (mm_nt(gz_ref[...], red_ref[...].reshape(width, width)) * slope).astype(bf16)
    vg_ref[pl.ds(4 + step, 1), :] = jnp.sum(grad_hidden.astype(f32), axis=0, keepdims=True)
    gc_ref[...] += mm(grad_hidden, fc_ref[...].reshape(width, width))

    @pl.when(step == pl.num_programs(0) - 1)
    def _():
        grad = gr_ref[...].astype(f32)
        normed, inv_std = normalized(mid_ref[...])
        grad_second = gc_ref[...]
        grad_mid = grad + norm_backward(grad_second, normed, inv_std, vec_ref[5:6, :])
        gmid_ref[...] = grad_mid
        gy = grad_mid.astype(bf16)
        gy_ref[...] = gy
        vg_ref[0:1, :] = jnp.sum(gy.astype(f32), axis=0, keepdims=True)
        vg_ref[1:2, :] = jnp.sum(grad_second * normed, axis=0, keepdims=True)
        vg_ref[2:3, :] = jnp.sum(grad_second, axis=0, keepdims=True)
        vg_ref[3:4, :] = jnp.sum(gz_ref[...].astype(f32), axis=0, keepdims=True)
        grad_attn = mm(gy, mix_ref[...].reshape(width, width))
        hd = go_ref.shape[2] // 2
        for h in range(HEADS):
            go_ref[h] = pair_lanes(grad_attn, rows // 2, h * hd, hd).astype(bf16)
        for h in range(HEADS, go_ref.shape[0]):
            go_ref[h] = jnp.zeros(go_ref.shape[1:], bf16)


def mlp_backward(gr, mid, hidden, vec, weights, at, own_ff, own_mix):
    rows, width = mid.shape
    ctx = weights.shape[0]
    steps = hidden.shape[1] // width
    hd = width // HEADS
    fc_array, fc_spec = shard_blocks(weights, at["fc"], own_ff, steps)
    red_array, red_spec = shard_blocks(weights, at["red"], own_ff, steps)
    mix_array, mix_spec = shard_blocks(weights, at["mix"], own_mix, 1)
    whole = lambda i: (0, 0)
    return pl.pallas_call(
        mlp_bwd_kernel,
        grid=(steps,),
        in_specs=[
            pl.BlockSpec((rows, width), whole),
            pl.BlockSpec((rows, width), whole),
            pl.BlockSpec((rows, width), lambda i: (0, i)),
            pl.BlockSpec(vec.shape, whole),
            mix_spec,
            fc_spec,
            red_spec,
        ],
        out_specs=[
            pl.BlockSpec((rows, width), whole),
            pl.BlockSpec((rows, width), whole),
            pl.BlockSpec((rows, width), whole),
            pl.BlockSpec((ctx, rows // 2, 2 * hd), lambda i: (0, 0, 0)),
            pl.BlockSpec((PIECES, width), whole),
        ],
        out_shape=[
            jax.ShapeDtypeStruct((rows, width), bf16),
            jax.ShapeDtypeStruct((rows, width), f32),
            jax.ShapeDtypeStruct((rows, width), bf16),
            jax.ShapeDtypeStruct((ctx, rows // 2, 2 * hd), bf16),
            jax.ShapeDtypeStruct((PIECES, width), f32),
        ],
        scratch_shapes=[pltpu.VMEM((rows, width), f32)],
        compiler_params=params(1),
        cost_estimate=cost(8),
        name="mlp_backward",
    )(gr, mid, hidden, vec, mix_array, fc_array, red_array)


def qkv_bwd_kernel(d_ref, x_ref, gmid_ref, vec_ref, w_ref, gin_ref, vg_ref, d_all_ref, ga_ref):
    step = pl.program_id(0)
    steps, rows, chunk = d_all_ref.shape
    width = x_ref.shape[1]

    @pl.when(step == 0)
    def _():
        hd = d_ref.shape[2] // 6
        parts = []
        for part in range(3):
            for s in range(2):
                start = (2 * part + s) * hd
                parts.append(
                    jnp.concatenate(
                        [d_ref[h, :, start : start + hd].astype(f32) for h in range(HEADS)], axis=1
                    )
                )
        joined = jnp.concatenate(
            [jnp.concatenate([parts[2 * part], parts[2 * part + 1]], axis=0) for part in range(3)],
            axis=1,
        )
        vg_ref[...] = jnp.zeros_like(vg_ref)
        vg_ref[2:3, :] = jnp.sum(joined[:, :width], axis=0, keepdims=True)
        vg_ref[3:4, :] = jnp.sum(joined[:, 2 * width :], axis=0, keepdims=True)
        for i in range(steps):
            d_all_ref[i] = joined[:, i * chunk : (i + 1) * chunk].astype(bf16)
        ga_ref[...] = jnp.zeros_like(ga_ref)

    ga_ref[...] += mm(d_all_ref[step], w_ref[...].reshape(chunk, width))

    @pl.when(step == steps - 1)
    def _():
        normed, inv_std = normalized(x_ref[...].astype(f32))
        grad_first = ga_ref[...]
        gin_ref[...] = gmid_ref[...] + norm_backward(grad_first, normed, inv_std, vec_ref[0:1, :])
        vg_ref[0:1, :] = jnp.sum(grad_first * normed, axis=0, keepdims=True)
        vg_ref[1:2, :] = jnp.sum(grad_first, axis=0, keepdims=True)


def qkv_backward(dqkv, x, gmid, vec, weights, at, own_in):
    rows, width = x.shape
    steps = 4
    w_array, w_spec = shard_blocks(weights, at, own_in, steps)
    whole = lambda i: (0, 0)
    return pl.pallas_call(
        qkv_bwd_kernel,
        grid=(steps,),
        in_specs=[
            pl.BlockSpec(dqkv.shape, lambda i: (0, 0, 0)),
            pl.BlockSpec((rows, width), whole),
            pl.BlockSpec((rows, width), whole),
            pl.BlockSpec(vec.shape, whole),
            w_spec,
        ],
        out_specs=[
            pl.BlockSpec((rows, width), whole),
            pl.BlockSpec((PIECES, width), whole),
        ],
        out_shape=[
            jax.ShapeDtypeStruct((rows, width), f32),
            jax.ShapeDtypeStruct((PIECES, width), f32),
        ],
        scratch_shapes=[
            pltpu.VMEM((steps, rows, 3 * width // steps), bf16),
            pltpu.VMEM((rows, width), f32),
        ],
        compiler_params=params(1),
        cost_estimate=cost(5),
        name="qkv_backward",
    )(dqkv, x, gmid, vec, w_array)


def hidden_grads_kernel(c_ref, gz_ref, fc_ref, red_ref, bias_ref, gfc_ref, gred_ref):
    own, width = gfc_ref.shape
    second = c_ref[...].reshape(-1, width)
    branch = gz_ref[...].reshape(-1, width)
    hidden = mm_nt(fc_ref[...], second) + bias_ref[...]
    inner, slope = gelu_slope(hidden)
    active = (0.5 * hidden * (1.0 + inner)).astype(bf16)
    grad_hidden = (mm_nt(red_ref[...], branch) * slope).astype(bf16)

    @pl.when(pl.program_id(0) == 0)
    def _():
        gfc_ref[...] = jnp.zeros_like(gfc_ref)
        gred_ref[...] = jnp.zeros_like(gred_ref)

    gfc_ref[...] += mm(grad_hidden, second)
    gred_ref[...] += mm(active, branch)


def hidden_grads(c_all, c_at, gz_all, gz_at, fc_own, red_own, bias, rows):
    ctx, _, width = c_all.shape
    own_ff = fc_own.shape[0]
    steps = ctx // 4
    c_array, c_spec = shard_blocks(c_all, c_at, rows, steps)
    gz_array, gz_spec = shard_blocks(gz_all, gz_at, rows, steps)
    whole = lambda i: (0, 0)
    return pl.pallas_call(
        hidden_grads_kernel,
        grid=(steps,),
        in_specs=[
            c_spec,
            gz_spec,
            pl.BlockSpec((own_ff, width), whole),
            pl.BlockSpec((own_ff, width), whole),
            pl.BlockSpec((own_ff, 1), whole),
        ],
        out_specs=[pl.BlockSpec((own_ff, width), whole)] * 2,
        out_shape=[jax.ShapeDtypeStruct((own_ff, width), f32)] * 2,
        compiler_params=params(1),
        cost_estimate=cost(6),
        name="hidden_grads",
    )(c_array, gz_array, fc_own, red_own, bias)


def hidden_ready_kernel(c_ref, fc_ref, bias_ref, u_ref, slope_ref):
    width = fc_ref.shape[1]
    hidden = mm_nt(fc_ref[...], c_ref[...].reshape(-1, width)) + bias_ref[...]
    inner, slope = gelu_slope(hidden)
    u_ref[...] = (0.5 * hidden * (1.0 + inner)).astype(bf16)
    slope_ref[...] = slope


def rows_by_z(c_all, c_at, rows):
    ctx, _, width = c_all.shape
    assert c_at % rows == 0
    view = c_all.reshape(ctx // 16, 4, 4, *c_all.shape[1:])
    return view, pl.BlockSpec(
        (1, 4, 1, rows, width),
        lambda i: (i // 4, 0, (i % 2) * 2 + (i // 2) % 2, c_at // rows, 0),
    )


def hidden_ready(c_all, c_at, fc_own, bias, rows):
    ctx, _, width = c_all.shape
    own_ff = fc_own.shape[0]
    c_array, c_spec = rows_by_z(c_all, c_at, rows)
    whole = lambda i: (0, 0)
    return pl.pallas_call(
        hidden_ready_kernel,
        grid=(ctx // 4,),
        in_specs=[
            c_spec,
            pl.BlockSpec((own_ff, width), whole),
            pl.BlockSpec((own_ff, 1), whole),
        ],
        out_specs=[pl.BlockSpec((own_ff, 4 * rows), lambda i: (0, i))] * 2,
        out_shape=[
            jax.ShapeDtypeStruct((own_ff, ctx * rows), bf16),
            jax.ShapeDtypeStruct((own_ff, ctx * rows), f32),
        ],
        compiler_params=params(1),
        cost_estimate=cost(5),
        name="hidden_ready",
    )(c_array, fc_own, bias)


def hidden_last_kernel(c_ref, gz_ref, u_ref, slope_ref, red_ref, gfc_ref, gred_ref):
    width = red_ref.shape[1]
    second = c_ref[...].reshape(-1, width)
    branch = gz_ref[...].reshape(-1, width)
    grad_hidden = (mm_nt(red_ref[...], branch) * slope_ref[...]).astype(bf16)

    @pl.when(pl.program_id(0) == 0)
    def _():
        gfc_ref[...] = jnp.zeros_like(gfc_ref)
        gred_ref[...] = jnp.zeros_like(gred_ref)

    gred_ref[...] += mm(u_ref[...], branch)
    gfc_ref[...] += mm(grad_hidden, second)


def hidden_last(c_all, c_at, gz_all, active, slope, red_own, rows):
    steps, _, width = gz_all.shape
    own_ff = red_own.shape[0]
    c_array, c_spec = rows_by_z(c_all, c_at, rows)
    whole = lambda i: (0, 0)
    return pl.pallas_call(
        hidden_last_kernel,
        grid=(steps,),
        in_specs=[
            c_spec,
            pl.BlockSpec((1, 4 * rows, width), lambda i: (i, 0, 0)),
            pl.BlockSpec((own_ff, 4 * rows), lambda i: (0, i)),
            pl.BlockSpec((own_ff, 4 * rows), lambda i: (0, i)),
            pl.BlockSpec((own_ff, width), whole),
        ],
        out_specs=[pl.BlockSpec((own_ff, width), whole)] * 2,
        out_shape=[jax.ShapeDtypeStruct((own_ff, width), f32)] * 2,
        compiler_params=params(1),
        cost_estimate=cost(5),
        name="hidden_last",
    )(c_array, gz_all, active, slope, red_own)


def head_grads_kernel(pack_ref, rows_ref, out_ref):
    length, lanes = pack_ref.shape
    _, rows, width = rows_ref.shape
    local = rows // 2
    hd = width // HEADS
    for s in range(2):
        piece = rows_ref[:, s * local : (s + 1) * local, :].reshape(length, width)
        result = mm_tn(pack_ref[...], piece)
        for part in range(out_ref.shape[0] // hd):
            start = (2 * part + s) * hd
            if s == 0:
                out_ref[part * hd : (part + 1) * hd, :] = result[start : start + hd]
            else:
                out_ref[part * hd : (part + 1) * hd, :] += result[start : start + hd]


def head_grads(pack, rows_all, at, rows):
    length, lanes = pack.shape
    ctx, _, width = rows_all.shape
    rows_array, rows_spec = shard_blocks(rows_all, at, rows, 1)
    return pl.pallas_call(
        head_grads_kernel,
        grid=(1,),
        in_specs=[
            pl.BlockSpec((length, lanes), lambda i: (0, 0)),
            rows_spec,
        ],
        out_specs=pl.BlockSpec((lanes // 2, width), lambda i: (0, 0)),
        out_shape=jax.ShapeDtypeStruct((lanes // 2, width), f32),
        compiler_params=params(1),
        cost_estimate=cost(4),
        name="head_grads",
    )(pack, rows_array)


def copy_all(moves, sems):
    copies = [pltpu.make_async_copy(src, dst, sems.at[i]) for i, (src, dst) in enumerate(moves)]
    for copy in copies:
        copy.start()
    for copy in copies:
        copy.wait()


def ns_kernel(own, parts_count, role_ref, *refs):
    parts, (sums_ref, out_ref) = refs[:parts_count], refs[parts_count : parts_count + 2]
    y_ref, full_ref, low_ref, gram_ref, poly_ref, sems = refs[parts_count + 2 :]
    length, side = y_ref.shape
    own_in, own_ff, own_mix = own
    tile = 256
    role = role_ref[0]
    is_in, is_mix = role == 0, role == 3
    is_long = (role == 1) | (role == 2)
    kinds = ((is_long, length, own_ff), (is_in, 3 * side, own_in), (is_mix, side, own_mix))
    chunks = jnp.where(is_mix, 1, jnp.where(is_in, 3, length // side))

    @pl.when(is_long)
    def _():
        moves, start = [], 0
        for part in parts:
            moves.append((part, y_ref.at[start : start + part.shape[0]]))
            start += part.shape[0]
        copy_all(moves, sems)

    @pl.when(is_in)
    def _():
        copy_all([(sums_ref, y_ref.at[: 3 * side])], sems)

    @pl.when(is_mix)
    def _():
        copy_all([(sums_ref.at[:side], y_ref.at[:side])], sems)

    eye = jnp.where(
        lax.broadcasted_iota(jnp.int32, (side, side), 0)
        == lax.broadcasted_iota(jnp.int32, (side, side), 1),
        1.0,
        0.0,
    )

    def each_chunk(work):
        def one(i, carry):
            work(pl.ds(pl.multiple_of(i * side, side), side))
            return carry

        lax.fori_loop(0, chunks, one, 0)

    def gram():
        for kind, columns, _ in kinds:

            @pl.when(kind)
            def _():
                for i in range(side // tile):
                    rows = slice(i * tile, (i + 1) * tile)
                    gram_ref[rows, i * tile :] = mm_nt(
                        low_ref[rows, :columns], low_ref[i * tile :, :columns]
                    )

        for i in range(side // tile):
            for j in range(i + 1, side // tile):
                gram_ref[j * tile : (j + 1) * tile, i * tile : (i + 1) * tile] = gram_ref[
                    i * tile : (i + 1) * tile, j * tile : (j + 1) * tile
                ].T

    def load(cols):
        low_ref[:, cols] = y_ref[cols, :].T

    each_chunk(load)
    gram()
    scale = 1.0 / (jnp.sqrt(jnp.sum(gram_ref[...] * eye, keepdims=True)) + ortho_epsilon)
    gram_ref[...] = gram_ref[...] * (scale * scale)

    linear_only = coef_second * gram_ref[...]
    low_gram = gram_ref[...].astype(bf16)
    poly_ref[...] = (scale * (linear_only + coef_third * mm(low_gram, low_gram))).astype(bf16)

    def first(cols):
        matrix = low_ref[:, cols]
        fresh = (coef_first * scale) * matrix.astype(f32) + mm(poly_ref[...], matrix)
        full_ref[:, cols] = fresh
        low_ref[:, cols] = fresh.astype(bf16)

    each_chunk(first)
    gram()

    def polynomial(k):
        shift = jnp.float32(shifts[1])
        for number in range(2, NS_STEPS):
            shift = jnp.where(k == number, shifts[number], shift)
        linear = coef_second + 2.0 * coef_third * shift
        diff = gram_ref[...] - shift * eye
        low_diff = diff.astype(bf16)
        poly_ref[...] = (linear * diff + coef_third * mm(low_diff, low_diff)).astype(bf16)
        return coef_first + coef_second * shift + coef_third * shift * shift

    def sweep(k, carry):
        base = polynomial(k)

        def update(cols):
            fresh = base * full_ref[:, cols] + mm(poly_ref[...], low_ref[:, cols])
            full_ref[:, cols] = fresh
            low_ref[:, cols] = fresh.astype(bf16)

        each_chunk(update)
        gram()
        return carry

    lax.fori_loop(1, NS_STEPS - 1, sweep, 0)
    base = polynomial(NS_STEPS - 1)
    wanted = -(-4 * own_ff // tile) * tile
    fresh = base * full_ref[:, :wanted] + mm(poly_ref[...], low_ref[:, :wanted])
    gram_ref[:wanted, :] = fresh.T
    for kind, _, size in kinds:

        @pl.when(kind)
        def _():
            for k in range(4):
                piece = gram_ref[k * size : (k + 1) * size, :].astype(bf16)
                if size < own_ff:
                    piece = jnp.concatenate(
                        [piece, jnp.zeros((own_ff - size, side), bf16)], axis=0
                    )
                out_ref[k * own_ff : (k + 1) * own_ff, :] = piece


def orthogonal(role, columns, sums, own):
    width = sums.shape[1]
    parts = [part.reshape(-1, width) for column in columns for part in column]
    length = sum(part.shape[0] for part in parts)
    return pl.pallas_call(
        functools.partial(ns_kernel, own, len(parts)),
        out_shape=jax.ShapeDtypeStruct((4 * own[1], width), bf16),
        in_specs=[pl.BlockSpec(memory_space=pltpu.SMEM)]
        + [pl.BlockSpec(memory_space=pl.ANY)] * (len(parts) + 1),
        out_specs=pl.BlockSpec(memory_space=pltpu.VMEM),
        scratch_shapes=[
            pltpu.VMEM((length, width), bf16),
            pltpu.VMEM((width, length), f32),
            pltpu.VMEM((width, length), bf16),
            pltpu.VMEM((width, width), f32),
            pltpu.VMEM((width, width), bf16),
            pltpu.SemaphoreType.DMA((len(parts),)),
        ],
        compiler_params=pltpu.CompilerParams(vmem_limit_bytes=vmem_limit),
        cost_estimate=cost(46),
        name="newton_schulz",
    )(role, *parts, sums)


def column_place(mask):
    return ((mask >> 1) & 1) + 2 * (mask & 1)


def sum_heads_kernel(own_mix, old_at, role_ref, near_ref, *refs):
    parts, (acts_ref, y_out_ref, fresh_ref) = refs[:8], refs[8:11]
    held_ref, old_ref, y_ref, natural_ref, turned_ref, sems = refs[11:]
    width = held_ref.shape[3]
    own_in = fresh_ref.shape[1]
    hd = width // HEADS
    block = 16
    place = [column_place(near_ref[0] ^ n) for n in range(4)]

    def fetch(size, at, own):
        moves = [(acts_ref.at[:, at : at + own], old_ref.at[:, :own])]
        for c in range(4):
            moves.append((parts[2 * c].at[:size], held_ref.at[c, 0, :size]))
            moves.append((parts[2 * c + 1].at[:, :size], held_ref.at[c, 1:, :size]))
        copy_all(moves, sems)

    @pl.when(role_ref[0] == 0)
    def _():
        fetch(3 * hd, old_at, own_in)
        for z in range(4):
            for n in range(4):
                for start in range(0, own_in, block):
                    first = (4 * z + n) * own_in + start
                    part, rest = divmod(first, width)
                    h, off = divmod(rest, hd)
                    at = part * hd + off
                    source = held_ref[place[h & 3], h >> 2, at : at + block, :]
                    natural_ref[place[n], z, start : start + block, :] = source
                    old = old_ref[4 * z + n, start : start + block, :]
                    y_ref[pl.ds((place[n] * 4 + z) * own_in + start, block), :] = (
                        muon_moment * old.astype(f32) + source.astype(f32)
                    ).astype(bf16)
        fresh_ref[...] = natural_ref[0]
        copy_all([(y_ref, y_out_ref)], sems)

    @pl.when(role_ref[0] == 3)
    def _():
        fetch(hd, old_at + own_in, own_mix)
        for h in range(HEADS):
            turned_ref[h * hd : (h + 1) * hd, :] = held_ref[
                place[h & 3], 3 ^ (h >> 2), :hd
            ].astype(f32)
        turned_ref[...] = turned_ref[...].T
        fresh_ref[...] = jnp.zeros_like(fresh_ref)
        for z in range(4):
            for n in range(4):
                first = (4 * z + n) * own_mix
                source = turned_ref[first : first + own_mix, :]
                natural_ref[place[n], 3 ^ z, :own_mix] = source.astype(bf16)
                old = old_ref[4 * z + n, :own_mix]
                y_ref[pl.ds((place[n] * 4 + (3 ^ z)) * own_mix, own_mix), :] = (
                    muon_moment * old.astype(f32) + source
                ).astype(bf16)
        fresh_ref[:, :own_mix] = natural_ref[0, :, :own_mix]
        copy_all([(y_ref.at[:width], y_out_ref.at[:width])], sems)

    @pl.when((role_ref[0] == 1) | (role_ref[0] == 2))
    def _():
        fresh_ref[...] = jnp.zeros_like(fresh_ref)


def sum_heads(role, near, columns, acts, old_at, own_in, own_mix):
    ctx, _, width = acts.shape
    parts = [part for column in columns for part in column]
    size = parts[0].shape[0]
    smem = pl.BlockSpec(memory_space=pltpu.SMEM)
    hbm = pl.BlockSpec(memory_space=pl.ANY)
    return pl.pallas_call(
        functools.partial(sum_heads_kernel, own_mix, old_at),
        out_shape=[
            jax.ShapeDtypeStruct((ctx * own_in, width), bf16),
            jax.ShapeDtypeStruct((4, own_in, width), bf16),
        ],
        in_specs=[smem, smem] + [hbm] * 9,
        out_specs=[hbm, pl.BlockSpec(memory_space=pltpu.VMEM)],
        scratch_shapes=[
            pltpu.VMEM((4, 4, size, width), bf16),
            pltpu.VMEM((ctx, own_in, width), bf16),
            pltpu.VMEM((ctx * own_in, width), bf16),
            pltpu.VMEM((4, 4, own_in, width), bf16),
            pltpu.VMEM((width, width), f32),
            pltpu.SemaphoreType.DMA((9,)),
        ],
        compiler_params=pltpu.CompilerParams(vmem_limit_bytes=vmem_limit),
        cost_estimate=cost(4),
        name="sum_heads",
    )(role, near, *parts, acts)


def exchange(packed):
    return lax.all_to_all(packed, "ctx", split_axis=0, concat_axis=0, tiled=True)


def gather(array):
    return lax.all_gather(array, "ctx", axis=0, tiled=False)


def flip(array, mask, ctx):
    return lax.ppermute(array, "ctx", [(j, j ^ mask) for j in range(ctx)])


def spread_z(array, z_here, ctx):
    held = [array] + [flip(array, 4 * k, ctx) for k in (1, 2, 3)]
    odd, high = (z_here & 1) == 1, z_here >= 2
    first = [jnp.where(odd, held[k ^ 1], held[k]) for k in range(4)]
    return jnp.stack([jnp.where(high, first[k ^ 2], first[k]) for k in range(4)])


def both_sides(held, other, mask, ctx_index):
    upper = (ctx_index & mask) != 0
    return jnp.stack([jnp.where(upper, other, held), jnp.where(upper, held, other)])


def gather_start(piece_for, z_here, ctx):
    own = piece_for(z_here)
    far = [flip(piece_for(z_here ^ k), 4 * k, ctx) for k in (1, 2, 3)]
    return own, far, [flip(own, mask, ctx) for mask in (2, 1)]


def gather_finish(started, ctx):
    own, far, own_sides = started
    far = jnp.stack(far)
    far_sides = [flip(far, mask, ctx) for mask in (2, 1)]
    across = tuple(flip(part, 1, ctx) for part in (own_sides[0], far_sides[0]))
    columns = [(own, far), (own_sides[0], far_sides[0]), (own_sides[1], far_sides[1]), across]
    for mask in [1 << n for n in range(4, ctx.bit_length() - 1)]:
        columns = columns + [tuple(flip(part, mask, ctx) for part in column) for column in columns]
    return columns


def column_at(mask):
    high = mask >> 4
    return ((mask >> 1) & 1) + 2 * (mask & 1) + 4 * high


def body(
    ctx,
    tokens,
    cotangent,
    block_order,
    input_weight,
    output_weight,
    expand_weight,
    reduce_weight,
    vectors,
    input_moment,
    output_moment,
    expand_moment,
    reduce_moment,
    vector_first,
    vector_second,
):
    seqs, local, width = tokens.shape
    rows = seqs * local
    length = ctx * local
    hd = width // HEADS
    layers = 2
    own_in = input_weight.shape[2]
    own_mix = output_weight.shape[2]
    own_ff = expand_weight.shape[2]
    own_vec = vectors.shape[1]
    dp_index = lax.axis_index("dp")
    ctx_index = lax.axis_index("ctx")
    owner_first = dp_index == 0

    ring_rows = 688

    def sections(parts):
        at, pieces, used = {}, [], 0
        for name, array in parts:
            size = array.shape[0]
            aligned = size % 16 == 0 and not name.startswith("old")
            start = -(-used // size) * size if aligned else used
            pieces.append(jnp.pad(array, ((start - used, 0), (0, 0))))
            at[name], used = start, start + size
        goal = -(-used // 16) * 16
        if ctx == 16 and goal > 512:
            goal = max(goal, ring_rows)
        pieces.append(jnp.zeros((goal - used, width), bf16))
        return jnp.concatenate(pieces, axis=0), at

    x_own = tokens.reshape(rows, width)
    cot = cotangent.reshape(rows, width)
    vec_row = jnp.pad(vectors.astype(bf16), ((0, 15), (0, width - own_vec)))
    pack = jnp.concatenate(
        [
            expand_weight[0].T.astype(bf16),
            reduce_weight[0].astype(bf16),
            output_weight[0].T.astype(bf16),
            input_weight[0].T.astype(bf16),
            vec_row,
        ],
        axis=0,
    )
    pack_other = lax.ppermute(pack, "dp", [(0, 1), (1, 0)])
    cuts = (own_ff, 2 * own_ff, 2 * own_ff + own_mix, 2 * own_ff + own_mix + own_in)
    own_parts = []
    for l in range(layers):
        mine = jnp.where(owner_first, (pack, pack_other)[l], (pack_other, pack)[l])
        own_parts.append(jnp.split(mine, cuts))
    pack_first, at_first = sections(
        [
            ("fc", own_parts[0][0]),
            ("red", own_parts[0][1]),
            ("tokens", x_own),
            ("vec", jnp.concatenate([own_parts[l][4][:8] for l in range(layers)], axis=0)),
            ("mix", own_parts[0][2]),
            ("in", own_parts[0][3]),
            ("next", own_parts[1][3]),
        ]
    )
    pack_second, at_second = sections(
        [
            ("fc", own_parts[1][0]),
            ("red", own_parts[1][1]),
            ("cot", cot),
            ("mix", own_parts[1][2]),
        ]
    )
    all_first, all_second = gather(pack_first), gather(pack_second)
    weights = (all_first, all_second)
    places = (at_first, at_second)
    in_at = (at_first["in"], at_first["next"])
    vecs = [
        all_first[:, at_first["vec"] + 8 * l, :own_vec].reshape(-1, width).astype(f32)
        for l in range(layers)
    ]

    block_len = length // block_order.shape[0]
    positions = (
        block_order[:, None] * block_len + jnp.arange(block_len, dtype=jnp.int32)[None, :]
    ).reshape(length)
    qpos = positions[:, None]
    kpos = positions[None, :]

    head = jnp.minimum(ctx_index, HEADS - 1)
    head_bias = jnp.concatenate(
        [
            lax.dynamic_slice_in_dim(vecs[0][2], head * hd, hd),
            jnp.zeros((hd,), f32),
            lax.dynamic_slice_in_dim(vecs[0][3], head * hd, hd),
        ]
    )
    stream = x_own
    saved = []
    for l in range(layers):
        if l == 0:
            a, qkv = head_qkv(
                head[None], all_first, at_first["tokens"], vecs[0], head_bias[None],
                all_first, at_first["in"], own_in, rows,
            )
        else:
            a, qkv_pack = qkv_forward(stream, vecs[l], all_first, in_at[l], own_in, local)
            qkv = exchange(qkv_pack).reshape(length, 6 * hd)
        out_full, out_low, prob = attn_forward(qkv, qpos, kpos)
        o_pack = exchange(out_low.reshape(ctx, local, 2 * hd))
        mid, c, hidden, fresh = mlp_forward(
            o_pack, stream, vecs[l], weights[l], places[l], own_ff, own_mix
        )
        saved.append((stream, a, qkv, out_full, out_low, prob, mid, c, hidden))
        stream = fresh
    block_output = stream.reshape(seqs, local, width)

    bias = [
        lax.dynamic_slice_in_dim(vecs[l][PIECES:].reshape(-1), ctx_index * own_ff, own_ff)[:, None]
        for l in range(layers)
    ]

    role = (ctx_index // 4) % 4

    grad = cot
    kept = [None, None]
    vec_grads = [None, None]
    for l in (1, 0):
        x, a, qkv, out_full, out_low, prob, mid, c, hidden = saved[l]
        gz, gmid, gy, go_pack, vg_late = mlp_backward(
            grad, mid, hidden, vecs[l], weights[l], places[l], own_ff, own_mix
        )
        if l == 1:
            pack_acts, at_acts = sections(
                [
                    ("c", saved[0][7]),
                    ("next_a", saved[1][1]),
                    ("next_c", saved[1][7]),
                    ("next_gy", gy),
                    ("old_in", input_moment[0].T.astype(bf16)),
                    ("old_mix", output_moment[0].T.astype(bf16)),
                ]
            )
            acts = gather(pack_acts)
        if l == 0:
            gz_held = spread_z(gz, role, ctx)
        go = exchange(go_pack).reshape(length, 2 * hd)
        dqkv = attn_backward(qkv, go, out_full, prob)
        if l == 0:
            dqkv, gz_held = lax.optimization_barrier((dqkv, gz_held))
            gz_other = flip(gz_held, 2, ctx)
        dqkv_own = exchange(dqkv.reshape(ctx, local, 6 * hd))
        if l == 0:
            g_head = [
                head_grads(dqkv, saved[0][1], 0, rows),
                head_grads(kept[1][2], acts, at_acts["next_a"], rows),
                head_grads(saved[1][4], acts, at_acts["next_gy"], rows),
            ]
            g_hidden_second = hidden_grads(
                acts, at_acts["next_c"], all_second, at_second["cot"],
                *own_parts[1][:2], bias[1], rows,
            )
            ready = hidden_ready(acts, at_acts["c"], own_parts[0][0], bias[0], rows)
            dqkv_own, g_head, ready, g_hidden_second, gz_other = lax.optimization_barrier(
                (dqkv_own, g_head, ready, g_hidden_second, gz_other)
            )
            gz_held = both_sides(gz_held, gz_other, 2, ctx_index)
            for mask in [1] + [1 << n for n in range(4, ctx.bit_length() - 1)]:
                gz_held = both_sides(gz_held, flip(gz_held, mask, ctx), mask, ctx_index)
            gz_all = gz_held.reshape(ctx // 4, 4 * rows, width)
        gin, vg_early = qkv_backward(dqkv_own, x, gmid, vecs[l], all_first, in_at[l], own_in)
        vec_grads[l] = jnp.concatenate([vg_early[:4], vg_late], axis=0)
        kept[l] = (gz, gy, dqkv)
        grad = gin
    input_grad = grad.reshape(seqs, local, width)

    gy_all = gather(kept[0][1])

    def owned(first, second):
        given = jnp.where(owner_first, second, first).astype(bf16)
        taken = lax.ppermute(given, "dp", [(0, 1), (1, 0)]).astype(f32)
        return jnp.where(owner_first, first, second) + taken

    g_in_head = owned(g_head[0], g_head[1]).astype(bf16)
    hidden_second = jnp.concatenate(g_hidden_second, axis=0)
    old_hidden = jnp.concatenate([expand_moment[0].T, reduce_moment[0]], axis=0)
    vec_terms = jnp.stack(vec_grads).reshape(layers, ctx, own_vec).swapaxes(0, 1)
    gz_all, input_grad, hidden_second, old_hidden, g_in_head, vec_terms, ready, g_head = (
        lax.optimization_barrier(
            (gz_all, input_grad, hidden_second, old_hidden, g_in_head, vec_terms, ready, g_head)
        )
    )
    hidden_first = jnp.concatenate(
        hidden_last(acts, at_acts["c"], gz_all, *ready, own_parts[0][1], rows), axis=0
    )
    vec_terms, hidden_first = lax.optimization_barrier((vec_terms, hidden_first))
    vec_sums = jnp.sum(exchange(vec_terms), axis=0)
    moved = muon_moment * old_hidden + owned(hidden_first, hidden_second)
    m_fc = moved[:own_ff].T
    m_red = moved[own_ff:]

    big = max(own_ff, 3 * hd)

    def padded(piece):
        return jnp.pad(piece.astype(bf16), ((0, big - piece.shape[0]), (0, 0)))

    g_mix_first = head_grads(saved[0][4], gy_all, 0, rows)
    g_mix_head = owned(g_mix_first, g_head[2])
    pieces = (g_in_head, padded(moved[:own_ff]), padded(m_red), padded(g_mix_head))

    def piece_for(z):
        low = jnp.where(z == 0, pieces[0], pieces[1])
        return jnp.where(z < 2, low, jnp.where(z == 2, pieces[2], pieces[3]))

    started, vec_sums = lax.optimization_barrier((gather_start(piece_for, role, ctx), vec_sums))
    columns = gather_finish(started, ctx)

    groups = ctx // 4
    near = ctx_index % 4
    masks = [m for m in range(ctx) if m & 12 == 0]
    order = sorted(masks, key=column_at)

    def absolute(array, size):
        mine = (ctx_index // 16) * 4 + near
        spots = jnp.array([column_at(((n >> 2) << 4) | (n & 3)) for n in range(groups)])
        listed = jnp.stack(
            [
                lax.dynamic_index_in_dim(array, spots[n ^ mine], 0, keepdims=False)[:, :size]
                for n in range(groups)
            ]
        )
        listed = listed.reshape(ctx // 16, 4, 4, size, width).swapaxes(1, 2)
        return listed.reshape(ctx, size, width)

    def relative(array):
        size = array.shape[1]
        split = array.reshape(ctx // 16, 4, 4, size, width).swapaxes(1, 2)
        split = split.reshape(groups, 4, size, width)
        mine = (ctx_index // 16) * 4 + near
        spread = jnp.stack(
            [
                lax.dynamic_index_in_dim(
                    split, mine ^ (((m >> 4) << 2) | (m & 3)), 0, keepdims=False
                )
                for m in order
            ]
        )
        return spread

    old_at = at_acts["old_in"]
    if ctx == 16 and own_in % 16 == 0 and own_mix % 16 == 0:
        sums, fresh = sum_heads(role[None], near[None], columns, acts, old_at, own_in, own_mix)
    else:
        old = acts[:, old_at : old_at + own_in + own_mix].astype(f32)

        def joined(parts):
            return jnp.stack([jnp.concatenate([own[None], far]) for own, far in parts])

        new_in = absolute(joined(columns), 3 * hd)[:HEADS].reshape(HEADS, 3, hd, width)
        new_in = new_in.swapaxes(0, 1).reshape(ctx, own_in, width)
        sum_in = relative((muon_moment * old[:, :own_in] + new_in.astype(f32)).astype(bf16))
        new_mix = absolute(joined(columns)[:, ::-1], hd)[:HEADS].reshape(width, width)
        new_mix = new_mix.T.reshape(ctx, own_mix, width)
        sum_mix = relative((muon_moment * old[:, own_in:] + new_mix.astype(f32)).astype(bf16))
        sum_mix = jnp.pad(sum_mix[:, ::-1].reshape(width, width), ((0, 2 * width), (0, 0)))
        sums = jnp.where(role == 3, sum_mix, sum_in.reshape(3 * width, width))
        new_mix = jnp.pad(relative(new_mix)[0, ::-1], ((0, 0), (0, own_in - own_mix), (0, 0)))
        fresh = jnp.where(role == 3, new_mix, relative(new_in)[0])

    taken = [fresh[0]]
    for k in (1, 2, 3):
        pairs = [(j, j ^ (4 * k)) for j in range(ctx) if (j // 4) % 4 in (0, 3)]
        taken.append(lax.ppermute(fresh[k], "ctx", pairs))
    direction = orthogonal(
        role[None],
        [(own[:own_ff], far[:, :own_ff]) for own, far in columns],
        sums,
        (own_in, own_ff, own_mix),
    )
    direction, taken, vec_sums = lax.optimization_barrier((direction, taken, vec_sums))
    vec_given = jnp.where(owner_first, vec_sums[1], vec_sums[0])
    vec_kept = jnp.where(owner_first, vec_sums[0], vec_sums[1])
    vec_grad = (vec_kept + lax.ppermute(vec_given, "dp", [(0, 1), (1, 0)]))[None]
    direction = direction.reshape(4, own_ff, width)
    by_distance = [direction[0]] + [flip(direction[k], 4 * k, ctx) for k in (1, 2, 3)]

    def from_role(by_distance, wanted):
        result = by_distance[wanted]
        for k in range(4):
            if k != wanted:
                result = jnp.where(role == wanted ^ k, by_distance[k], result)
        return result

    m_in = muon_moment * input_moment[0] + from_role(taken, 0).astype(f32).T
    m_mix = muon_moment * output_moment[0] + from_role(taken, 3)[:own_mix].astype(f32).T

    got = [from_role(by_distance, wanted) for wanted in range(4)]
    steps = (
        got[0][:own_in].astype(f32).T,
        got[3][:own_mix].astype(f32).T,
        got[1].astype(f32).T,
        got[2].astype(f32),
    )
    hidden_units = ctx * own_ff
    largest = (3 * width, width, hidden_units, hidden_units)
    old_weights = (input_weight, output_weight, expand_weight, reduce_weight)
    new_weights = [
        old_weights[kind] * (1.0 - muon_rate * muon_decay)
        - muon_rate * 0.2 * math.sqrt(largest[kind]) * steps[kind][None]
        for kind in range(4)
    ]

    new_vector_first = beta_first * vector_first + (1.0 - beta_first) * vec_grad
    new_vector_second = beta_second * vector_second + (1.0 - beta_second) * vec_grad * vec_grad
    corr_first = 1.0 - beta_first**STEP
    corr_second = 1.0 - beta_second**STEP
    new_vectors = vectors - adam_rate * (new_vector_first / corr_first) / (
        jnp.sqrt(new_vector_second / corr_second) + adam_epsilon
    )
    return (
        block_output,
        input_grad,
        new_weights[0],
        new_weights[1],
        new_weights[2],
        new_weights[3],
        m_in[None],
        m_mix[None],
        m_fc[None],
        m_red[None],
        new_vectors,
        new_vector_first,
        new_vector_second,
    )


def solution(mesh):
    return jax.shard_map(
        functools.partial(body, mesh.shape["ctx"]),
        mesh=mesh,
        in_specs=(
            P("dp", "ctx", None),
            P("dp", "ctx", None),
            P(),
            P("dp", None, "ctx"),
            P("dp", None, "ctx"),
            P("dp", None, "ctx"),
            P("dp", "ctx", None),
            P("dp", "ctx"),
            P("dp", None, "ctx"),
            P("dp", None, "ctx"),
            P("dp", None, "ctx"),
            P("dp", "ctx", None),
            P("dp", "ctx"),
            P("dp", "ctx"),
        ),
        out_specs=(
            P("dp", "ctx", None),
            P("dp", "ctx", None),
            P("dp", None, "ctx"),
            P("dp", None, "ctx"),
            P("dp", None, "ctx"),
            P("dp", "ctx", None),
            P("dp", None, "ctx"),
            P("dp", None, "ctx"),
            P("dp", None, "ctx"),
            P("dp", "ctx", None),
            P("dp", "ctx"),
            P("dp", "ctx"),
            P("dp", "ctx"),
        ),
        check_vma=False,
    )
```

time: 4780 us -> 666 us (0.14)
  waiting for transfers between devices: 1660 us -> 273 us
  blocking collectives: 1210 us -> 86.9 us
  local copies, waits for them, and re-layouts: 707 us -> 19.3 us
  matrix products: 621 us -> 0 us
  other arithmetic: 359 us -> 28.9 us
  Pallas kernels: 0 us -> 168 us
  starting transfers between devices: 157 us -> 64.7 us
    all_to_all x5 -> x3, blocking collectives: 1050 us -> 86.9 us  [exchange(): lax.all_to_all(packed, 'ctx', split_axis=0, concat_axis=0, tiled=True)]
    all_to_all x5, waiting for transfers between devices: 803 us -> 53.2 us  [exchange(): lax.all_to_all(packed, 'ctx', split_axis=0, concat_axis=0, tiled=True)]
    all_gather x21 -> x4, waiting for transfers between devices: 778 us -> 132 us  [gather(): return lax.all_gather(array, 'ctx', axis=0, tiled=False)]
    dot_general x293 -> x0, matrix products: 621 us -> none  [the longest x5 144 us: body(): jnp.einsum('kij,kjl->kil', grams, grams, precision=highest)]
    dynamic_slice x321 -> x3, local copies, waits for them, and re-layouts: 236 us -> 0.24 us  [the longest x2 0.16 us: body(): lax.dynamic_slice_in_dim(vecs[l][PIECES:].reshape(-1), ctx_index * own_ff...]
    broadcast_in_dim x9 -> x5, local copies, waits for them, and re-layouts: 183 us -> 2.65 us  [the longest x2 1.54 us: body(): lax.dynamic_slice_in_dim(vecs[l][PIECES:].reshape(-1), ctx_index * own_ff...]
    add x168 -> x2, other arithmetic: 175 us -> 1.82 us  [the longest x1 1.75 us: body(): moved = muon_moment * old_hidden + owned(hidden_first, hidden_second)]
    pallas_call x0 -> x21, Pallas kernels: none -> 168 us  [the longest x1 37.1 us: orthogonal(): pl.pallas_call(functools.partial(ns_kernel, own, len(parts)), out_shape=j...]
  transfers between devices with their start and end apart: 30 -> 34, of which waited for: 18 -> 17; matrix products, arithmetic and copies ran while one was open for 27% -> 4% of each run, Pallas kernels for 0% -> 22%
where the time goes in v1:
time: 666 us; the launch traced here: 656 us
  waiting for transfers between devices  273 us (41%)
  Pallas kernels  168 us (25%)
  blocking collectives  86.9 us (13%)
  starting transfers between devices  64.7 us (10%)
  other arithmetic  28.9 us (4%)
  local copies, waits for them, and re-layouts  19.3 us (3%)
  between operations  15.1 us (2%)
    all_gather x4, waiting for transfers between devices, gather(): return lax.all_gather(array, 'ctx', axis=0, tiled=False)  132 us
    all_to_all x3, blocking collectives, exchange(): lax.all_to_all(packed, 'ctx', split_axis=0, concat_axis=0, tiled=True)  86.9 us
    ppermute x17, waiting for transfers between devices, flip(): return lax.ppermute(array, 'ctx', [(j, j ^ mask) for j in range(ctx)])  64.3 us
    all_to_all x5, waiting for transfers between devices, exchange(): lax.all_to_all(packed, 'ctx', split_axis=0, concat_axis=0, tiled=True)  53.2 us
    pallas_call x1, Pallas kernels, orthogonal(): pl.pallas_call(functools.partial(ns_kernel, own, len(parts)), out_shape=j...  37.1 us
    ppermute x17, starting transfers between devices, flip(): return lax.ppermute(array, 'ctx', [(j, j ^ mask) for j in range(ctx)])  30 us
    all_to_all x5, starting transfers between devices, exchange(): lax.all_to_all(packed, 'ctx', split_axis=0, concat_axis=0, tiled=True)  21.5 us
    ppermute x1, waiting for transfers between devices, body(): pack_other = lax.ppermute(pack, 'dp', [(0, 1), (1, 0)])  20.2 us
  transfers between devices with their start and end apart: 34, of which 17 were waited for; matrix products, arithmetic and copies ran while one was open for 4% of the time, Pallas kernels for 22%

profile of v1, /device:TPU:0, one launch (start us, length us, event | category | flops | bytes accessed | tf_op | source)
XLA Modules:
  0.0 655.6 jit_solution(14021350877171646167)
XLA Ops:
  13.3 20.2 %collective-permute-done = bf16[592,768]{1,0:T(8,128)(2,1)S(1)} collective-permute-done((bf16[592,768]{1,0:T(8,128)(2,1)S(1)}, bf16[592,768]{1,0:T(8,128)(2,1)S(1)}, u32[]{:S(2)}, u32[]{:S(2)}) %collective-permute-start) | collective-permute-done | bytes 909344 | tf_op jit(solution)/shard_map/ppermute | solution.py:1053
  39.3 108.1 %all-gather.9.cloned.1.call-done = bf16[13824,768]{1,0:T(8,128)(2,1)} async-done(((bf16[864,768]{1,0:T(8,128)(2,1)}), bf16[13824,768]{1,0:T(8,128)(2,1)}) %all-gather.9.cloned.1.call-update) | async-done | bytes 21233680 | tf_op jit(solution)/shard_map/all_gather | solution.py:953
  156.6 7.9 %attn_forward.2 = (f32[1024,128]{1,0:T(8,128)}, bf16[1024,128]{1,0:T(8,128)(2,1)}, bf16[2,1024,1024]{2,1,0:T(8,128)(2,1)}) custom-call(s32[1024,1]{1,0:T(8,128)} %add.108.qpos_ref, s32[1,1024]{1,0:T(1,128)} %add.92.kpos_ref, bf16[1024,384]{1,0:T(8,128)(2,1)} %get-tuple-element.87.q_ref.k_ref.v_ref, bf16[1024,384]{1,0:T(8,128)(2,1)} %get-tuple-element.87.q_ref.k_ref.v_ref, ...), custom_call_target="tpu_custom_call" | custom-call | flops 8000000000 | bytes 8000000 | tf_op jit(solution)/shard_map/attn_forward/pallas_call | solution.py:246
  170.0 13.9 %all-to-all-done.o_ref = bf16[16,64,128]{2,1,0:T(8,128)(2,1)S(1)} async-done(((bf16[16,64,128]{2,1,0:T(8,128)(2,1)}), bf16[16,64,128]{2,1,0:T(8,128)(2,1)S(1)}, u32[]{:S(2)}, u32[]{:S(2)}) %all-to-all-start) | async-done | bytes 262176 | tf_op jit(solution)/shard_map/all_to_all | solution.py:949
  184.5 8.2 %mlp_forward.2 = (f32[128,768]{1,0:T(8,128)}, bf16[128,768]{1,0:T(8,128)(2,1)}, f32[128,3072]{1,0:T(8,128)}, f32[128,768]{1,0:T(8,128)}) custom-call(bf16[16,64,128]{2,1,0:T(8,128)(2,1)} %copy-done.21, bf16[128,768]{1,0:T(8,128)(2,1)} %bitcast.150, f32[12,768]{1,0:T(8,128)} %copy-done.18, bf16[16,864,768]{2,1,0:T(8,128)(2,1)} %bitcast.125, ...), custom_call_target="tpu_custom_call" | custom-call | flops 8000000000 | bytes 8000000 | tf_op jit(solution)/shard_map/mlp_forward/pallas_call | solution.py:355
  198.3 35.7 %all_to_all.40 = bf16[16,64,384]{2,1,0:T(8,128)(2,1)} all-to-all(bf16[16,64,384]{2,1,0:T(8,128)(2,1)} %get-tuple-element.90), channel_id=1, replica_groups=mesh['ctx'=16,'dp'=2] {'ctx'}, dimensions={0} | all-to-all | bytes 1572864 | tf_op jit(solution)/shard_map/all_to_all | solution.py:949
  234.0 7.9 %attn_forward.3 = (f32[1024,128]{1,0:T(8,128)}, bf16[1024,128]{1,0:T(8,128)(2,1)}, bf16[2,1024,1024]{2,1,0:T(8,128)(2,1)}) custom-call(s32[1024,1]{1,0:T(8,128)} %add.108.qpos_ref, s32[1,1024]{1,0:T(1,128)} %add.92.kpos_ref, bf16[1024,384]{1,0:T(8,128)(2,1)} %bitcast.157, bf16[1024,384]{1,0:T(8,128)(2,1)} %bitcast.158, bf16[1024,384]{1,0:T(8,128)(2,1)} %bitcast.159), custom_call_target="tpu_custom_call" | custom-call | flops 8000000000 | bytes 8000000 | tf_op jit(solution)/shard_map/attn_forward/pallas_call | solution.py:246
  245.6 14.2 %all-gather.11.cloned.1.call-done = bf16[11008,768]{1,0:T(8,128)(2,1)} async-done(((bf16[688,768]{1,0:T(8,128)(2,1)}), bf16[11008,768]{1,0:T(8,128)(2,1)}) %all-gather.11.cloned.1.call-update) | async-done | bytes 16908304 | tf_op jit(solution)/shard_map/all_gather | solution.py:953
  260.7 8.1 %mlp_forward.3 = (f32[128,768]{1,0:T(8,128)}, bf16[128,768]{1,0:T(8,128)(2,1)}, f32[128,3072]{1,0:T(8,128)}, f32[128,768]{1,0:T(8,128)}) custom-call(bf16[16,64,128]{2,1,0:T(8,128)(2,1)} %copy-done.20, f32[128,768]{1,0:T(8,128)} %get-tuple-element.89.x_ref, f32[12,768]{1,0:T(8,128)} %reshape.191.vec_ref, bf16[16,688,768]{2,1,0:T(8,128)(2,1)} %bitcast.134, ...), custom_call_target="tpu_custom_call" | custom-call | flops 8000000000 | bytes 8000000 | tf_op jit(solution)/shard_map/mlp_forward/pallas_call | solution.py:355
  268.9 8.6 %mlp_backward.2 = (bf16[128,768]{1,0:T(8,128)(2,1)}, f32[128,768]{1,0:T(8,128)}, bf16[128,768]{1,0:T(8,128)(2,1)}, bf16[16,64,128]{2,1,0:T(8,128)(2,1)}, f32[8,768]{1,0:T(8,128)}) custom-call(bf16[128,768]{1,0:T(8,128)(2,1)} %bitcast.155, f32[128,768]{1,0:T(8,128)} %get-tuple-element.93.mid_ref, f32[128,3072]{1,0:T(8,128)} %get-tuple-element.94.h_ref, ...), custom_call_target="tpu_custom_call" | custom-call | flops 8000000000 | bytes 8000000 | tf_op jit(solution)/shard_map/mlp_backward/pallas_call | solution.py:440
  279.6 25.1 %all_to_all.41 = bf16[16,64,128]{2,1,0:T(8,128)(2,1)} all-to-all(bf16[16,64,128]{2,1,0:T(8,128)(2,1)S(1)} %copy-done.34), channel_id=1, replica_groups=mesh['ctx'=16,'dp'=2] {'ctx'}, dimensions={0} | all-to-all | bytes 524288 | tf_op jit(solution)/shard_map/all_to_all | solution.py:949
  315.8 31.4 %all-to-all-done.4.d_ref = bf16[16,64,384]{2,1,0:T(8,128)(2,1)S(1)} async-done(((bf16[16,64,384]{2,1,0:T(8,128)(2,1)}), bf16[16,64,384]{2,1,0:T(8,128)(2,1)S(1)}, u32[]{:S(2)}, u32[]{:S(2)}) %all-to-all-start.4) | async-done | bytes 786464 | tf_op jit(solution)/shard_map/all_to_all | solution.py:949
  353.6 8.8 %mlp_backward.3 = (bf16[128,768]{1,0:T(8,128)(2,1)}, f32[128,768]{1,0:T(8,128)}, bf16[128,768]{1,0:T(8,128)(2,1)}, bf16[16,64,128]{2,1,0:T(8,128)(2,1)}, f32[8,768]{1,0:T(8,128)}) custom-call(f32[128,768]{1,0:T(8,128)} %get-tuple-element.99.gr_ref, f32[128,768]{1,0:T(8,128)} %get-tuple-element.100.mid_ref, f32[128,3072]{1,0:T(8,128)} %get-tuple-element.101.h_ref, ...), custom_call_target="tpu_custom_call" | custom-call | flops 8000000000 | bytes 8000000 | tf_op jit(solution)/shard_map/mlp_backward/pallas_call | solution.py:440
  376.4 13.2 %collective-permute-done.2 = bf16[128,768]{1,0:T(8,128)(2,1)S(1)} collective-permute-done((bf16[128,768]{1,0:T(8,128)(2,1)}, bf16[128,768]{1,0:T(8,128)(2,1)S(1)}, u32[]{:S(2)}, u32[]{:S(2)}) %collective-permute-start.2) | collective-permute-done | bytes 196640 | tf_op jit(solution)/shard_map/ppermute | solution.py:957
  389.9 7.8 %all-to-all-done.5 = bf16[16,64,128]{2,1,0:T(8,128)(2,1)S(1)} async-done(((bf16[16,64,128]{2,1,0:T(8,128)(2,1)}), bf16[16,64,128]{2,1,0:T(8,128)(2,1)S(1)}, u32[]{:S(2)}, u32[]{:S(2)}) %all-to-all-start.5) | async-done | bytes 262176 | tf_op jit(solution)/shard_map/all_to_all | solution.py:949
  398.4 7.4 %attn_backward.3.pack_ref = bf16[1024,384]{1,0:T(8,128)(2,1)} custom-call(bf16[1024,384]{1,0:T(8,128)(2,1)} %get-tuple-element.87.q_ref.k_ref.v_ref, bf16[1024,128]{1,0:T(8,128)(2,1)} %bitcast.170, f32[1024,128]{1,0:T(8,128)} %get-tuple-element.103.of_ref, bf16[2,1024,1024]{2,1,0:T(8,128)(2,1)} %get-tuple-element.104.p_ref, ...), custom_call_target="tpu_custom_call" | custom-call | flops 8000000000 | bytes 8000000 | tf_op jit(solution)/shard_map/attn_backward/pallas_call | solution.py:305
  431.4 7.5 %hidden_grads.1 = (f32[192,768]{1,0:T(8,128)}, f32[192,768]{1,0:T(8,128)}) custom-call(bf16[16,704,768]{2,1,0:T(8,128)(2,1)} %bitcast.144, bf16[16,688,768]{2,1,0:T(8,128)(2,1)} %bitcast.140, bf16[192,768]{1,0:T(8,128)(2,1)} %get-tuple-element.190.fc_ref, bf16[192,768]{1,0:T(8,128)(2,1)} %get-tuple-element.189.red_ref, f32[192,1]{1,0:T(8,128)} %copy.34.bias_ref), custom_call_target="tpu_custom_call" | custom-call | flops 6000000000 | bytes 6000000 | tf_op jit(solution)/shard_map/hidden_grads/pallas_call | solution.py:570
  471.5 9.4 %all-gather.15.cloned.1.call-done = bf16[2048,768]{1,0:T(8,128)(2,1)} async-done(((bf16[128,768]{1,0:T(8,128)(2,1)}), bf16[2048,768]{1,0:T(8,128)(2,1)}) %all-gather.15.cloned.1.call-update) | async-done | bytes 3145744 | tf_op jit(solution)/shard_map/all_gather | solution.py:953
  493.1 13.9 %collective-permute-start.9 = (bf16[192,768]{1,0:T(8,128)(2,1)S(1)}, bf16[192,768]{1,0:T(8,128)(2,1)S(1)}, u32[]{:S(2)}, u32[]{:S(2)}) collective-permute-start(bf16[192,768]{1,0:T(8,128)(2,1)S(1)} %get-tuple-element.184), channel_id=1, source_target_pairs={{0,8},{2,10},{4,12},{6,14},{8,0},{10,2},{12,4},{14,6},{16,24},{18,... | collective-permute-start | bytes 884744 | tf_op jit(solution)/shard_map/ppermute | solution.py:957
  510.7 26.1 %all_to_all.42 = f32[16,2,576]{2,1,0:T(2,128)S(1)} all-to-all(f32[16,2,576]{2,1,0:T(2,128)S(1)} %copy-done.31), channel_id=1, replica_groups=mesh['ctx'=16,'dp'=2] {'ctx'}, dimensions={0} | all-to-all | bytes 147456 | tf_op jit(solution)/shard_map/all_to_all | solution.py:949
  537.9 20.8 %collective-permute-done.14.refs_3_ = bf16[3,192,768]{2,1,0:T(8,128)(2,1)S(1)} collective-permute-done((bf16[3,192,768]{2,1,0:T(8,128)(2,1)S(1)}, bf16[3,192,768]{2,1,0:T(8,128)(2,1)S(1)}, u32[]{:S(2)}, u32[]{:S(2)}) %collective-permute-start.14) | collective-permute-done | bytes 884768 | tf_op jit(solution)/shard_map/ppermute | solution.py:957
  562.2 7.5 %sum_heads.1 = (bf16[2304,768]{1,0:T(8,128)(2,1)}, bf16[4,144,768]{2,1,0:T(8,128)(2,1)}) custom-call(s32[1]{0:T(128)} %bitcast.45.role_ref, s32[1]{0:T(128)} %bitcast.54.near_ref, bf16[192,768]{1,0:T(8,128)(2,1)} %copy-done.19, bf16[3,192,768]{2,1,0:T(8,128)(2,1)} %copy-done.1, bf16[192,768]{1,0:T(8,128)(2,1)} %collective-permute-done.12.refs_2_, ...), custom_call_target="tpu_custom_call" | custom-call | flops 4000000000 | bytes 4000000 | tf_op jit(solution)/shard_map/sum_heads/pallas_call | solution.py:926
  575.5 37.1 %newton_schulz.1 = bf16[768,768]{1,0:T(8,128)(2,1)} custom-call(s32[1]{0:T(128)} %bitcast.45.role_ref, bf16[192,768]{1,0:T(8,128)(2,1)} %copy-done.19, bf16[576,768]{1,0:T(8,128)(2,1)} %bitcast.148, bf16[192,768]{1,0:T(8,128)(2,1)} %collective-permute-done.12.refs_2_, bf16[576,768]{1,0:T(8,128)(2,1)} %bitcast.154, ...), custom_call_target="tpu_custom_call" | custom-call | flops 46000001024 | bytes 46000000 | tf_op jit(solution)/shard_map/newton_schulz/pallas_call | solution.py:835
  627.5 17.4 %collective-permute-done.22 = bf16[192,768]{1,0:T(8,128)(2,1)S(1)} collective-permute-done((bf16[192,768]{1,0:T(8,128)(2,1)S(1)}, bf16[192,768]{1,0:T(8,128)(2,1)S(1)}, u32[]{:S(2)}, u32[]{:S(2)}) %collective-permute-start.22) | collective-permute-done | bytes 294944 | tf_op jit(solution)/shard_map/ppermute | solution.py:957
  (248 shorter events, 174.1 us)
Async XLA Ops:
  7.2 140.2 %all-gather.9.cloned.1.call-start = ((), (), s32[]{:S(2)}) async-start(), calls=%async_computation.8 | async-start | bytes 22560768 | tf_op jit(solution)/shard_map/all_gather | solution.py:953
  10.3 23.2 %collective-permute-start = (bf16[592,768]{1,0:T(8,128)(2,1)S(1)}, bf16[592,768]{1,0:T(8,128)(2,1)S(1)}, u32[]{:S(2)}, u32[]{:S(2)}) collective-permute-start(bf16[592,768]{1,0:T(8,128)(2,1)S(1)} %constant_dynamic-update-slice_fusion), channel_id=1, source_target_pairs={{0,1},{1,0},{2,3},{3,2},{4,5},{5,4},{6,7},{7,6},{8,9},{9,8},{10,11... | collective-permute-start | bytes 2727944 | tf_op jit(solution)/shard_map/ppermute | solution.py:1053
  35.7 224.1 %all-gather.11.cloned.1.call-start = ((), (), s32[]{:S(2)}) async-start(), calls=%async_computation.9 | async-start | bytes 17965056 | tf_op jit(solution)/shard_map/all_gather | solution.py:953
  245.5 172.9 %all-gather.13.cloned.1.call-start = ((), (), s32[]{:S(2)}) async-start(), calls=%async_computation.10 | async-start | bytes 18382848 | tf_op jit(solution)/shard_map/all_gather | solution.py:953
  312.2 35.0 %all-to-all-start.4 = ((bf16[16,64,384]{2,1,0:T(8,128)(2,1)}), bf16[16,64,384]{2,1,0:T(8,128)(2,1)S(1)}, u32[]{:S(2)}, u32[]{:S(2)}) async-start(bf16[16,64,384]{2,1,0:T(8,128)(2,1)} %bitcast.149), calls=%async_computation.4 | async-start | bytes 1572864 | tf_op jit(solution)/shard_map/all_to_all | solution.py:949
  362.5 27.2 %collective-permute-start.2 = (bf16[128,768]{1,0:T(8,128)(2,1)}, bf16[128,768]{1,0:T(8,128)(2,1)S(1)}, u32[]{:S(2)}, u32[]{:S(2)}) collective-permute-start(bf16[128,768]{1,0:T(8,128)(2,1)} %get-tuple-element.105), channel_id=1, source_target_pairs={{0,16},{2,18},{4,20},{6,22},{8,24},{10,26},{12,28},{14,30},{16,0},... | collective-permute-start | bytes 589832 | tf_op jit(solution)/shard_map/ppermute | solution.py:957
  362.7 27.0 %collective-permute-start.3 = (bf16[128,768]{1,0:T(8,128)(2,1)}, bf16[128,768]{1,0:T(8,128)(2,1)S(1)}, u32[]{:S(2)}, u32[]{:S(2)}) collective-permute-start(bf16[128,768]{1,0:T(8,128)(2,1)} %get-tuple-element.105), channel_id=1, source_target_pairs={{0,8},{2,10},{4,12},{6,14},{8,0},{10,2},{12,4},{14,6},{16,24},{18,... | collective-permute-start | bytes 589832 | tf_op jit(solution)/shard_map/ppermute | solution.py:957
  366.9 30.8 %all-to-all-start.5 = ((bf16[16,64,128]{2,1,0:T(8,128)(2,1)}), bf16[16,64,128]{2,1,0:T(8,128)(2,1)S(1)}, u32[]{:S(2)}, u32[]{:S(2)}) async-start(bf16[16,64,128]{2,1,0:T(8,128)(2,1)} %get-tuple-element.102), calls=%async_computation.5 | async-start | bytes 524288 | tf_op jit(solution)/shard_map/all_to_all | solution.py:949
  370.4 110.5 %all-gather.15.cloned.1.call-start = ((), (), s32[]{:S(2)}) async-start(), calls=%async_computation.11 | async-start | bytes 3342336 | tf_op jit(solution)/shard_map/all_gather | solution.py:953
  405.8 34.5 %all-to-all-start.6 = ((bf16[16,64,384]{2,1,0:T(8,128)(2,1)}), bf16[16,64,384]{2,1,0:T(8,128)(2,1)S(1)}, u32[]{:S(2)}, u32[]{:S(2)}) async-start(bf16[16,64,384]{2,1,0:T(8,128)(2,1)} %bitcast.163), calls=%async_computation.6 | async-start | bytes 1572864 | tf_op jit(solution)/shard_map/all_to_all | solution.py:949
  411.8 28.4 %collective-permute-start.4 = (bf16[4,128,768]{2,1,0:T(8,128)(2,1)S(1)}, bf16[4,128,768]{2,1,0:T(8,128)(2,1)S(1)}, u32[]{:S(2)}, u32[]{:S(2)}) collective-permute-start(bf16[4,128,768]{2,1,0:T(8,128)(2,1)S(1)} %pad_maximum_fusion.6), channel_id=1, source_target_pairs={{0,4},{2,6},{4,0},{6,2},{8,12},{10,14},{12,8},{14,10},{16,20},{18,... | collective-permute-start | bytes 2359304 | tf_op jit(solution)/shard_map/ppermute | solution.py:957
  470.0 20.9 %collective-permute-start.7 = (bf16[384,768]{1,0:T(8,128)(2,1)S(1)}, bf16[384,768]{1,0:T(8,128)(2,1)}, u32[]{:S(2)}, u32[]{:S(2)}) collective-permute-start(bf16[384,768]{1,0:T(8,128)(2,1)S(1)} %select_convert_fusion), channel_id=1, source_target_pairs={{0,1},{1,0},{2,3},{3,2},{4,5},{5,4},{6,7},{7,6},{8,9},{9,8},{10,11... | collective-permute-start | bytes 1769480 | tf_op jit(solution)/shard_map/ppermute | solution.py:1185
  493.1 43.7 %collective-permute-start.9 = (bf16[192,768]{1,0:T(8,128)(2,1)S(1)}, bf16[192,768]{1,0:T(8,128)(2,1)S(1)}, u32[]{:S(2)}, u32[]{:S(2)}) collective-permute-start(bf16[192,768]{1,0:T(8,128)(2,1)S(1)} %get-tuple-element.184), channel_id=1, source_target_pairs={{0,8},{2,10},{4,12},{6,14},{8,0},{10,2},{12,4},{14,6},{16,24},{18,... | collective-permute-start | bytes 884744 | tf_op jit(solution)/shard_map/ppermute | solution.py:957
  507.0 29.8 %collective-permute-start.10 = (bf16[192,768]{1,0:T(8,128)(2,1)S(1)}, bf16[192,768]{1,0:T(8,128)(2,1)S(1)}, u32[]{:S(2)}, u32[]{:S(2)}) collective-permute-start(bf16[192,768]{1,0:T(8,128)(2,1)S(1)} %get-tuple-element.183), channel_id=1, source_target_pairs={{0,16},{2,18},{4,20},{6,22},{8,24},{10,26},{12,28},{14,30},{16,0},... | collective-permute-start | bytes 884744 | tf_op jit(solution)/shard_map/ppermute | solution.py:957
  507.2 29.6 %collective-permute-start.11 = (bf16[192,768]{1,0:T(8,128)(2,1)S(1)}, bf16[192,768]{1,0:T(8,128)(2,1)S(1)}, u32[]{:S(2)}, u32[]{:S(2)}) collective-permute-start(bf16[192,768]{1,0:T(8,128)(2,1)S(1)} %get-tuple-element.168), channel_id=1, source_target_pairs={{0,24},{2,26},{4,28},{6,30},{8,16},{10,18},{12,20},{14,22},{16,8},... | collective-permute-start | bytes 884744 | tf_op jit(solution)/shard_map/ppermute | solution.py:957
  509.5 27.4 %collective-permute-start.12 = (bf16[192,768]{1,0:T(8,128)(2,1)S(1)}, bf16[192,768]{1,0:T(8,128)(2,1)}, u32[]{:S(2)}, u32[]{:S(2)}) collective-permute-start(bf16[192,768]{1,0:T(8,128)(2,1)S(1)} %get-tuple-element.146.refs_0_), channel_id=1, source_target_pairs={{0,4},{2,6},{4,0},{6,2},{8,12},{10,14},{12,8},{14,10},{16,20},{18,... | collective-permute-start | bytes 884744 | tf_op jit(solution)/shard_map/ppermute | solution.py:957
  510.7 26.2 %collective-permute-start.13 = (bf16[192,768]{1,0:T(8,128)(2,1)S(1)}, bf16[192,768]{1,0:T(8,128)(2,1)}, u32[]{:S(2)}, u32[]{:S(2)}) collective-permute-start(bf16[192,768]{1,0:T(8,128)(2,1)S(1)} %get-tuple-element.146.refs_0_), channel_id=1, source_target_pairs={{0,2},{2,0},{4,6},{6,4},{8,10},{10,8},{12,14},{14,12},{16,18},{18,... | collective-permute-start | bytes 884744 | tf_op jit(solution)/shard_map/ppermute | solution.py:957
  537.0 21.7 %collective-permute-start.14 = (bf16[3,192,768]{2,1,0:T(8,128)(2,1)S(1)}, bf16[3,192,768]{2,1,0:T(8,128)(2,1)S(1)}, u32[]{:S(2)}, u32[]{:S(2)}) collective-permute-start(bf16[3,192,768]{2,1,0:T(8,128)(2,1)S(1)} %pad_maximum_fusion.5.refs_1_), channel_id=1, source_target_pairs={{0,4},{2,6},{4,0},{6,2},{8,12},{10,14},{12,8},{14,10},{16,20},{18,... | collective-permute-start | bytes 2654216 | tf_op jit(solution)/shard_map/ppermute | solution.py:957
  537.9 23.5 %collective-permute-start.15 = (bf16[3,192,768]{2,1,0:T(8,128)(2,1)S(1)}, bf16[3,192,768]{2,1,0:T(8,128)(2,1)}, u32[]{:S(2)}, u32[]{:S(2)}) collective-permute-start(bf16[3,192,768]{2,1,0:T(8,128)(2,1)S(1)} %pad_maximum_fusion.5.refs_1_), channel_id=1, source_target_pairs={{0,2},{2,0},{4,6},{6,4},{8,10},{10,8},{12,14},{14,12},{16,18},{18,... | collective-permute-start | bytes 2654216 | tf_op jit(solution)/shard_map/ppermute | solution.py:957
  571.0 41.6 %collective-permute-start.18 = (bf16[144,768]{1,0:T(8,128)(2,1)S(1)}, bf16[144,768]{1,0:T(8,128)(2,1)S(1)}, u32[]{:S(2)}, u32[]{:S(2)}) collective-permute-start(bf16[144,768]{1,0:T(8,128)(2,1)S(1)} %get-tuple-element.193), channel_id=1, source_target_pairs={{0,8},{2,10},{4,12},{6,14},{24,16},{26,18},{28,20},{30,22},{1,9},{... | collective-permute-start | bytes 663560 | tf_op jit(solution)/shard_map/ppermute | solution.py:1277
  572.3 40.3 %collective-permute-start.19 = (bf16[144,768]{1,0:T(8,128)(2,1)S(1)}, bf16[144,768]{1,0:T(8,128)(2,1)S(1)}, u32[]{:S(2)}, u32[]{:S(2)}) collective-permute-start(bf16[144,768]{1,0:T(8,128)(2,1)S(1)} %get-tuple-element.192), channel_id=1, source_target_pairs={{0,16},{2,18},{4,20},{6,22},{24,8},{26,10},{28,12},{30,14},{1,17},... | collective-permute-start | bytes 663560 | tf_op jit(solution)/shard_map/ppermute | solution.py:1277
  573.6 39.0 %collective-permute-start.20 = (bf16[144,768]{1,0:T(8,128)(2,1)S(1)}, bf16[144,768]{1,0:T(8,128)(2,1)S(1)}, u32[]{:S(2)}, u32[]{:S(2)}) collective-permute-start(bf16[144,768]{1,0:T(8,128)(2,1)S(1)} %get-tuple-element.191), channel_id=1, source_target_pairs={{0,24},{2,26},{4,28},{6,30},{24,0},{26,2},{28,4},{30,6},{1,25},{3,... | collective-permute-start | bytes 663560 | tf_op jit(solution)/shard_map/ppermute | solution.py:1277
  615.7 29.2 %collective-permute-start.22 = (bf16[192,768]{1,0:T(8,128)(2,1)S(1)}, bf16[192,768]{1,0:T(8,128)(2,1)S(1)}, u32[]{:S(2)}, u32[]{:S(2)}) collective-permute-start(bf16[192,768]{1,0:T(8,128)(2,1)S(1)} %get-tuple-element.181), channel_id=1, source_target_pairs={{0,16},{2,18},{4,20},{6,22},{8,24},{10,26},{12,28},{14,30},{16,0},... | collective-permute-start | bytes 884744 | tf_op jit(solution)/shard_map/ppermute | solution.py:957
  618.7 26.2 %collective-permute-start.23 = (bf16[192,768]{1,0:T(8,128)(2,1)S(1)}, bf16[192,768]{1,0:T(8,128)(2,1)S(1)}, u32[]{:S(2)}, u32[]{:S(2)}) collective-permute-start(bf16[192,768]{1,0:T(8,128)(2,1)S(1)} %get-tuple-element.179), channel_id=1, source_target_pairs={{0,8},{2,10},{4,12},{6,14},{8,0},{10,2},{12,4},{14,6},{16,24},{18,... | collective-permute-start | bytes 884744 | tf_op jit(solution)/shard_map/ppermute | solution.py:957
  (58 other events, 514.8 us)
Sparse Core Ops, SparseCore 0:
  35.8 111.5 all-gather.8
  149.0 110.7 all-gather.10
  279.7 135.9 all-gather.12
  417.8 63.0 all-gather.14

commit v2 on v1

--- a/solution.py
+++ b/solution.py
@@ -580,7 +580,7 @@
         out_specs=[pl.BlockSpec((own_ff, width), whole)] * 2,
         out_shape=[jax.ShapeDtypeStruct((own_ff, width), f32)] * 2,
         compiler_params=params(1),
-        cost_estimate=cost(6),
+        cost_estimate=cost(1),
         name="hidden_grads",
     )(c_array, gz_array, fc_own, red_own, bias)
 
@@ -622,7 +622,7 @@
             jax.ShapeDtypeStruct((own_ff, ctx * rows), f32),
         ],
         compiler_params=params(1),
-        cost_estimate=cost(5),
+        cost_estimate=cost(1),
         name="hidden_ready",
     )(c_array, fc_own, bias)
 
@@ -660,7 +660,7 @@
         out_specs=[pl.BlockSpec((own_ff, width), whole)] * 2,
         out_shape=[jax.ShapeDtypeStruct((own_ff, width), f32)] * 2,
         compiler_params=params(1),
-        cost_estimate=cost(5),
+        cost_estimate=cost(1),
         name="hidden_last",
     )(c_array, gz_all, active, slope, red_own)
 
@@ -695,7 +695,7 @@
         out_specs=pl.BlockSpec((lanes // 2, width), lambda i: (0, 0)),
         out_shape=jax.ShapeDtypeStruct((lanes // 2, width), f32),
         compiler_params=params(1),
-        cost_estimate=cost(4),
+        cost_estimate=cost(1),
         name="head_grads",
     )(pack, rows_array)
 
@@ -1154,31 +1154,30 @@
             dqkv, gz_held = lax.optimization_barrier((dqkv, gz_held))
             gz_other = flip(gz_held, 2, ctx)
         dqkv_own = exchange(dqkv.reshape(ctx, local, 6 * hd))
-        if l == 0:
-            g_head = [
-                head_grads(dqkv, saved[0][1], 0, rows),
-                head_grads(kept[1][2], acts, at_acts["next_a"], rows),
-                head_grads(saved[1][4], acts, at_acts["next_gy"], rows),
-            ]
-            g_hidden_second = hidden_grads(
-                acts, at_acts["next_c"], all_second, at_second["cot"],
-                *own_parts[1][:2], bias[1], rows,
-            )
-            ready = hidden_ready(acts, at_acts["c"], own_parts[0][0], bias[0], rows)
-            dqkv_own, g_head, ready, g_hidden_second, gz_other = lax.optimization_barrier(
-                (dqkv_own, g_head, ready, g_hidden_second, gz_other)
-            )
-            gz_held = both_sides(gz_held, gz_other, 2, ctx_index)
-            for mask in [1] + [1 << n for n in range(4, ctx.bit_length() - 1)]:
-                gz_held = both_sides(gz_held, flip(gz_held, mask, ctx), mask, ctx_index)
-            gz_all = gz_held.reshape(ctx // 4, 4 * rows, width)
-        gin, vg_early = qkv_backward(dqkv_own, x, gmid, vecs[l], all_first, in_at[l], own_in)
-        vec_grads[l] = jnp.concatenate([vg_early[:4], vg_late], axis=0)
         kept[l] = (gz, gy, dqkv)
-        grad = gin
-    input_grad = grad.reshape(seqs, local, width)
+        if l == 1:
+            gin, vg_early = qkv_backward(dqkv_own, x, gmid, vecs[l], all_first, in_at[l], own_in)
+            vec_grads[l] = jnp.concatenate([vg_early[:4], vg_late], axis=0)
+            grad = gin
 
     gy_all = gather(kept[0][1])
+    ready = hidden_ready(acts, at_acts["c"], own_parts[0][0], bias[0], rows)
+    g_in_first = head_grads(kept[0][2], saved[0][1], 0, rows)
+    ready, gz_other, dqkv_own, g_in_first = lax.optimization_barrier(
+        (ready, gz_other, dqkv_own, g_in_first)
+    )
+    gz_held = both_sides(gz_held, gz_other, 2, ctx_index)
+    gz_other = flip(gz_held, 1, ctx)
+    g_head = [
+        g_in_first,
+        head_grads(kept[1][2], acts, at_acts["next_a"], rows),
+        head_grads(saved[1][4], acts, at_acts["next_gy"], rows),
+    ]
+    gz_other, g_head = lax.optimization_barrier((gz_other, g_head))
+    gz_held = both_sides(gz_held, gz_other, 1, ctx_index)
+    for bit in range(4, ctx.bit_length() - 1):
+        gz_held = both_sides(gz_held, flip(gz_held, 1 << bit, ctx), 1 << bit, ctx_index)
+    gz_all = gz_held.reshape(ctx // 4, 4 * rows, width)
 
     def owned(first, second):
         given = jnp.where(owner_first, second, first).astype(bf16)
@@ -1186,20 +1185,26 @@
         return jnp.where(owner_first, first, second) + taken
 
     g_in_head = owned(g_head[0], g_head[1]).astype(bf16)
-    hidden_second = jnp.concatenate(g_hidden_second, axis=0)
     old_hidden = jnp.concatenate([expand_moment[0].T, reduce_moment[0]], axis=0)
-    vec_terms = jnp.stack(vec_grads).reshape(layers, ctx, own_vec).swapaxes(0, 1)
-    gz_all, input_grad, hidden_second, old_hidden, g_in_head, vec_terms, ready, g_head = (
-        lax.optimization_barrier(
-            (gz_all, input_grad, hidden_second, old_hidden, g_in_head, vec_terms, ready, g_head)
-        )
-    )
+    gz_all, old_hidden = lax.optimization_barrier((gz_all, old_hidden))
     hidden_first = jnp.concatenate(
         hidden_last(acts, at_acts["c"], gz_all, *ready, own_parts[0][1], rows), axis=0
     )
-    vec_terms, hidden_first = lax.optimization_barrier((vec_terms, hidden_first))
-    vec_sums = jnp.sum(exchange(vec_terms), axis=0)
+    hidden_first, acts = lax.optimization_barrier((hidden_first, acts))
+    hidden_second = jnp.concatenate(
+        hidden_grads(
+            acts, at_acts["next_c"], all_second, at_second["cot"], *own_parts[1][:2], bias[1], rows
+        ),
+        axis=0,
+    )
+    gy_all, _ = lax.optimization_barrier((gy_all, hidden_second))
     moved = muon_moment * old_hidden + owned(hidden_first, hidden_second)
+    moved, dqkv_own = lax.optimization_barrier((moved, dqkv_own))
+    gin, vg_early = qkv_backward(dqkv_own, x, gmid, vecs[0], all_first, in_at[0], own_in)
+    vec_grads[0] = jnp.concatenate([vg_early[:4], vg_late], axis=0)
+    input_grad = gin.reshape(seqs, local, width)
+    vec_terms = jnp.stack(vec_grads).reshape(layers, ctx, own_vec).swapaxes(0, 1)
+    vec_terms = jnp.pad(vec_terms, ((0, 0), (0, 8 - layers), (0, width - own_vec)))
     m_fc = moved[:own_ff].T
     m_red = moved[own_ff:]
 
@@ -1216,7 +1221,8 @@
         low = jnp.where(z == 0, pieces[0], pieces[1])
         return jnp.where(z < 2, low, jnp.where(z == 2, pieces[2], pieces[3]))
 
-    started, vec_sums = lax.optimization_barrier((gather_start(piece_for, role, ctx), vec_sums))
+    started, vec_terms = lax.optimization_barrier((gather_start(piece_for, role, ctx), vec_terms))
+    vec_sums = lax.psum_scatter(vec_terms, "ctx", scatter_dimension=0)
     columns = gather_finish(started, ctx)
 
     groups = ctx // 4
@@ -1282,6 +1288,7 @@
         (own_in, own_ff, own_mix),
     )
     direction, taken, vec_sums = lax.optimization_barrier((direction, taken, vec_sums))
+    vec_sums = vec_sums[:layers, :own_vec]
     vec_given = jnp.where(owner_first, vec_sums[1], vec_sums[0])
     vec_kept = jnp.where(owner_first, vec_sums[0], vec_sums[1])
     vec_grad = (vec_kept + lax.ppermute(vec_given, "dp", [(0, 1), (1, 0)]))[None]

time: 666 us -> 669 us (level)
  blocking collectives: 86.9 us -> 108 us
  starting transfers between devices: 64.7 us -> 49.8 us
    all_to_all x5 -> x4, waiting for transfers between devices: 53.2 us -> 21.6 us  [exchange(): lax.all_to_all(packed, 'ctx', split_axis=0, concat_axis=0, tiled=True)]
    ppermute x17, waiting for transfers between devices: 64.3 us -> 92 us  [flip(): return lax.ppermute(array, 'ctx', [(j, j ^ mask) for j in range(ctx)])]
    all_to_all x3, blocking collectives: 86.9 us -> 108 us  [exchange(): lax.all_to_all(packed, 'ctx', split_axis=0, concat_axis=0, tiled=True)]
    ppermute x17, starting transfers between devices: 30 us -> 17.4 us  [flip(): return lax.ppermute(array, 'ctx', [(j, j ^ mask) for j in range(ctx)])]
    ppermute x3, waiting for transfers between devices: 3.21 us -> 15.7 us  [owned(): taken = lax.ppermute(given, 'dp', [(0, 1), (1, 0)]).astype(f32)]
    all_gather x4, waiting for transfers between devices: 132 us -> 122 us  [gather(): return lax.all_gather(array, 'ctx', axis=0, tiled=False)]
    all_to_all x5 -> x4, starting transfers between devices: 21.5 us -> 15.6 us  [exchange(): lax.all_to_all(packed, 'ctx', split_axis=0, concat_axis=0, tiled=True)]
  transfers between devices with their start and end apart: 34 -> 34, of which waited for: 17 -> 19; matrix products, arithmetic and copies ran while one was open for 4% -> 5% of each run, Pallas kernels for 22% -> 23%
where the time goes in v2:
time: 669 us; the launch traced here: 665 us
  waiting for transfers between devices  277 us (41%)
  Pallas kernels  168 us (25%)
  blocking collectives  108 us (16%)
  starting transfers between devices  49.8 us (7%)
  other arithmetic  25.9 us (4%)
  local copies, waits for them, and re-layouts  21 us (3%)
  between operations  14.7 us (2%)
    all_gather x4, waiting for transfers between devices, gather(): return lax.all_gather(array, 'ctx', axis=0, tiled=False)  122 us
    all_to_all x3, blocking collectives, exchange(): lax.all_to_all(packed, 'ctx', split_axis=0, concat_axis=0, tiled=True)  108 us
    ppermute x17, waiting for transfers between devices, flip(): return lax.ppermute(array, 'ctx', [(j, j ^ mask) for j in range(ctx)])  92 us
    pallas_call x1, Pallas kernels, orthogonal(): pl.pallas_call(functools.partial(ns_kernel, own, len(parts)), out_shape=j...  37.1 us
    all_to_all x4, waiting for transfers between devices, exchange(): lax.all_to_all(packed, 'ctx', split_axis=0, concat_axis=0, tiled=True)  21.6 us
    ppermute x1, waiting for transfers between devices, body(): pack_other = lax.ppermute(pack, 'dp', [(0, 1), (1, 0)])  20.2 us
    ppermute x17, starting transfers between devices, flip(): return lax.ppermute(array, 'ctx', [(j, j ^ mask) for j in range(ctx)])  17.4 us
    pallas_call x2, Pallas kernels, mlp_backward(): pl.pallas_call(mlp_bwd_kernel, grid=(steps,), in_specs=[pl.BlockSpec((row...  17.3 us
  transfers between devices with their start and end apart: 34, of which 19 were waited for; matrix products, arithmetic and copies ran while one was open for 5% of the time, Pallas kernels for 23%

profile of v2, /device:TPU:0, one launch (start us, length us, event | category | flops | bytes accessed | tf_op | source)
XLA Modules:
  0.0 665.1 jit_solution(4796736759104041626)
XLA Ops:
  13.3 20.2 %collective-permute-done = bf16[592,768]{1,0:T(8,128)(2,1)S(1)} collective-permute-done((bf16[592,768]{1,0:T(8,128)(2,1)S(1)}, bf16[592,768]{1,0:T(8,128)(2,1)S(1)}, u32[]{:S(2)}, u32[]{:S(2)}) %collective-permute-start) | collective-permute-done | bytes 909344 | tf_op jit(solution)/shard_map/ppermute | solution.py:1053
  39.4 108.1 %all-gather.9.cloned.1.call-done = bf16[13824,768]{1,0:T(8,128)(2,1)} async-done(((bf16[864,768]{1,0:T(8,128)(2,1)}), bf16[13824,768]{1,0:T(8,128)(2,1)}) %all-gather.9.cloned.1.call-update) | async-done | bytes 21233680 | tf_op jit(solution)/shard_map/all_gather | solution.py:953
  156.6 7.9 %attn_forward.2 = (f32[1024,128]{1,0:T(8,128)}, bf16[1024,128]{1,0:T(8,128)(2,1)}, bf16[2,1024,1024]{2,1,0:T(8,128)(2,1)}) custom-call(s32[1024,1]{1,0:T(8,128)} %add.112.qpos_ref, s32[1,1024]{1,0:T(1,128)} %add.96.kpos_ref, bf16[1024,384]{1,0:T(8,128)(2,1)} %get-tuple-element.83.q_ref.k_ref.v_ref, bf16[1024,384]{1,0:T(8,128)(2,1)} %get-tuple-element.83.q_ref.k_ref.v_ref, ...), custom_call_target="tpu_custom_call" | custom-call | flops 8000000000 | bytes 8000000 | tf_op jit(solution)/shard_map/attn_forward/pallas_call | solution.py:246
  170.0 13.9 %all-to-all-done.o_ref = bf16[16,64,128]{2,1,0:T(8,128)(2,1)S(1)} async-done(((bf16[16,64,128]{2,1,0:T(8,128)(2,1)}), bf16[16,64,128]{2,1,0:T(8,128)(2,1)S(1)}, u32[]{:S(2)}, u32[]{:S(2)}) %all-to-all-start) | async-done | bytes 262176 | tf_op jit(solution)/shard_map/all_to_all | solution.py:949
  184.6 8.2 %mlp_forward.2 = (f32[128,768]{1,0:T(8,128)}, bf16[128,768]{1,0:T(8,128)(2,1)}, f32[128,3072]{1,0:T(8,128)}, f32[128,768]{1,0:T(8,128)}) custom-call(bf16[16,64,128]{2,1,0:T(8,128)(2,1)} %copy-done.19, bf16[128,768]{1,0:T(8,128)(2,1)} %bitcast.152, f32[12,768]{1,0:T(8,128)} %copy-done.16, bf16[16,864,768]{2,1,0:T(8,128)(2,1)} %bitcast.126, ...), custom_call_target="tpu_custom_call" | custom-call | flops 8000000000 | bytes 8000000 | tf_op jit(solution)/shard_map/mlp_forward/pallas_call | solution.py:355
  198.3 35.7 %all_to_all.35 = bf16[16,64,384]{2,1,0:T(8,128)(2,1)} all-to-all(bf16[16,64,384]{2,1,0:T(8,128)(2,1)} %get-tuple-element.86), channel_id=1, replica_groups=mesh['ctx'=16,'dp'=2] {'ctx'}, dimensions={0} | all-to-all | bytes 1572864 | tf_op jit(solution)/shard_map/all_to_all | solution.py:949
  234.1 7.9 %attn_forward.3 = (f32[1024,128]{1,0:T(8,128)}, bf16[1024,128]{1,0:T(8,128)(2,1)}, bf16[2,1024,1024]{2,1,0:T(8,128)(2,1)}) custom-call(s32[1024,1]{1,0:T(8,128)} %add.112.qpos_ref, s32[1,1024]{1,0:T(1,128)} %add.96.kpos_ref, bf16[1024,384]{1,0:T(8,128)(2,1)} %bitcast.159, bf16[1024,384]{1,0:T(8,128)(2,1)} %bitcast.160, bf16[1024,384]{1,0:T(8,128)(2,1)} %bitcast.161), custom_call_target="tpu_custom_call" | custom-call | flops 8000000000 | bytes 8000000 | tf_op jit(solution)/shard_map/attn_forward/pallas_call | solution.py:246
  245.7 14.2 %all-gather.11.cloned.1.call-done = bf16[11008,768]{1,0:T(8,128)(2,1)} async-done(((bf16[688,768]{1,0:T(8,128)(2,1)}), bf16[11008,768]{1,0:T(8,128)(2,1)}) %all-gather.11.cloned.1.call-update) | async-done | bytes 16908304 | tf_op jit(solution)/shard_map/all_gather | solution.py:953
  260.8 8.1 %mlp_forward.3 = (f32[128,768]{1,0:T(8,128)}, bf16[128,768]{1,0:T(8,128)(2,1)}, f32[128,3072]{1,0:T(8,128)}, f32[128,768]{1,0:T(8,128)}) custom-call(bf16[16,64,128]{2,1,0:T(8,128)(2,1)} %copy-done.18, f32[128,768]{1,0:T(8,128)} %get-tuple-element.85.x_ref, f32[12,768]{1,0:T(8,128)} %reshape.191.vec_ref, bf16[16,688,768]{2,1,0:T(8,128)(2,1)} %bitcast.135, ...), custom_call_target="tpu_custom_call" | custom-call | flops 8000000000 | bytes 8000000 | tf_op jit(solution)/shard_map/mlp_forward/pallas_call | solution.py:355
  269.0 8.6 %mlp_backward.2 = (bf16[128,768]{1,0:T(8,128)(2,1)}, f32[128,768]{1,0:T(8,128)}, bf16[128,768]{1,0:T(8,128)(2,1)}, bf16[16,64,128]{2,1,0:T(8,128)(2,1)}, f32[8,768]{1,0:T(8,128)}) custom-call(bf16[128,768]{1,0:T(8,128)(2,1)} %bitcast.157, f32[128,768]{1,0:T(8,128)} %get-tuple-element.92.mid_ref, f32[128,3072]{1,0:T(8,128)} %get-tuple-element.93.h_ref, ...), custom_call_target="tpu_custom_call" | custom-call | flops 8000000000 | bytes 8000000 | tf_op jit(solution)/shard_map/mlp_backward/pallas_call | solution.py:440
  279.7 36.8 %all_to_all.36 = bf16[16,64,128]{2,1,0:T(8,128)(2,1)} all-to-all(bf16[16,64,128]{2,1,0:T(8,128)(2,1)S(1)} %copy-done.32), channel_id=1, replica_groups=mesh['ctx'=16,'dp'=2] {'ctx'}, dimensions={0} | all-to-all | bytes 524288 | tf_op jit(solution)/shard_map/all_to_all | solution.py:949
  316.5 7.6 %attn_backward.2.pack_ref = bf16[1024,384]{1,0:T(8,128)(2,1)} custom-call(bf16[1024,384]{1,0:T(8,128)(2,1)} %bitcast.162, bf16[1024,128]{1,0:T(8,128)(2,1)} %bitcast.172, f32[1024,128]{1,0:T(8,128)} %get-tuple-element.98.of_ref, bf16[2,1024,1024]{2,1,0:T(8,128)(2,1)} %get-tuple-element.99.p_ref, bf16[1024,384]{1,0:T(8,128)(2,1)} %bitcast.163, ...), custom_call_target="tpu_custom_call" | custom-call | flops 8000000000 | bytes 8000000 | tf_op jit(solution)/shard_map/attn_backward/pallas_call | solution.py:305
  324.1 35.7 %all_to_all.37.d_ref = bf16[16,64,384]{2,1,0:T(8,128)(2,1)} all-to-all(bf16[16,64,384]{2,1,0:T(8,128)(2,1)} %bitcast.150), channel_id=1, replica_groups=mesh['ctx'=16,'dp'=2] {'ctx'}, dimensions={0} | all-to-all | bytes 1572864 | tf_op jit(solution)/shard_map/all_to_all | solution.py:949
  365.2 8.7 %mlp_backward.3 = (bf16[128,768]{1,0:T(8,128)(2,1)}, f32[128,768]{1,0:T(8,128)}, bf16[128,768]{1,0:T(8,128)(2,1)}, bf16[16,64,128]{2,1,0:T(8,128)(2,1)}, f32[8,768]{1,0:T(8,128)}) custom-call(f32[128,768]{1,0:T(8,128)} %get-tuple-element.101.gr_ref, f32[128,768]{1,0:T(8,128)} %get-tuple-element.102.mid_ref, f32[128,3072]{1,0:T(8,128)} %get-tuple-element.103.h_ref, ...), custom_call_target="tpu_custom_call" | custom-call | flops 8000000000 | bytes 8000000 | tf_op jit(solution)/shard_map/mlp_backward/pallas_call | solution.py:440
  387.9 13.2 %collective-permute-done.2 = bf16[128,768]{1,0:T(8,128)(2,1)S(1)} collective-permute-done((bf16[128,768]{1,0:T(8,128)(2,1)}, bf16[128,768]{1,0:T(8,128)(2,1)S(1)}, u32[]{:S(2)}, u32[]{:S(2)}) %collective-permute-start.2) | collective-permute-done | bytes 196640 | tf_op jit(solution)/shard_map/ppermute | solution.py:957
  402.3 7.5 %all-to-all-done.5 = bf16[16,64,128]{2,1,0:T(8,128)(2,1)S(1)} async-done(((bf16[16,64,128]{2,1,0:T(8,128)(2,1)}), bf16[16,64,128]{2,1,0:T(8,128)(2,1)S(1)}, u32[]{:S(2)}, u32[]{:S(2)}) %all-to-all-start.5) | async-done | bytes 262176 | tf_op jit(solution)/shard_map/all_to_all | solution.py:949
  410.4 7.4 %attn_backward.3.pack_ref = bf16[1024,384]{1,0:T(8,128)(2,1)} custom-call(bf16[1024,384]{1,0:T(8,128)(2,1)} %get-tuple-element.83.q_ref.k_ref.v_ref, bf16[1024,128]{1,0:T(8,128)(2,1)} %bitcast.171, f32[1024,128]{1,0:T(8,128)} %get-tuple-element.105.of_ref, bf16[2,1024,1024]{2,1,0:T(8,128)(2,1)} %get-tuple-element.106.p_ref, ...), custom_call_target="tpu_custom_call" | custom-call | flops 8000000000 | bytes 8000000 | tf_op jit(solution)/shard_map/attn_backward/pallas_call | solution.py:305
  434.3 17.8 %collective-permute-done.4 = bf16[4,128,768]{2,1,0:T(8,128)(2,1)S(1)} collective-permute-done((bf16[4,128,768]{2,1,0:T(8,128)(2,1)S(1)}, bf16[4,128,768]{2,1,0:T(8,128)(2,1)S(1)}, u32[]{:S(2)}, u32[]{:S(2)}) %collective-permute-start.4) | collective-permute-done | bytes 786464 | tf_op jit(solution)/shard_map/ppermute | solution.py:957
  480.4 7.6 %hidden_grads.1 = (f32[192,768]{1,0:T(8,128)}, f32[192,768]{1,0:T(8,128)}) custom-call(bf16[16,704,768]{2,1,0:T(8,128)(2,1)} %bitcast.146, bf16[16,688,768]{2,1,0:T(8,128)(2,1)} %bitcast.141, bf16[192,768]{1,0:T(8,128)(2,1)} %get-tuple-element.180.fc_ref, bf16[192,768]{1,0:T(8,128)(2,1)} %get-tuple-element.179.red_ref, f32[192,1]{1,0:T(8,128)} %copy.34.bias_ref), custom_call_target="tpu_custom_call" | custom-call | flops 1000000000 | bytes 1000000 | tf_op jit(solution)/shard_map/hidden_grads/pallas_call | solution.py:570
  496.5 11.1 %collective-permute-done.8 = bf16[64,768]{1,0:T(8,128)(2,1)S(1)} collective-permute-done((bf16[64,768]{1,0:T(8,128)(2,1)S(1)}, bf16[64,768]{1,0:T(8,128)(2,1)S(1)}, u32[]{:S(2)}, u32[]{:S(2)}) %collective-permute-start.8) | collective-permute-done | bytes 98336 | tf_op jit(solution)/shard_map/ppermute | solution.py:1184
  540.4 19.9 %collective-permute-done.14.refs_3_ = bf16[3,192,768]{2,1,0:T(8,128)(2,1)S(1)} collective-permute-done((bf16[3,192,768]{2,1,0:T(8,128)(2,1)S(1)}, bf16[3,192,768]{2,1,0:T(8,128)(2,1)S(1)}, u32[]{:S(2)}, u32[]{:S(2)}) %collective-permute-start.14) | collective-permute-done | bytes 884768 | tf_op jit(solution)/shard_map/ppermute | solution.py:957
  563.7 7.7 %sum_heads.1 = (bf16[2304,768]{1,0:T(8,128)(2,1)}, bf16[4,144,768]{2,1,0:T(8,128)(2,1)}) custom-call(s32[1]{0:T(128)} %bitcast.44.role_ref, s32[1]{0:T(128)} %bitcast.54.near_ref, bf16[192,768]{1,0:T(8,128)(2,1)} %copy-done.17, bf16[3,192,768]{2,1,0:T(8,128)(2,1)} %copy-done.3, bf16[192,768]{1,0:T(8,128)(2,1)} %collective-permute-done.12.refs_2_, ...), custom_call_target="tpu_custom_call" | custom-call | flops 4000000000 | bytes 4000000 | tf_op jit(solution)/shard_map/sum_heads/pallas_call | solution.py:926
  581.1 37.1 %newton_schulz.1 = bf16[768,768]{1,0:T(8,128)(2,1)} custom-call(s32[1]{0:T(128)} %bitcast.44.role_ref, bf16[192,768]{1,0:T(8,128)(2,1)} %copy-done.17, bf16[576,768]{1,0:T(8,128)(2,1)} %bitcast.149, bf16[192,768]{1,0:T(8,128)(2,1)} %collective-permute-done.12.refs_2_, bf16[576,768]{1,0:T(8,128)(2,1)} %bitcast.156, ...), custom_call_target="tpu_custom_call" | custom-call | flops 46000001024 | bytes 46000000 | tf_op jit(solution)/shard_map/newton_schulz/pallas_call | solution.py:835
  640.1 14.7 %collective-permute-done.22 = bf16[192,768]{1,0:T(8,128)(2,1)S(1)} collective-permute-done((bf16[192,768]{1,0:T(8,128)(2,1)S(1)}, bf16[192,768]{1,0:T(8,128)(2,1)S(1)}, u32[]{:S(2)}, u32[]{:S(2)}) %collective-permute-start.22) | collective-permute-done | bytes 294944 | tf_op jit(solution)/shard_map/ppermute | solution.py:957
  (245 shorter events, 184.9 us)
Async XLA Ops:
  7.2 140.2 %all-gather.9.cloned.1.call-start = ((), (), s32[]{:S(2)}) async-start(), calls=%async_computation.9 | async-start | bytes 22560768 | tf_op jit(solution)/shard_map/all_gather | solution.py:953
  10.3 23.2 %collective-permute-start = (bf16[592,768]{1,0:T(8,128)(2,1)S(1)}, bf16[592,768]{1,0:T(8,128)(2,1)S(1)}, u32[]{:S(2)}, u32[]{:S(2)}) collective-permute-start(bf16[592,768]{1,0:T(8,128)(2,1)S(1)} %constant_dynamic-update-slice_fusion), channel_id=1, source_target_pairs={{0,1},{1,0},{2,3},{3,2},{4,5},{5,4},{6,7},{7,6},{8,9},{9,8},{10,11... | collective-permute-start | bytes 2727944 | tf_op jit(solution)/shard_map/ppermute | solution.py:1053
  35.8 224.1 %all-gather.11.cloned.1.call-start = ((), (), s32[]{:S(2)}) async-start(), calls=%async_computation.10 | async-start | bytes 17965056 | tf_op jit(solution)/shard_map/all_gather | solution.py:953
  164.6 19.3 %all-to-all-start = ((bf16[16,64,128]{2,1,0:T(8,128)(2,1)}), bf16[16,64,128]{2,1,0:T(8,128)(2,1)S(1)}, u32[]{:S(2)}, u32[]{:S(2)}) async-start(bf16[16,64,128]{2,1,0:T(8,128)(2,1)} %bitcast.170), calls=%async_computation | async-start | bytes 524288 | tf_op jit(solution)/shard_map/all_to_all | solution.py:949
  242.0 18.1 %all-to-all-start.2 = ((bf16[16,64,128]{2,1,0:T(8,128)(2,1)}), bf16[16,64,128]{2,1,0:T(8,128)(2,1)S(1)}, u32[]{:S(2)}, u32[]{:S(2)}) async-start(bf16[16,64,128]{2,1,0:T(8,128)(2,1)} %bitcast.155), calls=%async_computation.2 | async-start | bytes 524288 | tf_op jit(solution)/shard_map/all_to_all | solution.py:949
  245.6 183.3 %all-gather.13.cloned.1.call-start = ((), (), s32[]{:S(2)}) async-start(), calls=%async_computation.11 | async-start | bytes 18382848 | tf_op jit(solution)/shard_map/all_gather | solution.py:953
  374.0 27.2 %collective-permute-start.2 = (bf16[128,768]{1,0:T(8,128)(2,1)}, bf16[128,768]{1,0:T(8,128)(2,1)S(1)}, u32[]{:S(2)}, u32[]{:S(2)}) collective-permute-start(bf16[128,768]{1,0:T(8,128)(2,1)} %get-tuple-element.107), channel_id=1, source_target_pairs={{0,16},{2,18},{4,20},{6,22},{8,24},{10,26},{12,28},{14,30},{16,0},... | collective-permute-start | bytes 589832 | tf_op jit(solution)/shard_map/ppermute | solution.py:957
  374.2 27.0 %collective-permute-start.3 = (bf16[128,768]{1,0:T(8,128)(2,1)}, bf16[128,768]{1,0:T(8,128)(2,1)S(1)}, u32[]{:S(2)}, u32[]{:S(2)}) collective-permute-start(bf16[128,768]{1,0:T(8,128)(2,1)} %get-tuple-element.107), channel_id=1, source_target_pairs={{0,8},{2,10},{4,12},{6,14},{8,0},{10,2},{12,4},{14,6},{16,24},{18,... | collective-permute-start | bytes 589832 | tf_op jit(solution)/shard_map/ppermute | solution.py:957
  378.3 31.4 %all-to-all-start.5 = ((bf16[16,64,128]{2,1,0:T(8,128)(2,1)}), bf16[16,64,128]{2,1,0:T(8,128)(2,1)S(1)}, u32[]{:S(2)}, u32[]{:S(2)}) async-start(bf16[16,64,128]{2,1,0:T(8,128)(2,1)} %get-tuple-element.104), calls=%async_computation.5 | async-start | bytes 524288 | tf_op jit(solution)/shard_map/all_to_all | solution.py:949
  381.9 109.0 %all-gather.15.cloned.1.call-start = ((), (), s32[]{:S(2)}) async-start(), calls=%async_computation.12 | async-start | bytes 3342336 | tf_op jit(solution)/shard_map/all_gather | solution.py:953
  417.8 34.3 %all-to-all-start.6 = ((bf16[16,64,384]{2,1,0:T(8,128)(2,1)}), bf16[16,64,384]{2,1,0:T(8,128)(2,1)S(1)}, u32[]{:S(2)}, u32[]{:S(2)}) async-start(bf16[16,64,384]{2,1,0:T(8,128)(2,1)} %bitcast.151), calls=%async_computation.6 | async-start | bytes 1572864 | tf_op jit(solution)/shard_map/all_to_all | solution.py:949
  421.6 201.5 %reduce-scatter.2.cloned.1.call-start = ((), (), s32[]{:S(2)}) async-start(), calls=%async_computation.8 | async-start | bytes 417792 | tf_op jit(solution)/shard_map/reduce_scatter | solution.py:1225
  421.6 30.5 %collective-permute-start.4 = (bf16[4,128,768]{2,1,0:T(8,128)(2,1)S(1)}, bf16[4,128,768]{2,1,0:T(8,128)(2,1)S(1)}, u32[]{:S(2)}, u32[]{:S(2)}) collective-permute-start(bf16[4,128,768]{2,1,0:T(8,128)(2,1)S(1)} %pad_maximum_fusion.5), channel_id=1, source_target_pairs={{0,4},{2,6},{4,0},{6,2},{8,12},{10,14},{12,8},{14,10},{16,20},{18,... | collective-permute-start | bytes 2359304 | tf_op jit(solution)/shard_map/ppermute | solution.py:957
  489.4 18.3 %collective-permute-start.6 = (bf16[384,768]{1,0:T(8,128)(2,1)S(1)}, bf16[384,768]{1,0:T(8,128)(2,1)}, u32[]{:S(2)}, u32[]{:S(2)}) collective-permute-start(bf16[384,768]{1,0:T(8,128)(2,1)S(1)} %select_convert_fusion), channel_id=1, source_target_pairs={{0,1},{1,0},{2,3},{3,2},{4,5},{5,4},{6,7},{7,6},{8,9},{9,8},{10,11... | collective-permute-start | bytes 1769480 | tf_op jit(solution)/shard_map/ppermute | solution.py:1184
  496.1 17.6 %collective-permute-start.7 = (bf16[192,768]{1,0:T(8,128)(2,1)S(1)}, bf16[192,768]{1,0:T(8,128)(2,1)S(1)}, u32[]{:S(2)}, u32[]{:S(2)}) collective-permute-start(bf16[192,768]{1,0:T(8,128)(2,1)S(1)} %select_convert_fusion.1), channel_id=1, source_target_pairs={{0,1},{1,0},{2,3},{3,2},{4,5},{5,4},{6,7},{7,6},{8,9},{9,8},{10,11... | collective-permute-start | bytes 884744 | tf_op jit(solution)/shard_map/ppermute | solution.py:1184
  514.1 17.5 %collective-permute-start.12 = (bf16[192,768]{1,0:T(8,128)(2,1)S(1)}, bf16[192,768]{1,0:T(8,128)(2,1)}, u32[]{:S(2)}, u32[]{:S(2)}) collective-permute-start(bf16[192,768]{1,0:T(8,128)(2,1)S(1)} %get-tuple-element.138.refs_0_), channel_id=1, source_target_pairs={{0,4},{2,6},{4,0},{6,2},{8,12},{10,14},{12,8},{14,10},{16,20},{18,... | collective-permute-start | bytes 884744 | tf_op jit(solution)/shard_map/ppermute | solution.py:957
  518.7 20.2 %collective-permute-start.11 = (bf16[192,768]{1,0:T(8,128)(2,1)S(1)}, bf16[192,768]{1,0:T(8,128)(2,1)S(1)}, u32[]{:S(2)}, u32[]{:S(2)}) collective-permute-start(bf16[192,768]{1,0:T(8,128)(2,1)S(1)} %get-tuple-element.160), channel_id=1, source_target_pairs={{0,24},{2,26},{4,28},{6,30},{8,16},{10,18},{12,20},{14,22},{16,8},... | collective-permute-start | bytes 884744 | tf_op jit(solution)/shard_map/ppermute | solution.py:957
  539.0 21.3 %collective-permute-start.14 = (bf16[3,192,768]{2,1,0:T(8,128)(2,1)S(1)}, bf16[3,192,768]{2,1,0:T(8,128)(2,1)S(1)}, u32[]{:S(2)}, u32[]{:S(2)}) collective-permute-start(bf16[3,192,768]{2,1,0:T(8,128)(2,1)S(1)} %pad_maximum_fusion.4.refs_1_), channel_id=1, source_target_pairs={{0,4},{2,6},{4,0},{6,2},{8,12},{10,14},{12,8},{14,10},{16,20},{18,... | collective-permute-start | bytes 2654216 | tf_op jit(solution)/shard_map/ppermute | solution.py:957
  540.4 22.6 %collective-permute-start.15 = (bf16[3,192,768]{2,1,0:T(8,128)(2,1)S(1)}, bf16[3,192,768]{2,1,0:T(8,128)(2,1)}, u32[]{:S(2)}, u32[]{:S(2)}) collective-permute-start(bf16[3,192,768]{2,1,0:T(8,128)(2,1)S(1)} %pad_maximum_fusion.4.refs_1_), channel_id=1, source_target_pairs={{0,2},{2,0},{4,6},{6,4},{8,10},{10,8},{12,14},{14,12},{16,18},{18,... | collective-permute-start | bytes 2654216 | tf_op jit(solution)/shard_map/ppermute | solution.py:957
  572.7 50.4 %collective-permute-start.18 = (bf16[144,768]{1,0:T(8,128)(2,1)S(1)}, bf16[144,768]{1,0:T(8,128)(2,1)S(1)}, u32[]{:S(2)}, u32[]{:S(2)}) collective-permute-start(bf16[144,768]{1,0:T(8,128)(2,1)S(1)} %get-tuple-element.186), channel_id=1, source_target_pairs={{0,8},{2,10},{4,12},{6,14},{24,16},{26,18},{28,20},{30,22},{1,9},{... | collective-permute-start | bytes 663560 | tf_op jit(solution)/shard_map/ppermute | solution.py:1283
  574.5 48.6 %collective-permute-start.19 = (bf16[144,768]{1,0:T(8,128)(2,1)S(1)}, bf16[144,768]{1,0:T(8,128)(2,1)S(1)}, u32[]{:S(2)}, u32[]{:S(2)}) collective-permute-start(bf16[144,768]{1,0:T(8,128)(2,1)S(1)} %get-tuple-element.185), channel_id=1, source_target_pairs={{0,16},{2,18},{4,20},{6,22},{24,8},{26,10},{28,12},{30,14},{1,17},... | collective-permute-start | bytes 663560 | tf_op jit(solution)/shard_map/ppermute | solution.py:1283
  577.7 45.4 %collective-permute-start.20 = (bf16[144,768]{1,0:T(8,128)(2,1)S(1)}, bf16[144,768]{1,0:T(8,128)(2,1)S(1)}, u32[]{:S(2)}, u32[]{:S(2)}) collective-permute-start(bf16[144,768]{1,0:T(8,128)(2,1)S(1)} %get-tuple-element.184), channel_id=1, source_target_pairs={{0,24},{2,26},{4,28},{6,30},{24,0},{26,2},{28,4},{30,6},{1,25},{3,... | collective-permute-start | bytes 663560 | tf_op jit(solution)/shard_map/ppermute | solution.py:1283
  630.7 24.1 %collective-permute-start.22 = (bf16[192,768]{1,0:T(8,128)(2,1)S(1)}, bf16[192,768]{1,0:T(8,128)(2,1)S(1)}, u32[]{:S(2)}, u32[]{:S(2)}) collective-permute-start(bf16[192,768]{1,0:T(8,128)(2,1)S(1)} %get-tuple-element.174), channel_id=1, source_target_pairs={{0,16},{2,18},{4,20},{6,22},{8,24},{10,26},{12,28},{14,30},{16,0},... | collective-permute-start | bytes 884744 | tf_op jit(solution)/shard_map/ppermute | solution.py:957
  631.2 23.6 %collective-permute-start.23 = (bf16[192,768]{1,0:T(8,128)(2,1)S(1)}, bf16[192,768]{1,0:T(8,128)(2,1)S(1)}, u32[]{:S(2)}, u32[]{:S(2)}) collective-permute-start(bf16[192,768]{1,0:T(8,128)(2,1)S(1)} %get-tuple-element.172), channel_id=1, source_target_pairs={{0,8},{2,10},{4,12},{6,14},{8,0},{10,2},{12,4},{14,6},{16,24},{18,... | collective-permute-start | bytes 884744 | tf_op jit(solution)/shard_map/ppermute | solution.py:957
  (56 other events, 462.0 us)
Sparse Core Ops, SparseCore 0:
  35.9 111.5 all-gather.8
  149.0 110.7 all-gather.10
  279.8 135.1 all-gather.12
  417.2 55.0 all-gather.14
  562.0 60.9 reduce-scatter.1

commit v3 on v2

--- a/solution.py
+++ b/solution.py
@@ -627,42 +627,61 @@
     )(c_array, fc_own, bias)
 
 
-def hidden_last_kernel(c_ref, gz_ref, u_ref, slope_ref, red_ref, gfc_ref, gred_ref):
+def hidden_last_kernel(own_ref, c_ref, u_ref, slope_ref, red_ref, *refs):
+    gz_refs, (gfc_ref, gred_ref) = refs[:-2], refs[-2:]
     width = red_ref.shape[1]
-    second = c_ref[...].reshape(-1, width)
-    branch = gz_ref[...].reshape(-1, width)
-    grad_hidden = (mm_nt(red_ref[...], branch) * slope_ref[...]).astype(bf16)
 
     @pl.when(pl.program_id(0) == 0)
     def _():
         gfc_ref[...] = jnp.zeros_like(gfc_ref)
         gred_ref[...] = jnp.zeros_like(gred_ref)
 
-    gred_ref[...] += mm(u_ref[...], branch)
-    gfc_ref[...] += mm(grad_hidden, second)
-
-
-def hidden_last(c_all, c_at, gz_all, active, slope, red_own, rows):
-    steps, _, width = gz_all.shape
+    for step, gz_ref in enumerate(gz_refs):
+
+        @pl.when(pl.program_id(0) == step)
+        def _():
+            branch = gz_ref[...]
+            grad_hidden = (mm_nt(red_ref[...], branch) * slope_ref[...]).astype(bf16)
+            gred_ref[...] += mm(u_ref[...], branch)
+            gfc_ref[...] += mm(grad_hidden, c_ref[...].reshape(-1, width))
+
+
+def hidden_last(c_all, c_at, columns, masks, ctx_index, active, slope, red_own, rows):
+    width = red_own.shape[1]
     own_ff = red_own.shape[0]
     c_array, c_spec = rows_by_z(c_all, c_at, rows)
-    whole = lambda i: (0, 0)
+
+    def place(index):
+        return (index >> 4) * 4 + (index & 1) * 2 + ((index >> 1) & 1)
+
+    def block(step, own_ref):
+        distance = 0
+        for number, mask in enumerate(masks):
+            distance = jnp.where(step == number, place(mask), distance)
+        return own_ref[0] ^ distance
+
+    whole = lambda i, own: (0, 0)
     return pl.pallas_call(
         hidden_last_kernel,
-        grid=(steps,),
-        in_specs=[
-            c_spec,
-            pl.BlockSpec((1, 4 * rows, width), lambda i: (i, 0, 0)),
-            pl.BlockSpec((own_ff, 4 * rows), lambda i: (0, i)),
-            pl.BlockSpec((own_ff, 4 * rows), lambda i: (0, i)),
-            pl.BlockSpec((own_ff, width), whole),
-        ],
-        out_specs=[pl.BlockSpec((own_ff, width), whole)] * 2,
+        grid_spec=pltpu.PrefetchScalarGridSpec(
+            num_scalar_prefetch=1,
+            grid=(len(columns),),
+            in_specs=[
+                pl.BlockSpec(
+                    c_spec.block_shape, lambda i, own: c_spec.index_map(block(i, own))
+                ),
+                pl.BlockSpec((own_ff, 4 * rows), lambda i, own: (0, block(i, own))),
+                pl.BlockSpec((own_ff, 4 * rows), lambda i, own: (0, block(i, own))),
+                pl.BlockSpec((own_ff, width), whole),
+            ]
+            + [pl.BlockSpec((4 * rows, width), whole)] * len(columns),
+            out_specs=[pl.BlockSpec((own_ff, width), whole)] * 2,
+        ),
         out_shape=[jax.ShapeDtypeStruct((own_ff, width), f32)] * 2,
         compiler_params=params(1),
         cost_estimate=cost(1),
         name="hidden_last",
-    )(c_array, gz_all, active, slope, red_own)
+    )(place(ctx_index)[None], c_array, active, slope, red_own, *columns)
 
 
 def head_grads_kernel(pack_ref, rows_ref, out_ref):
@@ -962,11 +981,6 @@
     odd, high = (z_here & 1) == 1, z_here >= 2
     first = [jnp.where(odd, held[k ^ 1], held[k]) for k in range(4)]
     return jnp.stack([jnp.where(high, first[k ^ 2], first[k]) for k in range(4)])
-
-
-def both_sides(held, other, mask, ctx_index):
-    upper = (ctx_index & mask) != 0
-    return jnp.stack([jnp.where(upper, other, held), jnp.where(upper, held, other)])
 
 
 def gather_start(piece_for, z_here, ctx):
@@ -1152,7 +1166,8 @@
         dqkv = attn_backward(qkv, go, out_full, prob)
         if l == 0:
             dqkv, gz_held = lax.optimization_barrier((dqkv, gz_held))
-            gz_other = flip(gz_held, 2, ctx)
+            gz_held = gz_held.reshape(4 * rows, width)
+            gz_sides = [flip(gz_held, mask, ctx) for mask in (2, 1)]
         dqkv_own = exchange(dqkv.reshape(ctx, local, 6 * hd))
         kept[l] = (gz, gy, dqkv)
         if l == 1:
@@ -1163,21 +1178,21 @@
     gy_all = gather(kept[0][1])
     ready = hidden_ready(acts, at_acts["c"], own_parts[0][0], bias[0], rows)
     g_in_first = head_grads(kept[0][2], saved[0][1], 0, rows)
-    ready, gz_other, dqkv_own, g_in_first = lax.optimization_barrier(
-        (ready, gz_other, dqkv_own, g_in_first)
-    )
-    gz_held = both_sides(gz_held, gz_other, 2, ctx_index)
-    gz_other = flip(gz_held, 1, ctx)
+    old_hidden = jnp.concatenate([expand_moment[0].T, reduce_moment[0]], axis=0)
+    ready, gz_sides, dqkv_own, g_in_first, old_hidden = lax.optimization_barrier(
+        (ready, gz_sides, dqkv_own, g_in_first, old_hidden)
+    )
+    gz_masks = [0, 2, 1, 3]
+    gz_columns = [gz_held, *gz_sides, flip(gz_sides[0], 1, ctx)]
+    for mask in [1 << n for n in range(4, ctx.bit_length() - 1)]:
+        gz_masks = gz_masks + [mask | other for other in gz_masks]
+        gz_columns = gz_columns + [flip(column, mask, ctx) for column in gz_columns]
     g_head = [
         g_in_first,
         head_grads(kept[1][2], acts, at_acts["next_a"], rows),
         head_grads(saved[1][4], acts, at_acts["next_gy"], rows),
     ]
-    gz_other, g_head = lax.optimization_barrier((gz_other, g_head))
-    gz_held = both_sides(gz_held, gz_other, 1, ctx_index)
-    for bit in range(4, ctx.bit_length() - 1):
-        gz_held = both_sides(gz_held, flip(gz_held, 1 << bit, ctx), 1 << bit, ctx_index)
-    gz_all = gz_held.reshape(ctx // 4, 4 * rows, width)
+    gz_columns, g_head = lax.optimization_barrier((gz_columns, g_head))
 
     def owned(first, second):
         given = jnp.where(owner_first, second, first).astype(bf16)
@@ -1185,12 +1200,13 @@
         return jnp.where(owner_first, first, second) + taken
 
     g_in_head = owned(g_head[0], g_head[1]).astype(bf16)
-    old_hidden = jnp.concatenate([expand_moment[0].T, reduce_moment[0]], axis=0)
-    gz_all, old_hidden = lax.optimization_barrier((gz_all, old_hidden))
     hidden_first = jnp.concatenate(
-        hidden_last(acts, at_acts["c"], gz_all, *ready, own_parts[0][1], rows), axis=0
-    )
-    hidden_first, acts = lax.optimization_barrier((hidden_first, acts))
+        hidden_last(
+            acts, at_acts["c"], gz_columns, gz_masks, ctx_index, *ready, own_parts[0][1], rows
+        ),
+        axis=0,
+    )
+    hidden_first, acts, g_in_head = lax.optimization_barrier((hidden_first, acts, g_in_head))
     hidden_second = jnp.concatenate(
         hidden_grads(
             acts, at_acts["next_c"], all_second, at_second["cot"], *own_parts[1][:2], bias[1], rows

time: 669 us -> 658 us (0.984)
  waiting for transfers between devices: 277 us -> 268 us
    ppermute x17 -> x18, waiting for transfers between devices: 92 us -> 89.4 us  [flip(): return lax.ppermute(array, 'ctx', [(j, j ^ mask) for j in range(ctx)])]
    ppermute x17 -> x18, starting transfers between devices: 17.4 us -> 18.1 us  [flip(): return lax.ppermute(array, 'ctx', [(j, j ^ mask) for j in range(ctx)])]
  transfers between devices with their start and end apart: 34 -> 35, of which waited for: 19 -> 18; matrix products, arithmetic and copies ran while one was open for 5% -> 4% of each run, Pallas kernels for 23% -> 23%
where the time goes in v3:
time: 658 us; the launch traced here: 653 us
  waiting for transfers between devices  268 us (41%)
  Pallas kernels  168 us (26%)
  blocking collectives  109 us (17%)
  starting transfers between devices  50 us (8%)
  other arithmetic  22.2 us (3%)
  local copies, waits for them, and re-layouts  21.4 us (3%)
  between operations  14.8 us (2%)
    all_gather x4, waiting for transfers between devices, gather(): return lax.all_gather(array, 'ctx', axis=0, tiled=False)  122 us
    all_to_all x3, blocking collectives, exchange(): lax.all_to_all(packed, 'ctx', split_axis=0, concat_axis=0, tiled=True)  109 us
    ppermute x18, waiting for transfers between devices, flip(): return lax.ppermute(array, 'ctx', [(j, j ^ mask) for j in range(ctx)])  89.4 us
    pallas_call x1, Pallas kernels, orthogonal(): pl.pallas_call(functools.partial(ns_kernel, own, len(parts)), out_shape=j...  37 us
    all_to_all x4, waiting for transfers between devices, exchange(): lax.all_to_all(packed, 'ctx', split_axis=0, concat_axis=0, tiled=True)  21.4 us
    ppermute x1, waiting for transfers between devices, body(): pack_other = lax.ppermute(pack, 'dp', [(0, 1), (1, 0)])  20.2 us
    ppermute x18, starting transfers between devices, flip(): return lax.ppermute(array, 'ctx', [(j, j ^ mask) for j in range(ctx)])  18.1 us
    pallas_call x2, Pallas kernels, mlp_backward(): pl.pallas_call(mlp_bwd_kernel, grid=(steps,), in_specs=[pl.BlockSpec((row...  17.3 us
  transfers between devices with their start and end apart: 35, of which 18 were waited for; matrix products, arithmetic and copies ran while one was open for 4% of the time, Pallas kernels for 23%

profile of v3, /device:TPU:0, one launch (start us, length us, event | category | flops | bytes accessed | tf_op | source)
XLA Modules:
  0.0 652.9 jit_solution(8532302634973210323)
XLA Ops:
  12.3 20.2 %collective-permute-done = bf16[592,768]{1,0:T(8,128)(2,1)S(1)} collective-permute-done((bf16[592,768]{1,0:T(8,128)(2,1)S(1)}, bf16[592,768]{1,0:T(8,128)(2,1)S(1)}, u32[]{:S(2)}, u32[]{:S(2)}) %collective-permute-start) | collective-permute-done | bytes 909344 | tf_op jit(solution)/shard_map/ppermute | solution.py:1067
  39.2 108.1 %all-gather.9.cloned.1.call-done = bf16[13824,768]{1,0:T(8,128)(2,1)} async-done(((bf16[864,768]{1,0:T(8,128)(2,1)}), bf16[13824,768]{1,0:T(8,128)(2,1)}) %all-gather.9.cloned.1.call-update) | async-done | bytes 21233680 | tf_op jit(solution)/shard_map/all_gather | solution.py:972
  156.4 7.9 %attn_forward.2 = (f32[1024,128]{1,0:T(8,128)}, bf16[1024,128]{1,0:T(8,128)(2,1)}, bf16[2,1024,1024]{2,1,0:T(8,128)(2,1)}) custom-call(s32[1024,1]{1,0:T(8,128)} %add.120.qpos_ref, s32[1,1024]{1,0:T(1,128)} %add.102.kpos_ref, bf16[1024,384]{1,0:T(8,128)(2,1)} %get-tuple-element.87.q_ref.k_ref.v_ref, bf16[1024,384]{1,0:T(8,128)(2,1)} %get-tuple-element.87.q_ref.k_ref.v_ref, ...), custom_call_target="tpu_custom_call" | custom-call | flops 8000000000 | bytes 8000000 | tf_op jit(solution)/shard_map/attn_forward/pallas_call | solution.py:246
  169.8 13.9 %all-to-all-done.o_ref = bf16[16,64,128]{2,1,0:T(8,128)(2,1)S(1)} async-done(((bf16[16,64,128]{2,1,0:T(8,128)(2,1)}), bf16[16,64,128]{2,1,0:T(8,128)(2,1)S(1)}, u32[]{:S(2)}, u32[]{:S(2)}) %all-to-all-start) | async-done | bytes 262176 | tf_op jit(solution)/shard_map/all_to_all | solution.py:968
  184.4 8.3 %mlp_forward.2 = (f32[128,768]{1,0:T(8,128)}, bf16[128,768]{1,0:T(8,128)(2,1)}, f32[128,3072]{1,0:T(8,128)}, f32[128,768]{1,0:T(8,128)}) custom-call(bf16[16,64,128]{2,1,0:T(8,128)(2,1)} %copy-done.21, bf16[128,768]{1,0:T(8,128)(2,1)} %bitcast.147, f32[12,768]{1,0:T(8,128)} %copy-done.18, bf16[16,864,768]{2,1,0:T(8,128)(2,1)} %bitcast.119, ...), custom_call_target="tpu_custom_call" | custom-call | flops 8000000000 | bytes 8000000 | tf_op jit(solution)/shard_map/mlp_forward/pallas_call | solution.py:355
  198.1 35.7 %all_to_all.35 = bf16[16,64,384]{2,1,0:T(8,128)(2,1)} all-to-all(bf16[16,64,384]{2,1,0:T(8,128)(2,1)} %get-tuple-element.90), channel_id=1, replica_groups=mesh['ctx'=16,'dp'=2] {'ctx'}, dimensions={0} | all-to-all | bytes 1572864 | tf_op jit(solution)/shard_map/all_to_all | solution.py:968
  233.9 7.9 %attn_forward.3 = (f32[1024,128]{1,0:T(8,128)}, bf16[1024,128]{1,0:T(8,128)(2,1)}, bf16[2,1024,1024]{2,1,0:T(8,128)(2,1)}) custom-call(s32[1024,1]{1,0:T(8,128)} %add.120.qpos_ref, s32[1,1024]{1,0:T(1,128)} %add.102.kpos_ref, bf16[1024,384]{1,0:T(8,128)(2,1)} %bitcast.154, bf16[1024,384]{1,0:T(8,128)(2,1)} %bitcast.155, bf16[1024,384]{1,0:T(8,128)(2,1)} %bitcast.156), custom_call_target="tpu_custom_call" | custom-call | flops 8000000000 | bytes 8000000 | tf_op jit(solution)/shard_map/attn_forward/pallas_call | solution.py:246
  245.4 14.2 %all-gather.11.cloned.1.call-done = bf16[11008,768]{1,0:T(8,128)(2,1)} async-done(((bf16[688,768]{1,0:T(8,128)(2,1)}), bf16[11008,768]{1,0:T(8,128)(2,1)}) %all-gather.11.cloned.1.call-update) | async-done | bytes 16908304 | tf_op jit(solution)/shard_map/all_gather | solution.py:972
  260.6 8.1 %mlp_forward.3 = (f32[128,768]{1,0:T(8,128)}, bf16[128,768]{1,0:T(8,128)(2,1)}, f32[128,3072]{1,0:T(8,128)}, f32[128,768]{1,0:T(8,128)}) custom-call(bf16[16,64,128]{2,1,0:T(8,128)(2,1)} %copy-done.20, f32[128,768]{1,0:T(8,128)} %get-tuple-element.89.x_ref, f32[12,768]{1,0:T(8,128)} %reshape.191.vec_ref, bf16[16,688,768]{2,1,0:T(8,128)(2,1)} %bitcast.128, ...), custom_call_target="tpu_custom_call" | custom-call | flops 8000000000 | bytes 8000000 | tf_op jit(solution)/shard_map/mlp_forward/pallas_call | solution.py:355
  268.7 8.6 %mlp_backward.2 = (bf16[128,768]{1,0:T(8,128)(2,1)}, f32[128,768]{1,0:T(8,128)}, bf16[128,768]{1,0:T(8,128)(2,1)}, bf16[16,64,128]{2,1,0:T(8,128)(2,1)}, f32[8,768]{1,0:T(8,128)}) custom-call(bf16[128,768]{1,0:T(8,128)(2,1)} %bitcast.152, f32[128,768]{1,0:T(8,128)} %get-tuple-element.96.mid_ref, f32[128,3072]{1,0:T(8,128)} %get-tuple-element.97.h_ref, ...), custom_call_target="tpu_custom_call" | custom-call | flops 8000000000 | bytes 8000000 | tf_op jit(solution)/shard_map/mlp_backward/pallas_call | solution.py:440
  279.5 37.2 %all_to_all.36 = bf16[16,64,128]{2,1,0:T(8,128)(2,1)} all-to-all(bf16[16,64,128]{2,1,0:T(8,128)(2,1)S(1)} %copy-done.32), channel_id=1, replica_groups=mesh['ctx'=16,'dp'=2] {'ctx'}, dimensions={0} | all-to-all | bytes 524288 | tf_op jit(solution)/shard_map/all_to_all | solution.py:968
  316.7 7.5 %attn_backward.2.pack_ref = bf16[1024,384]{1,0:T(8,128)(2,1)} custom-call(bf16[1024,384]{1,0:T(8,128)(2,1)} %bitcast.157, bf16[1024,128]{1,0:T(8,128)(2,1)} %bitcast.167, f32[1024,128]{1,0:T(8,128)} %get-tuple-element.102.of_ref, bf16[2,1024,1024]{2,1,0:T(8,128)(2,1)} %get-tuple-element.103.p_ref, bf16[1024,384]{1,0:T(8,128)(2,1)} %bitcast.158, ...), custom_call_target="tpu_custom_call" | custom-call | flops 8000000000 | bytes 8000000 | tf_op jit(solution)/shard_map/attn_backward/pallas_call | solution.py:305
  324.2 35.7 %all_to_all.37.d_ref = bf16[16,64,384]{2,1,0:T(8,128)(2,1)} all-to-all(bf16[16,64,384]{2,1,0:T(8,128)(2,1)} %bitcast.142), channel_id=1, replica_groups=mesh['ctx'=16,'dp'=2] {'ctx'}, dimensions={0} | all-to-all | bytes 1572864 | tf_op jit(solution)/shard_map/all_to_all | solution.py:968
  365.3 8.7 %mlp_backward.3 = (bf16[128,768]{1,0:T(8,128)(2,1)}, f32[128,768]{1,0:T(8,128)}, bf16[128,768]{1,0:T(8,128)(2,1)}, bf16[16,64,128]{2,1,0:T(8,128)(2,1)}, f32[8,768]{1,0:T(8,128)}) custom-call(f32[128,768]{1,0:T(8,128)} %get-tuple-element.105.gr_ref, f32[128,768]{1,0:T(8,128)} %get-tuple-element.106.mid_ref, f32[128,3072]{1,0:T(8,128)} %get-tuple-element.107.h_ref, ...), custom_call_target="tpu_custom_call" | custom-call | flops 8000000000 | bytes 8000000 | tf_op jit(solution)/shard_map/mlp_backward/pallas_call | solution.py:440
  388.0 13.3 %collective-permute-done.2 = bf16[128,768]{1,0:T(8,128)(2,1)S(1)} collective-permute-done((bf16[128,768]{1,0:T(8,128)(2,1)}, bf16[128,768]{1,0:T(8,128)(2,1)S(1)}, u32[]{:S(2)}, u32[]{:S(2)}) %collective-permute-start.2) | collective-permute-done | bytes 196640 | tf_op jit(solution)/shard_map/ppermute | solution.py:976
  410.5 7.4 %attn_backward.3.pack_ref = bf16[1024,384]{1,0:T(8,128)(2,1)} custom-call(bf16[1024,384]{1,0:T(8,128)(2,1)} %get-tuple-element.87.q_ref.k_ref.v_ref, bf16[1024,128]{1,0:T(8,128)(2,1)} %bitcast.166, f32[1024,128]{1,0:T(8,128)} %get-tuple-element.109.of_ref, bf16[2,1024,1024]{2,1,0:T(8,128)(2,1)} %get-tuple-element.110.p_ref, ...), custom_call_target="tpu_custom_call" | custom-call | flops 8000000000 | bytes 8000000 | tf_op jit(solution)/shard_map/attn_backward/pallas_call | solution.py:305
  436.7 15.5 %collective-permute-done.4.refs_1_ = bf16[512,768]{1,0:T(8,128)(2,1)} collective-permute-done((bf16[512,768]{1,0:T(8,128)(2,1)S(1)}, bf16[512,768]{1,0:T(8,128)(2,1)}, u32[]{:S(2)}, u32[]{:S(2)}) %collective-permute-start.4) | collective-permute-done | bytes 786464 | tf_op jit(solution)/shard_map/ppermute | solution.py:976
  473.7 7.5 %hidden_grads.1 = (f32[192,768]{1,0:T(8,128)}, f32[192,768]{1,0:T(8,128)}) custom-call(bf16[16,704,768]{2,1,0:T(8,128)(2,1)} %bitcast.139, bf16[16,688,768]{2,1,0:T(8,128)(2,1)} %bitcast.134, bf16[192,768]{1,0:T(8,128)(2,1)} %get-tuple-element.183.fc_ref, bf16[192,768]{1,0:T(8,128)(2,1)} %get-tuple-element.182.red_ref, f32[192,1]{1,0:T(8,128)} %copy.34.bias_ref), custom_call_target="tpu_custom_call" | custom-call | flops 1000000000 | bytes 1000000 | tf_op jit(solution)/shard_map/hidden_grads/pallas_call | solution.py:570
  489.8 10.0 %collective-permute-done.9 = bf16[64,768]{1,0:T(8,128)(2,1)S(1)} collective-permute-done((bf16[64,768]{1,0:T(8,128)(2,1)S(1)}, bf16[64,768]{1,0:T(8,128)(2,1)S(1)}, u32[]{:S(2)}, u32[]{:S(2)}) %collective-permute-start.9) | collective-permute-done | bytes 98336 | tf_op jit(solution)/shard_map/ppermute | solution.py:1199
  518.8 9.5 %collective-permute-done.11 = bf16[192,768]{1,0:T(8,128)(2,1)S(1)} collective-permute-done((bf16[192,768]{1,0:T(8,128)(2,1)S(1)}, bf16[192,768]{1,0:T(8,128)(2,1)S(1)}, u32[]{:S(2)}, u32[]{:S(2)}) %collective-permute-start.11) | collective-permute-done | bytes 294944 | tf_op jit(solution)/shard_map/ppermute | solution.py:976
  530.2 18.7 %collective-permute-done.15.refs_3_ = bf16[3,192,768]{2,1,0:T(8,128)(2,1)S(1)} collective-permute-done((bf16[3,192,768]{2,1,0:T(8,128)(2,1)S(1)}, bf16[3,192,768]{2,1,0:T(8,128)(2,1)S(1)}, u32[]{:S(2)}, u32[]{:S(2)}) %collective-permute-start.15) | collective-permute-done | bytes 884768 | tf_op jit(solution)/shard_map/ppermute | solution.py:976
  552.3 7.7 %sum_heads.1 = (bf16[2304,768]{1,0:T(8,128)(2,1)}, bf16[4,144,768]{2,1,0:T(8,128)(2,1)}) custom-call(s32[1]{0:T(128)} %bitcast.41.role_ref, s32[1]{0:T(128)} %bitcast.51.near_ref, bf16[192,768]{1,0:T(8,128)(2,1)} %copy-done.19, bf16[3,192,768]{2,1,0:T(8,128)(2,1)} %copy-done.2, bf16[192,768]{1,0:T(8,128)(2,1)} %collective-permute-done.13.refs_2_, ...), custom_call_target="tpu_custom_call" | custom-call | flops 4000000000 | bytes 4000000 | tf_op jit(solution)/shard_map/sum_heads/pallas_call | solution.py:945
  569.5 37.0 %newton_schulz.1 = bf16[768,768]{1,0:T(8,128)(2,1)} custom-call(s32[1]{0:T(128)} %bitcast.41.role_ref, bf16[192,768]{1,0:T(8,128)(2,1)} %copy-done.19, bf16[576,768]{1,0:T(8,128)(2,1)} %bitcast.141, bf16[192,768]{1,0:T(8,128)(2,1)} %collective-permute-done.13.refs_2_, bf16[576,768]{1,0:T(8,128)(2,1)} %bitcast.151, ...), custom_call_target="tpu_custom_call" | custom-call | flops 46000001024 | bytes 46000000 | tf_op jit(solution)/shard_map/newton_schulz/pallas_call | solution.py:854
  628.0 14.5 %collective-permute-done.23 = bf16[192,768]{1,0:T(8,128)(2,1)S(1)} collective-permute-done((bf16[192,768]{1,0:T(8,128)(2,1)S(1)}, bf16[192,768]{1,0:T(8,128)(2,1)S(1)}, u32[]{:S(2)}, u32[]{:S(2)}) %collective-permute-start.23) | collective-permute-done | bytes 294944 | tf_op jit(solution)/shard_map/ppermute | solution.py:976
  (244 shorter events, 174.9 us)
Async XLA Ops:
  7.2 140.0 %all-gather.9.cloned.1.call-start = ((), (), s32[]{:S(2)}) async-start(), calls=%async_computation.9 | async-start | bytes 22560768 | tf_op jit(solution)/shard_map/all_gather | solution.py:972
  9.3 23.2 %collective-permute-start = (bf16[592,768]{1,0:T(8,128)(2,1)S(1)}, bf16[592,768]{1,0:T(8,128)(2,1)S(1)}, u32[]{:S(2)}, u32[]{:S(2)}) collective-permute-start(bf16[592,768]{1,0:T(8,128)(2,1)S(1)} %constant_dynamic-update-slice_fusion), channel_id=1, source_target_pairs={{0,1},{1,0},{2,3},{3,2},{4,5},{5,4},{6,7},{7,6},{8,9},{9,8},{10,11... | collective-permute-start | bytes 2727944 | tf_op jit(solution)/shard_map/ppermute | solution.py:1067
  35.6 224.1 %all-gather.11.cloned.1.call-start = ((), (), s32[]{:S(2)}) async-start(), calls=%async_computation.10 | async-start | bytes 17965056 | tf_op jit(solution)/shard_map/all_gather | solution.py:972
  164.3 19.3 %all-to-all-start = ((bf16[16,64,128]{2,1,0:T(8,128)(2,1)}), bf16[16,64,128]{2,1,0:T(8,128)(2,1)S(1)}, u32[]{:S(2)}, u32[]{:S(2)}) async-start(bf16[16,64,128]{2,1,0:T(8,128)(2,1)} %bitcast.165), calls=%async_computation | async-start | bytes 524288 | tf_op jit(solution)/shard_map/all_to_all | solution.py:968
  245.3 185.9 %all-gather.13.cloned.1.call-start = ((), (), s32[]{:S(2)}) async-start(), calls=%async_computation.11 | async-start | bytes 18382848 | tf_op jit(solution)/shard_map/all_gather | solution.py:972
  279.5 204.9 %all-gather.15.cloned.1.call-start = ((), (), s32[]{:S(2)}) async-start(), calls=%async_computation.12 | async-start | bytes 3342336 | tf_op jit(solution)/shard_map/all_gather | solution.py:972
  374.1 27.3 %collective-permute-start.2 = (bf16[128,768]{1,0:T(8,128)(2,1)}, bf16[128,768]{1,0:T(8,128)(2,1)S(1)}, u32[]{:S(2)}, u32[]{:S(2)}) collective-permute-start(bf16[128,768]{1,0:T(8,128)(2,1)} %get-tuple-element.111), channel_id=1, source_target_pairs={{0,16},{2,18},{4,20},{6,22},{8,24},{10,26},{12,28},{14,30},{16,0},... | collective-permute-start | bytes 589832 | tf_op jit(solution)/shard_map/ppermute | solution.py:976
  374.4 27.0 %collective-permute-start.3 = (bf16[128,768]{1,0:T(8,128)(2,1)}, bf16[128,768]{1,0:T(8,128)(2,1)S(1)}, u32[]{:S(2)}, u32[]{:S(2)}) collective-permute-start(bf16[128,768]{1,0:T(8,128)(2,1)} %get-tuple-element.111), channel_id=1, source_target_pairs={{0,8},{2,10},{4,12},{6,14},{8,0},{10,2},{12,4},{14,6},{16,24},{18,... | collective-permute-start | bytes 589832 | tf_op jit(solution)/shard_map/ppermute | solution.py:976
  378.5 31.3 %all-to-all-start.5 = ((bf16[16,64,128]{2,1,0:T(8,128)(2,1)}), bf16[16,64,128]{2,1,0:T(8,128)(2,1)S(1)}, u32[]{:S(2)}, u32[]{:S(2)}) async-start(bf16[16,64,128]{2,1,0:T(8,128)(2,1)} %get-tuple-element.108), calls=%async_computation.5 | async-start | bytes 524288 | tf_op jit(solution)/shard_map/all_to_all | solution.py:968
  417.9 34.3 %all-to-all-start.6 = ((bf16[16,64,384]{2,1,0:T(8,128)(2,1)}), bf16[16,64,384]{2,1,0:T(8,128)(2,1)S(1)}, u32[]{:S(2)}, u32[]{:S(2)}) async-start(bf16[16,64,384]{2,1,0:T(8,128)(2,1)} %bitcast.146), calls=%async_computation.6 | async-start | bytes 1572864 | tf_op jit(solution)/shard_map/all_to_all | solution.py:968
  421.5 189.4 %reduce-scatter.2.cloned.1.call-start = ((), (), s32[]{:S(2)}) async-start(), calls=%async_computation.8 | async-start | bytes 417792 | tf_op jit(solution)/shard_map/reduce_scatter | solution.py:1241
  421.6 30.6 %collective-permute-start.4 = (bf16[512,768]{1,0:T(8,128)(2,1)S(1)}, bf16[512,768]{1,0:T(8,128)(2,1)}, u32[]{:S(2)}, u32[]{:S(2)}) collective-permute-start(bf16[512,768]{1,0:T(8,128)(2,1)S(1)} %bitcast.143), channel_id=1, source_target_pairs={{0,4},{2,6},{4,0},{6,2},{8,12},{10,14},{12,8},{14,10},{16,20},{18,... | collective-permute-start | bytes 2359304 | tf_op jit(solution)/shard_map/ppermute | solution.py:976
  423.6 28.6 %collective-permute-start.5 = (bf16[512,768]{1,0:T(8,128)(2,1)S(1)}, bf16[512,768]{1,0:T(8,128)(2,1)S(1)}, u32[]{:S(2)}, u32[]{:S(2)}) collective-permute-start(bf16[512,768]{1,0:T(8,128)(2,1)S(1)} %bitcast.144), channel_id=1, source_target_pairs={{0,2},{2,0},{4,6},{6,4},{8,10},{10,8},{12,14},{14,12},{16,18},{18,... | collective-permute-start | bytes 2359304 | tf_op jit(solution)/shard_map/ppermute | solution.py:976
  503.0 25.3 %collective-permute-start.13 = (bf16[192,768]{1,0:T(8,128)(2,1)S(1)}, bf16[192,768]{1,0:T(8,128)(2,1)}, u32[]{:S(2)}, u32[]{:S(2)}) collective-permute-start(bf16[192,768]{1,0:T(8,128)(2,1)S(1)} %get-tuple-element.146.refs_0_), channel_id=1, source_target_pairs={{0,4},{2,6},{4,0},{6,2},{8,12},{10,14},{12,8},{14,10},{16,20},{18,... | collective-permute-start | bytes 884744 | tf_op jit(solution)/shard_map/ppermute | solution.py:976
  503.5 24.8 %collective-permute-start.14 = (bf16[192,768]{1,0:T(8,128)(2,1)S(1)}, bf16[192,768]{1,0:T(8,128)(2,1)}, u32[]{:S(2)}, u32[]{:S(2)}) collective-permute-start(bf16[192,768]{1,0:T(8,128)(2,1)S(1)} %get-tuple-element.146.refs_0_), channel_id=1, source_target_pairs={{0,2},{2,0},{4,6},{6,4},{8,10},{10,8},{12,14},{14,12},{16,18},{18,... | collective-permute-start | bytes 884744 | tf_op jit(solution)/shard_map/ppermute | solution.py:976
  504.9 23.4 %collective-permute-start.11 = (bf16[192,768]{1,0:T(8,128)(2,1)S(1)}, bf16[192,768]{1,0:T(8,128)(2,1)S(1)}, u32[]{:S(2)}, u32[]{:S(2)}) collective-permute-start(bf16[192,768]{1,0:T(8,128)(2,1)S(1)} %get-tuple-element.179), channel_id=1, source_target_pairs={{0,16},{2,18},{4,20},{6,22},{8,24},{10,26},{12,28},{14,30},{16,0},... | collective-permute-start | bytes 884744 | tf_op jit(solution)/shard_map/ppermute | solution.py:976
  507.3 21.0 %collective-permute-start.12 = (bf16[192,768]{1,0:T(8,128)(2,1)S(1)}, bf16[192,768]{1,0:T(8,128)(2,1)S(1)}, u32[]{:S(2)}, u32[]{:S(2)}) collective-permute-start(bf16[192,768]{1,0:T(8,128)(2,1)S(1)} %get-tuple-element.168), channel_id=1, source_target_pairs={{0,24},{2,26},{4,28},{6,30},{8,16},{10,18},{12,20},{14,22},{16,8},... | collective-permute-start | bytes 884744 | tf_op jit(solution)/shard_map/ppermute | solution.py:976
  528.4 20.4 %collective-permute-start.15 = (bf16[3,192,768]{2,1,0:T(8,128)(2,1)S(1)}, bf16[3,192,768]{2,1,0:T(8,128)(2,1)S(1)}, u32[]{:S(2)}, u32[]{:S(2)}) collective-permute-start(bf16[3,192,768]{2,1,0:T(8,128)(2,1)S(1)} %pad_maximum_fusion.2.refs_1_), channel_id=1, source_target_pairs={{0,4},{2,6},{4,0},{6,2},{8,12},{10,14},{12,8},{14,10},{16,20},{18,... | collective-permute-start | bytes 2654216 | tf_op jit(solution)/shard_map/ppermute | solution.py:976
  530.2 21.4 %collective-permute-start.16 = (bf16[3,192,768]{2,1,0:T(8,128)(2,1)S(1)}, bf16[3,192,768]{2,1,0:T(8,128)(2,1)}, u32[]{:S(2)}, u32[]{:S(2)}) collective-permute-start(bf16[3,192,768]{2,1,0:T(8,128)(2,1)S(1)} %pad_maximum_fusion.2.refs_1_), channel_id=1, source_target_pairs={{0,2},{2,0},{4,6},{6,4},{8,10},{10,8},{12,14},{14,12},{16,18},{18,... | collective-permute-start | bytes 2654216 | tf_op jit(solution)/shard_map/ppermute | solution.py:976
  561.3 49.7 %collective-permute-start.19 = (bf16[144,768]{1,0:T(8,128)(2,1)S(1)}, bf16[144,768]{1,0:T(8,128)(2,1)S(1)}, u32[]{:S(2)}, u32[]{:S(2)}) collective-permute-start(bf16[144,768]{1,0:T(8,128)(2,1)S(1)} %get-tuple-element.189), channel_id=1, source_target_pairs={{0,8},{2,10},{4,12},{6,14},{24,16},{26,18},{28,20},{30,22},{1,9},{... | collective-permute-start | bytes 663560 | tf_op jit(solution)/shard_map/ppermute | solution.py:1299
  563.8 47.1 %collective-permute-start.20 = (bf16[144,768]{1,0:T(8,128)(2,1)S(1)}, bf16[144,768]{1,0:T(8,128)(2,1)S(1)}, u32[]{:S(2)}, u32[]{:S(2)}) collective-permute-start(bf16[144,768]{1,0:T(8,128)(2,1)S(1)} %get-tuple-element.188), channel_id=1, source_target_pairs={{0,16},{2,18},{4,20},{6,22},{24,8},{26,10},{28,12},{30,14},{1,17},... | collective-permute-start | bytes 663560 | tf_op jit(solution)/shard_map/ppermute | solution.py:1299
  566.1 44.9 %collective-permute-start.21 = (bf16[144,768]{1,0:T(8,128)(2,1)S(1)}, bf16[144,768]{1,0:T(8,128)(2,1)S(1)}, u32[]{:S(2)}, u32[]{:S(2)}) collective-permute-start(bf16[144,768]{1,0:T(8,128)(2,1)S(1)} %get-tuple-element.187), channel_id=1, source_target_pairs={{0,24},{2,26},{4,28},{6,30},{24,0},{26,2},{28,4},{30,6},{1,25},{3,... | collective-permute-start | bytes 663560 | tf_op jit(solution)/shard_map/ppermute | solution.py:1299
  618.6 24.0 %collective-permute-start.23 = (bf16[192,768]{1,0:T(8,128)(2,1)S(1)}, bf16[192,768]{1,0:T(8,128)(2,1)S(1)}, u32[]{:S(2)}, u32[]{:S(2)}) collective-permute-start(bf16[192,768]{1,0:T(8,128)(2,1)S(1)} %get-tuple-element.177), channel_id=1, source_target_pairs={{0,16},{2,18},{4,20},{6,22},{8,24},{10,26},{12,28},{14,30},{16,0},... | collective-permute-start | bytes 884744 | tf_op jit(solution)/shard_map/ppermute | solution.py:976
  619.1 23.4 %collective-permute-start.24 = (bf16[192,768]{1,0:T(8,128)(2,1)S(1)}, bf16[192,768]{1,0:T(8,128)(2,1)S(1)}, u32[]{:S(2)}, u32[]{:S(2)}) collective-permute-start(bf16[192,768]{1,0:T(8,128)(2,1)S(1)} %get-tuple-element.175), channel_id=1, source_target_pairs={{0,8},{2,10},{4,12},{6,14},{8,0},{10,2},{12,4},{14,6},{16,24},{18,... | collective-permute-start | bytes 884744 | tf_op jit(solution)/shard_map/ppermute | solution.py:976
  (57 other events, 428.5 us)
Sparse Core Ops, SparseCore 0:
  35.7 111.5 all-gather.8
  148.8 110.7 all-gather.10
  279.6 134.9 all-gather.12
  416.7 55.5 all-gather.14
  550.6 60.2 reduce-scatter.1

commit v4 on v3

--- a/solution.py
+++ b/solution.py
@@ -728,8 +728,9 @@
 
 
 def ns_kernel(own, parts_count, role_ref, *refs):
-    parts, (sums_ref, out_ref) = refs[:parts_count], refs[parts_count : parts_count + 2]
-    y_ref, full_ref, low_ref, gram_ref, poly_ref, sems = refs[parts_count + 2 :]
+    parts, sums_ref = refs[:parts_count], refs[parts_count]
+    out_refs = refs[parts_count + 1 : parts_count + 5]
+    y_ref, full_ref, low_ref, gram_ref, poly_ref, sems = refs[parts_count + 5 :]
     length, side = y_ref.shape
     own_in, own_ff, own_mix = own
     tile = 256
@@ -844,7 +845,7 @@
                     piece = jnp.concatenate(
                         [piece, jnp.zeros((own_ff - size, side), bf16)], axis=0
                     )
-                out_ref[k * own_ff : (k + 1) * own_ff, :] = piece
+                out_refs[k][...] = piece
 
 
 def orthogonal(role, columns, sums, own):
@@ -853,10 +854,10 @@
     length = sum(part.shape[0] for part in parts)
     return pl.pallas_call(
         functools.partial(ns_kernel, own, len(parts)),
-        out_shape=jax.ShapeDtypeStruct((4 * own[1], width), bf16),
+        out_shape=[jax.ShapeDtypeStruct((own[1], width), bf16)] * 4,
         in_specs=[pl.BlockSpec(memory_space=pltpu.SMEM)]
         + [pl.BlockSpec(memory_space=pl.ANY)] * (len(parts) + 1),
-        out_specs=pl.BlockSpec(memory_space=pltpu.VMEM),
+        out_specs=[pl.BlockSpec(memory_space=pltpu.VMEM)] * 4,
         scratch_shapes=[
             pltpu.VMEM((length, width), bf16),
             pltpu.VMEM((width, length), f32),
@@ -876,10 +877,10 @@
 
 
 def sum_heads_kernel(own_mix, old_at, role_ref, near_ref, *refs):
-    parts, (acts_ref, y_out_ref, fresh_ref) = refs[:8], refs[8:11]
-    held_ref, old_ref, y_ref, natural_ref, turned_ref, sems = refs[11:]
+    parts, (acts_ref, y_out_ref), fresh_refs = refs[:8], refs[8:10], refs[10:14]
+    held_ref, old_ref, y_ref, natural_ref, turned_ref, sems = refs[14:]
     width = held_ref.shape[3]
-    own_in = fresh_ref.shape[1]
+    own_in = fresh_refs[0].shape[0]
     hd = width // HEADS
     block = 16
     place = [column_place(near_ref[0] ^ n) for n in range(4)]
@@ -907,7 +908,8 @@
                     y_ref[pl.ds((place[n] * 4 + z) * own_in + start, block), :] = (
                         muon_moment * old.astype(f32) + source.astype(f32)
                     ).astype(bf16)
-        fresh_ref[...] = natural_ref[0]
+        for k in range(4):
+            fresh_refs[k][...] = natural_ref[0, k]
         copy_all([(y_ref, y_out_ref)], sems)
 
     @pl.when(role_ref[0] == 3)
@@ -918,7 +920,6 @@
                 place[h & 3], 3 ^ (h >> 2), :hd
             ].astype(f32)
         turned_ref[...] = turned_ref[...].T
-        fresh_ref[...] = jnp.zeros_like(fresh_ref)
         for z in range(4):
             for n in range(4):
                 first = (4 * z + n) * own_mix
@@ -928,12 +929,15 @@
                 y_ref[pl.ds((place[n] * 4 + (3 ^ z)) * own_mix, own_mix), :] = (
                     muon_moment * old.astype(f32) + source
                 ).astype(bf16)
-        fresh_ref[:, :own_mix] = natural_ref[0, :, :own_mix]
+        for k in range(4):
+            fresh_refs[k][...] = jnp.zeros_like(fresh_refs[k])
+            fresh_refs[k][:own_mix, :] = natural_ref[0, k, :own_mix]
         copy_all([(y_ref.at[:width], y_out_ref.at[:width])], sems)
 
     @pl.when((role_ref[0] == 1) | (role_ref[0] == 2))
     def _():
-        fresh_ref[...] = jnp.zeros_like(fresh_ref)
+        for k in range(4):
+            fresh_refs[k][...] = jnp.zeros_like(fresh_refs[k])
 
 
 def sum_heads(role, near, columns, acts, old_at, own_in, own_mix):
@@ -946,10 +950,10 @@
         functools.partial(sum_heads_kernel, own_mix, old_at),
         out_shape=[
             jax.ShapeDtypeStruct((ctx * own_in, width), bf16),
-            jax.ShapeDtypeStruct((4, own_in, width), bf16),
-        ],
+        ]
+        + [jax.ShapeDtypeStruct((own_in, width), bf16)] * 4,
         in_specs=[smem, smem] + [hbm] * 9,
-        out_specs=[hbm, pl.BlockSpec(memory_space=pltpu.VMEM)],
+        out_specs=[hbm] + [pl.BlockSpec(memory_space=pltpu.VMEM)] * 4,
         scratch_shapes=[
             pltpu.VMEM((4, 4, size, width), bf16),
             pltpu.VMEM((ctx, own_in, width), bf16),
@@ -1194,8 +1198,8 @@
     ]
     gz_columns, g_head = lax.optimization_barrier((gz_columns, g_head))
 
-    def owned(first, second):
-        given = jnp.where(owner_first, second, first).astype(bf16)
+    def owned(first, second, sent_as=bf16):
+        given = jnp.where(owner_first, second, first).astype(sent_as)
         taken = lax.ppermute(given, "dp", [(0, 1), (1, 0)]).astype(f32)
         return jnp.where(owner_first, first, second) + taken
 
@@ -1219,10 +1223,6 @@
     gin, vg_early = qkv_backward(dqkv_own, x, gmid, vecs[0], all_first, in_at[0], own_in)
     vec_grads[0] = jnp.concatenate([vg_early[:4], vg_late], axis=0)
     input_grad = gin.reshape(seqs, local, width)
-    vec_terms = jnp.stack(vec_grads).reshape(layers, ctx, own_vec).swapaxes(0, 1)
-    vec_terms = jnp.pad(vec_terms, ((0, 0), (0, 8 - layers), (0, width - own_vec)))
-    m_fc = moved[:own_ff].T
-    m_red = moved[own_ff:]
 
     big = max(own_ff, 3 * hd)
 
@@ -1231,13 +1231,15 @@
 
     g_mix_first = head_grads(saved[0][4], gy_all, 0, rows)
     g_mix_head = owned(g_mix_first, g_head[2])
-    pieces = (g_in_head, padded(moved[:own_ff]), padded(m_red), padded(g_mix_head))
+    pieces = (g_in_head, padded(moved[:own_ff]), padded(moved[own_ff:]), padded(g_mix_head))
 
     def piece_for(z):
         low = jnp.where(z == 0, pieces[0], pieces[1])
         return jnp.where(z < 2, low, jnp.where(z == 2, pieces[2], pieces[3]))
 
-    started, vec_terms = lax.optimization_barrier((gather_start(piece_for, role, ctx), vec_terms))
+    started, vec_grads = lax.optimization_barrier((gather_start(piece_for, role, ctx), vec_grads))
+    vec_terms = owned(vec_grads[0], vec_grads[1], f32).reshape(ctx, 1, own_vec)
+    vec_terms = jnp.pad(vec_terms, ((0, 0), (0, 7), (0, width - own_vec)))
     vec_sums = lax.psum_scatter(vec_terms, "ctx", scatter_dimension=0)
     columns = gather_finish(started, ctx)
 
@@ -1275,7 +1277,7 @@
 
     old_at = at_acts["old_in"]
     if ctx == 16 and own_in % 16 == 0 and own_mix % 16 == 0:
-        sums, fresh = sum_heads(role[None], near[None], columns, acts, old_at, own_in, own_mix)
+        sums, *fresh = sum_heads(role[None], near[None], columns, acts, old_at, own_in, own_mix)
     else:
         old = acts[:, old_at : old_at + own_in + own_mix].astype(f32)
 
@@ -1303,13 +1305,12 @@
         sums,
         (own_in, own_ff, own_mix),
     )
-    direction, taken, vec_sums = lax.optimization_barrier((direction, taken, vec_sums))
-    vec_sums = vec_sums[:layers, :own_vec]
-    vec_given = jnp.where(owner_first, vec_sums[1], vec_sums[0])
-    vec_kept = jnp.where(owner_first, vec_sums[0], vec_sums[1])
-    vec_grad = (vec_kept + lax.ppermute(vec_given, "dp", [(0, 1), (1, 0)]))[None]
-    direction = direction.reshape(4, own_ff, width)
+    direction, taken, moved = lax.optimization_barrier((direction, taken, moved))
+    m_fc = moved[:own_ff].T
+    m_red = moved[own_ff:]
     by_distance = [direction[0]] + [flip(direction[k], 4 * k, ctx) for k in (1, 2, 3)]
+    by_distance[1], vec_sums = lax.optimization_barrier((by_distance[1], vec_sums))
+    vec_grad = vec_sums[:1, :own_vec]
 
     def from_role(by_distance, wanted):
         result = by_distance[wanted]

time: 658 us -> 655 us (level)
    ppermute x3 -> x4, waiting for transfers between devices: 10 us -> 14 us  [owned(): taken = lax.ppermute(given, 'dp', [(0, 1), (1, 0)]).astype(f32)]
  transfers between devices with their start and end apart: 35 -> 35, of which waited for: 18 -> 17; matrix products, arithmetic and copies ran while one was open for 4% -> 4% of each run, Pallas kernels for 23% -> 23%
where the time goes in v4:
time: 655 us; the launch traced here: 650 us
  waiting for transfers between devices  266 us (41%)
  Pallas kernels  168 us (26%)
  blocking collectives  109 us (17%)
  starting transfers between devices  51.3 us (8%)
  other arithmetic  21.9 us (3%)
  local copies, waits for them, and re-layouts  19.2 us (3%)
  between operations  14.8 us (2%)
    all_gather x4, waiting for transfers between devices, gather(): return lax.all_gather(array, 'ctx', axis=0, tiled=False)  122 us
    all_to_all x3, blocking collectives, exchange(): lax.all_to_all(packed, 'ctx', split_axis=0, concat_axis=0, tiled=True)  109 us
    ppermute x18, waiting for transfers between devices, flip(): return lax.ppermute(array, 'ctx', [(j, j ^ mask) for j in range(ctx)])  87.9 us
    pallas_call x1, Pallas kernels, orthogonal(): pl.pallas_call(functools.partial(ns_kernel, own, len(parts)), out_shape=[...  37 us
    all_to_all x4, waiting for transfers between devices, exchange(): lax.all_to_all(packed, 'ctx', split_axis=0, concat_axis=0, tiled=True)  21.4 us
    ppermute x18, starting transfers between devices, flip(): return lax.ppermute(array, 'ctx', [(j, j ^ mask) for j in range(ctx)])  20.4 us
    ppermute x1, waiting for transfers between devices, body(): pack_other = lax.ppermute(pack, 'dp', [(0, 1), (1, 0)])  20.2 us
    pallas_call x2, Pallas kernels, mlp_backward(): pl.pallas_call(mlp_bwd_kernel, grid=(steps,), in_specs=[pl.BlockSpec((row...  17.3 us
  transfers between devices with their start and end apart: 35, of which 17 were waited for; matrix products, arithmetic and copies ran while one was open for 4% of the time, Pallas kernels for 23%

profile of v4, /device:TPU:0, one launch (start us, length us, event | category | flops | bytes accessed | tf_op | source)
XLA Modules:
  0.0 649.7 jit_solution(16095795588939499418)
XLA Ops:
  12.3 20.2 %collective-permute-done = bf16[592,768]{1,0:T(8,128)(2,1)S(1)} collective-permute-done((bf16[592,768]{1,0:T(8,128)(2,1)S(1)}, bf16[592,768]{1,0:T(8,128)(2,1)S(1)}, u32[]{:S(2)}, u32[]{:S(2)}) %collective-permute-start) | collective-permute-done | bytes 909344 | tf_op jit(solution)/shard_map/ppermute | solution.py:1071
  39.2 108.1 %all-gather.9.cloned.1.call-done = bf16[13824,768]{1,0:T(8,128)(2,1)} async-done(((bf16[864,768]{1,0:T(8,128)(2,1)}), bf16[13824,768]{1,0:T(8,128)(2,1)}) %all-gather.9.cloned.1.call-update) | async-done | bytes 21233680 | tf_op jit(solution)/shard_map/all_gather | solution.py:976
  156.4 7.9 %attn_forward.2 = (f32[1024,128]{1,0:T(8,128)}, bf16[1024,128]{1,0:T(8,128)(2,1)}, bf16[2,1024,1024]{2,1,0:T(8,128)(2,1)}) custom-call(s32[1024,1]{1,0:T(8,128)} %add.120.qpos_ref, s32[1,1024]{1,0:T(1,128)} %add.102.kpos_ref, bf16[1024,384]{1,0:T(8,128)(2,1)} %get-tuple-element.100.q_ref.k_ref.v_ref, bf16[1024,384]{1,0:T(8,128)(2,1)} %get-tuple-element.100.q_ref.k_ref.v_ref, ...), custom_call_target="tpu_custom_call" | custom-call | flops 8000000000 | bytes 8000000 | tf_op jit(solution)/shard_map/attn_forward/pallas_call | solution.py:246
  169.8 13.9 %all-to-all-done.o_ref = bf16[16,64,128]{2,1,0:T(8,128)(2,1)S(1)} async-done(((bf16[16,64,128]{2,1,0:T(8,128)(2,1)}), bf16[16,64,128]{2,1,0:T(8,128)(2,1)S(1)}, u32[]{:S(2)}, u32[]{:S(2)}) %all-to-all-start) | async-done | bytes 262176 | tf_op jit(solution)/shard_map/all_to_all | solution.py:972
  184.4 8.3 %mlp_forward.2 = (f32[128,768]{1,0:T(8,128)}, bf16[128,768]{1,0:T(8,128)(2,1)}, f32[128,3072]{1,0:T(8,128)}, f32[128,768]{1,0:T(8,128)}) custom-call(bf16[16,64,128]{2,1,0:T(8,128)(2,1)} %copy-done.22, bf16[128,768]{1,0:T(8,128)(2,1)} %bitcast.137, f32[12,768]{1,0:T(8,128)} %copy-done.19, bf16[16,864,768]{2,1,0:T(8,128)(2,1)} %bitcast.109, ...), custom_call_target="tpu_custom_call" | custom-call | flops 8000000000 | bytes 8000000 | tf_op jit(solution)/shard_map/mlp_forward/pallas_call | solution.py:355
  198.2 35.7 %all_to_all.35 = bf16[16,64,384]{2,1,0:T(8,128)(2,1)} all-to-all(bf16[16,64,384]{2,1,0:T(8,128)(2,1)} %get-tuple-element.103), channel_id=1, replica_groups=mesh['ctx'=16,'dp'=2] {'ctx'}, dimensions={0} | all-to-all | bytes 1572864 | tf_op jit(solution)/shard_map/all_to_all | solution.py:972
  233.9 7.9 %attn_forward.3 = (f32[1024,128]{1,0:T(8,128)}, bf16[1024,128]{1,0:T(8,128)(2,1)}, bf16[2,1024,1024]{2,1,0:T(8,128)(2,1)}) custom-call(s32[1024,1]{1,0:T(8,128)} %add.120.qpos_ref, s32[1,1024]{1,0:T(1,128)} %add.102.kpos_ref, bf16[1024,384]{1,0:T(8,128)(2,1)} %bitcast.144, bf16[1024,384]{1,0:T(8,128)(2,1)} %bitcast.145, bf16[1024,384]{1,0:T(8,128)(2,1)} %bitcast.146), custom_call_target="tpu_custom_call" | custom-call | flops 8000000000 | bytes 8000000 | tf_op jit(solution)/shard_map/attn_forward/pallas_call | solution.py:246
  245.5 14.2 %all-gather.11.cloned.1.call-done = bf16[11008,768]{1,0:T(8,128)(2,1)} async-done(((bf16[688,768]{1,0:T(8,128)(2,1)}), bf16[11008,768]{1,0:T(8,128)(2,1)}) %all-gather.11.cloned.1.call-update) | async-done | bytes 16908304 | tf_op jit(solution)/shard_map/all_gather | solution.py:976
  260.6 8.2 %mlp_forward.3 = (f32[128,768]{1,0:T(8,128)}, bf16[128,768]{1,0:T(8,128)(2,1)}, f32[128,3072]{1,0:T(8,128)}, f32[128,768]{1,0:T(8,128)}) custom-call(bf16[16,64,128]{2,1,0:T(8,128)(2,1)} %copy-done.21, f32[128,768]{1,0:T(8,128)} %get-tuple-element.102.x_ref, f32[12,768]{1,0:T(8,128)} %reshape.174.vec_ref, bf16[16,688,768]{2,1,0:T(8,128)(2,1)} %bitcast.118, ...), custom_call_target="tpu_custom_call" | custom-call | flops 8000000000 | bytes 8000000 | tf_op jit(solution)/shard_map/mlp_forward/pallas_call | solution.py:355
  268.8 8.6 %mlp_backward.2 = (bf16[128,768]{1,0:T(8,128)(2,1)}, f32[128,768]{1,0:T(8,128)}, bf16[128,768]{1,0:T(8,128)(2,1)}, bf16[16,64,128]{2,1,0:T(8,128)(2,1)}, f32[8,768]{1,0:T(8,128)}) custom-call(bf16[128,768]{1,0:T(8,128)(2,1)} %bitcast.142, f32[128,768]{1,0:T(8,128)} %get-tuple-element.109.mid_ref, f32[128,3072]{1,0:T(8,128)} %get-tuple-element.110.h_ref, ...), custom_call_target="tpu_custom_call" | custom-call | flops 8000000000 | bytes 8000000 | tf_op jit(solution)/shard_map/mlp_backward/pallas_call | solution.py:440
  279.6 37.1 %all_to_all.36 = bf16[16,64,128]{2,1,0:T(8,128)(2,1)} all-to-all(bf16[16,64,128]{2,1,0:T(8,128)(2,1)S(1)} %copy-done.37), channel_id=1, replica_groups=mesh['ctx'=16,'dp'=2] {'ctx'}, dimensions={0} | all-to-all | bytes 524288 | tf_op jit(solution)/shard_map/all_to_all | solution.py:972
  316.7 7.5 %attn_backward.2.pack_ref = bf16[1024,384]{1,0:T(8,128)(2,1)} custom-call(bf16[1024,384]{1,0:T(8,128)(2,1)} %bitcast.147, bf16[1024,128]{1,0:T(8,128)(2,1)} %bitcast.157, f32[1024,128]{1,0:T(8,128)} %get-tuple-element.115.of_ref, bf16[2,1024,1024]{2,1,0:T(8,128)(2,1)} %get-tuple-element.116.p_ref, bf16[1024,384]{1,0:T(8,128)(2,1)} %bitcast.148, ...), custom_call_target="tpu_custom_call" | custom-call | flops 8000000000 | bytes 8000000 | tf_op jit(solution)/shard_map/attn_backward/pallas_call | solution.py:305
  324.2 35.7 %all_to_all.37.d_ref = bf16[16,64,384]{2,1,0:T(8,128)(2,1)} all-to-all(bf16[16,64,384]{2,1,0:T(8,128)(2,1)} %bitcast.132), channel_id=1, replica_groups=mesh['ctx'=16,'dp'=2] {'ctx'}, dimensions={0} | all-to-all | bytes 1572864 | tf_op jit(solution)/shard_map/all_to_all | solution.py:972
  365.3 8.7 %mlp_backward.3 = (bf16[128,768]{1,0:T(8,128)(2,1)}, f32[128,768]{1,0:T(8,128)}, bf16[128,768]{1,0:T(8,128)(2,1)}, bf16[16,64,128]{2,1,0:T(8,128)(2,1)}, f32[8,768]{1,0:T(8,128)}) custom-call(f32[128,768]{1,0:T(8,128)} %get-tuple-element.118.gr_ref, f32[128,768]{1,0:T(8,128)} %get-tuple-element.119.mid_ref, f32[128,3072]{1,0:T(8,128)} %get-tuple-element.120.h_ref, ...), custom_call_target="tpu_custom_call" | custom-call | flops 8000000000 | bytes 8000000 | tf_op jit(solution)/shard_map/mlp_backward/pallas_call | solution.py:440
  388.0 13.3 %collective-permute-done.2 = bf16[128,768]{1,0:T(8,128)(2,1)S(1)} collective-permute-done((bf16[128,768]{1,0:T(8,128)(2,1)}, bf16[128,768]{1,0:T(8,128)(2,1)S(1)}, u32[]{:S(2)}, u32[]{:S(2)}) %collective-permute-start.2) | collective-permute-done | bytes 196640 | tf_op jit(solution)/shard_map/ppermute | solution.py:980
  410.5 7.4 %attn_backward.3.pack_ref = bf16[1024,384]{1,0:T(8,128)(2,1)} custom-call(bf16[1024,384]{1,0:T(8,128)(2,1)} %get-tuple-element.100.q_ref.k_ref.v_ref, bf16[1024,128]{1,0:T(8,128)(2,1)} %bitcast.156, f32[1024,128]{1,0:T(8,128)} %get-tuple-element.122.of_ref, bf16[2,1024,1024]{2,1,0:T(8,128)(2,1)} %get-tuple-element.123.p_ref, ...), custom_call_target="tpu_custom_call" | custom-call | flops 8000000000 | bytes 8000000 | tf_op jit(solution)/shard_map/attn_backward/pallas_call | solution.py:305
  436.6 15.4 %collective-permute-done.4.refs_1_ = bf16[512,768]{1,0:T(8,128)(2,1)S(1)} collective-permute-done((bf16[512,768]{1,0:T(8,128)(2,1)S(1)}, bf16[512,768]{1,0:T(8,128)(2,1)S(1)}, u32[]{:S(2)}, u32[]{:S(2)}) %collective-permute-start.4) | collective-permute-done | bytes 786464 | tf_op jit(solution)/shard_map/ppermute | solution.py:980
  473.6 7.5 %hidden_grads.1 = (f32[192,768]{1,0:T(8,128)}, f32[192,768]{1,0:T(8,128)}) custom-call(bf16[16,704,768]{2,1,0:T(8,128)(2,1)} %bitcast.129, bf16[16,688,768]{2,1,0:T(8,128)(2,1)} %bitcast.124, bf16[192,768]{1,0:T(8,128)(2,1)} %get-tuple-element.200.fc_ref, bf16[192,768]{1,0:T(8,128)(2,1)} %get-tuple-element.199.red_ref, f32[192,1]{1,0:T(8,128)} %copy.31.bias_ref), custom_call_target="tpu_custom_call" | custom-call | flops 1000000000 | bytes 1000000 | tf_op jit(solution)/shard_map/hidden_grads/pallas_call | solution.py:570
  489.1 10.6 %collective-permute-done.9 = bf16[64,768]{1,0:T(8,128)(2,1)S(1)} collective-permute-done((bf16[64,768]{1,0:T(8,128)(2,1)S(1)}, bf16[64,768]{1,0:T(8,128)(2,1)S(1)}, u32[]{:S(2)}, u32[]{:S(2)}) %collective-permute-start.9) | collective-permute-done | bytes 98336 | tf_op jit(solution)/shard_map/ppermute | solution.py:1203
  519.4 9.5 %collective-permute-done.11 = bf16[192,768]{1,0:T(8,128)(2,1)S(1)} collective-permute-done((bf16[192,768]{1,0:T(8,128)(2,1)S(1)}, bf16[192,768]{1,0:T(8,128)(2,1)S(1)}, u32[]{:S(2)}, u32[]{:S(2)}) %collective-permute-start.11) | collective-permute-done | bytes 294944 | tf_op jit(solution)/shard_map/ppermute | solution.py:980
  530.9 18.6 %collective-permute-done.15.refs_3_ = bf16[3,192,768]{2,1,0:T(8,128)(2,1)S(1)} collective-permute-done((bf16[3,192,768]{2,1,0:T(8,128)(2,1)S(1)}, bf16[3,192,768]{2,1,0:T(8,128)(2,1)S(1)}, u32[]{:S(2)}, u32[]{:S(2)}) %collective-permute-start.15) | collective-permute-done | bytes 884768 | tf_op jit(solution)/shard_map/ppermute | solution.py:980
  555.8 7.6 %sum_heads.1 = (bf16[2304,768]{1,0:T(8,128)(2,1)}, bf16[144,768]{1,0:T(8,128)(2,1)}, bf16[144,768]{1,0:T(8,128)(2,1)}, bf16[144,768]{1,0:T(8,128)(2,1)}, bf16[144,768]{1,0:T(8,128)(2,1)}) custom-call(s32[1]{0:T(128)} %bitcast.41.role_ref, s32[1]{0:T(128)} %bitcast.50.near_ref, bf16[192,768]{1,0:T(8,128)(2,1)} %copy-done.20, bf16[3,192,768]{2,1,0:T(8,128)(2,1)} %copy-done.3, ...), custom_call_target="tpu_custom_call" | custom-call | flops 4000000000 | bytes 4000000 | tf_op jit(solution)/shard_map/sum_heads/pallas_call | solution.py:949
  571.6 37.0 %newton_schulz.1 = (bf16[192,768]{1,0:T(8,128)(2,1)}, bf16[192,768]{1,0:T(8,128)(2,1)}, bf16[192,768]{1,0:T(8,128)(2,1)}, bf16[192,768]{1,0:T(8,128)(2,1)}) custom-call(s32[1]{0:T(128)} %bitcast.41.role_ref, bf16[192,768]{1,0:T(8,128)(2,1)} %copy-done.20, bf16[576,768]{1,0:T(8,128)(2,1)} %bitcast.131, bf16[192,768]{1,0:T(8,128)(2,1)} %collective-permute-done.13.refs_2_, ...), custom_call_target="tpu_custom_call" | custom-call | flops 46000001024 | bytes 46000000 | tf_op jit(solution)/shard_map/newton_schulz/pallas_call | solution.py:855
  629.7 9.7 %collective-permute-done.23 = bf16[192,768]{1,0:T(8,128)(2,1)S(1)} collective-permute-done((bf16[192,768]{1,0:T(8,128)(2,1)}, bf16[192,768]{1,0:T(8,128)(2,1)S(1)}, u32[]{:S(2)}, u32[]{:S(2)}) %collective-permute-start.23) | collective-permute-done | bytes 294944 | tf_op jit(solution)/shard_map/ppermute | solution.py:980
  (249 shorter events, 176.3 us)
Async XLA Ops:
  7.2 140.0 %all-gather.9.cloned.1.call-start = ((), (), s32[]{:S(2)}) async-start(), calls=%async_computation.9 | async-start | bytes 22560768 | tf_op jit(solution)/shard_map/all_gather | solution.py:976
  9.3 23.2 %collective-permute-start = (bf16[592,768]{1,0:T(8,128)(2,1)S(1)}, bf16[592,768]{1,0:T(8,128)(2,1)S(1)}, u32[]{:S(2)}, u32[]{:S(2)}) collective-permute-start(bf16[592,768]{1,0:T(8,128)(2,1)S(1)} %constant_dynamic-update-slice_fusion), channel_id=1, source_target_pairs={{0,1},{1,0},{2,3},{3,2},{4,5},{5,4},{6,7},{7,6},{8,9},{9,8},{10,11... | collective-permute-start | bytes 2727944 | tf_op jit(solution)/shard_map/ppermute | solution.py:1071
  35.6 224.1 %all-gather.11.cloned.1.call-start = ((), (), s32[]{:S(2)}) async-start(), calls=%async_computation.10 | async-start | bytes 17965056 | tf_op jit(solution)/shard_map/all_gather | solution.py:976
  164.3 19.3 %all-to-all-start = ((bf16[16,64,128]{2,1,0:T(8,128)(2,1)}), bf16[16,64,128]{2,1,0:T(8,128)(2,1)S(1)}, u32[]{:S(2)}, u32[]{:S(2)}) async-start(bf16[16,64,128]{2,1,0:T(8,128)(2,1)} %bitcast.155), calls=%async_computation | async-start | bytes 524288 | tf_op jit(solution)/shard_map/all_to_all | solution.py:972
  245.3 185.8 %all-gather.13.cloned.1.call-start = ((), (), s32[]{:S(2)}) async-start(), calls=%async_computation.11 | async-start | bytes 18382848 | tf_op jit(solution)/shard_map/all_gather | solution.py:976
  279.5 205.1 %all-gather.15.cloned.1.call-start = ((), (), s32[]{:S(2)}) async-start(), calls=%async_computation.12 | async-start | bytes 3342336 | tf_op jit(solution)/shard_map/all_gather | solution.py:976
  374.1 27.3 %collective-permute-start.2 = (bf16[128,768]{1,0:T(8,128)(2,1)}, bf16[128,768]{1,0:T(8,128)(2,1)S(1)}, u32[]{:S(2)}, u32[]{:S(2)}) collective-permute-start(bf16[128,768]{1,0:T(8,128)(2,1)} %get-tuple-element.124), channel_id=1, source_target_pairs={{0,16},{2,18},{4,20},{6,22},{8,24},{10,26},{12,28},{14,30},{16,0},... | collective-permute-start | bytes 589832 | tf_op jit(solution)/shard_map/ppermute | solution.py:980
  374.4 27.0 %collective-permute-start.3 = (bf16[128,768]{1,0:T(8,128)(2,1)}, bf16[128,768]{1,0:T(8,128)(2,1)S(1)}, u32[]{:S(2)}, u32[]{:S(2)}) collective-permute-start(bf16[128,768]{1,0:T(8,128)(2,1)} %get-tuple-element.124), channel_id=1, source_target_pairs={{0,8},{2,10},{4,12},{6,14},{8,0},{10,2},{12,4},{14,6},{16,24},{18,... | collective-permute-start | bytes 589832 | tf_op jit(solution)/shard_map/ppermute | solution.py:980
  378.5 31.3 %all-to-all-start.5 = ((bf16[16,64,128]{2,1,0:T(8,128)(2,1)}), bf16[16,64,128]{2,1,0:T(8,128)(2,1)S(1)}, u32[]{:S(2)}, u32[]{:S(2)}) async-start(bf16[16,64,128]{2,1,0:T(8,128)(2,1)} %get-tuple-element.121), calls=%async_computation.5 | async-start | bytes 524288 | tf_op jit(solution)/shard_map/all_to_all | solution.py:972
  417.9 34.2 %all-to-all-start.6 = ((bf16[16,64,384]{2,1,0:T(8,128)(2,1)}), bf16[16,64,384]{2,1,0:T(8,128)(2,1)S(1)}, u32[]{:S(2)}, u32[]{:S(2)}) async-start(bf16[16,64,384]{2,1,0:T(8,128)(2,1)} %bitcast.136), calls=%async_computation.6 | async-start | bytes 1572864 | tf_op jit(solution)/shard_map/all_to_all | solution.py:972
  421.5 196.3 %reduce-scatter.2.cloned.1.call-start = ((), (), s32[]{:S(2)}) async-start(), calls=%async_computation.8 | async-start | bytes 417792 | tf_op jit(solution)/shard_map/reduce_scatter | solution.py:1243
  421.6 30.5 %collective-permute-start.4 = (bf16[512,768]{1,0:T(8,128)(2,1)S(1)}, bf16[512,768]{1,0:T(8,128)(2,1)S(1)}, u32[]{:S(2)}, u32[]{:S(2)}) collective-permute-start(bf16[512,768]{1,0:T(8,128)(2,1)S(1)} %bitcast.133), channel_id=1, source_target_pairs={{0,4},{2,6},{4,0},{6,2},{8,12},{10,14},{12,8},{14,10},{16,20},{18,... | collective-permute-start | bytes 2359304 | tf_op jit(solution)/shard_map/ppermute | solution.py:980
  423.6 28.5 %collective-permute-start.5 = (bf16[512,768]{1,0:T(8,128)(2,1)S(1)}, bf16[512,768]{1,0:T(8,128)(2,1)}, u32[]{:S(2)}, u32[]{:S(2)}) collective-permute-start(bf16[512,768]{1,0:T(8,128)(2,1)S(1)} %bitcast.134), channel_id=1, source_target_pairs={{0,2},{2,0},{4,6},{6,4},{8,10},{10,8},{12,14},{14,12},{16,18},{18,... | collective-permute-start | bytes 2359304 | tf_op jit(solution)/shard_map/ppermute | solution.py:980
  482.6 18.1 %collective-permute-start.8 = (bf16[384,768]{1,0:T(8,128)(2,1)S(1)}, bf16[384,768]{1,0:T(8,128)(2,1)}, u32[]{:S(2)}, u32[]{:S(2)}) collective-permute-start(bf16[384,768]{1,0:T(8,128)(2,1)S(1)} %select_convert_fusion), channel_id=1, source_target_pairs={{0,1},{1,0},{2,3},{3,2},{4,5},{5,4},{6,7},{7,6},{8,9},{9,8},{10,11... | collective-permute-start | bytes 1769480 | tf_op jit(solution)/shard_map/ppermute | solution.py:1203
  503.2 25.7 %collective-permute-start.13 = (bf16[192,768]{1,0:T(8,128)(2,1)S(1)}, bf16[192,768]{1,0:T(8,128)(2,1)}, u32[]{:S(2)}, u32[]{:S(2)}) collective-permute-start(bf16[192,768]{1,0:T(8,128)(2,1)S(1)} %fusion.5.refs_0_), channel_id=1, source_target_pairs={{0,4},{2,6},{4,0},{6,2},{8,12},{10,14},{12,8},{14,10},{16,20},{18,... | collective-permute-start | bytes 884744 | tf_op jit(solution)/shard_map/ppermute | solution.py:980
  503.8 25.2 %collective-permute-start.14 = (bf16[192,768]{1,0:T(8,128)(2,1)S(1)}, bf16[192,768]{1,0:T(8,128)(2,1)S(1)}, u32[]{:S(2)}, u32[]{:S(2)}) collective-permute-start(bf16[192,768]{1,0:T(8,128)(2,1)S(1)} %fusion.5.refs_0_), channel_id=1, source_target_pairs={{0,2},{2,0},{4,6},{6,4},{8,10},{10,8},{12,14},{14,12},{16,18},{18,... | collective-permute-start | bytes 884744 | tf_op jit(solution)/shard_map/ppermute | solution.py:980
  505.5 23.4 %collective-permute-start.11 = (bf16[192,768]{1,0:T(8,128)(2,1)S(1)}, bf16[192,768]{1,0:T(8,128)(2,1)S(1)}, u32[]{:S(2)}, u32[]{:S(2)}) collective-permute-start(bf16[192,768]{1,0:T(8,128)(2,1)S(1)} %get-tuple-element.198), channel_id=1, source_target_pairs={{0,16},{2,18},{4,20},{6,22},{8,24},{10,26},{12,28},{14,30},{16,0},... | collective-permute-start | bytes 884744 | tf_op jit(solution)/shard_map/ppermute | solution.py:980
  507.9 21.0 %collective-permute-start.12 = (bf16[192,768]{1,0:T(8,128)(2,1)S(1)}, bf16[192,768]{1,0:T(8,128)(2,1)S(1)}, u32[]{:S(2)}, u32[]{:S(2)}) collective-permute-start(bf16[192,768]{1,0:T(8,128)(2,1)S(1)} %get-tuple-element.196), channel_id=1, source_target_pairs={{0,24},{2,26},{4,28},{6,30},{8,16},{10,18},{12,20},{14,22},{16,8},... | collective-permute-start | bytes 884744 | tf_op jit(solution)/shard_map/ppermute | solution.py:980
  529.1 20.4 %collective-permute-start.15 = (bf16[3,192,768]{2,1,0:T(8,128)(2,1)S(1)}, bf16[3,192,768]{2,1,0:T(8,128)(2,1)S(1)}, u32[]{:S(2)}, u32[]{:S(2)}) collective-permute-start(bf16[3,192,768]{2,1,0:T(8,128)(2,1)S(1)} %pad_maximum_fusion.2.refs_1_), channel_id=1, source_target_pairs={{0,4},{2,6},{4,0},{6,2},{8,12},{10,14},{12,8},{14,10},{16,20},{18,... | collective-permute-start | bytes 2654216 | tf_op jit(solution)/shard_map/ppermute | solution.py:980
  530.9 24.2 %collective-permute-start.16 = (bf16[3,192,768]{2,1,0:T(8,128)(2,1)S(1)}, bf16[3,192,768]{2,1,0:T(8,128)(2,1)}, u32[]{:S(2)}, u32[]{:S(2)}) collective-permute-start(bf16[3,192,768]{2,1,0:T(8,128)(2,1)S(1)} %pad_maximum_fusion.2.refs_1_), channel_id=1, source_target_pairs={{0,2},{2,0},{4,6},{6,4},{8,10},{10,8},{12,14},{14,12},{16,18},{18,... | collective-permute-start | bytes 2654216 | tf_op jit(solution)/shard_map/ppermute | solution.py:980
  563.5 45.1 %collective-permute-start.19 = (bf16[144,768]{1,0:T(8,128)(2,1)}, bf16[144,768]{1,0:T(8,128)(2,1)S(1)}, u32[]{:S(2)}, u32[]{:S(2)}) collective-permute-start(bf16[144,768]{1,0:T(8,128)(2,1)} %get-tuple-element.171), channel_id=1, source_target_pairs={{0,8},{2,10},{4,12},{6,14},{24,16},{26,18},{28,20},{30,22},{1,9},{... | collective-permute-start | bytes 663560 | tf_op jit(solution)/shard_map/ppermute | solution.py:1301
  566.0 42.6 %collective-permute-start.20 = (bf16[144,768]{1,0:T(8,128)(2,1)}, bf16[144,768]{1,0:T(8,128)(2,1)S(1)}, u32[]{:S(2)}, u32[]{:S(2)}) collective-permute-start(bf16[144,768]{1,0:T(8,128)(2,1)} %get-tuple-element.172), channel_id=1, source_target_pairs={{0,16},{2,18},{4,20},{6,22},{24,8},{26,10},{28,12},{30,14},{1,17},... | collective-permute-start | bytes 663560 | tf_op jit(solution)/shard_map/ppermute | solution.py:1301
  568.2 40.4 %collective-permute-start.21 = (bf16[144,768]{1,0:T(8,128)(2,1)}, bf16[144,768]{1,0:T(8,128)(2,1)S(1)}, u32[]{:S(2)}, u32[]{:S(2)}) collective-permute-start(bf16[144,768]{1,0:T(8,128)(2,1)} %get-tuple-element.173), channel_id=1, source_target_pairs={{0,24},{2,26},{4,28},{6,30},{24,0},{26,2},{28,4},{30,6},{1,25},{3,... | collective-permute-start | bytes 663560 | tf_op jit(solution)/shard_map/ppermute | solution.py:1301
  615.1 24.3 %collective-permute-start.23 = (bf16[192,768]{1,0:T(8,128)(2,1)}, bf16[192,768]{1,0:T(8,128)(2,1)S(1)}, u32[]{:S(2)}, u32[]{:S(2)}) collective-permute-start(bf16[192,768]{1,0:T(8,128)(2,1)} %get-tuple-element.175), channel_id=1, source_target_pairs={{0,16},{2,18},{4,20},{6,22},{8,24},{10,26},{12,28},{14,30},{16,0},... | collective-permute-start | bytes 884744 | tf_op jit(solution)/shard_map/ppermute | solution.py:980
  (61 other events, 479.9 us)
Sparse Core Ops, SparseCore 0:
  35.7 111.5 all-gather.8
  148.9 110.7 all-gather.10
  279.6 134.8 all-gather.12
  416.7 55.5 all-gather.14
  555.2 61.3 reduce-scatter.1
